TPU v7x, 32 devices: a whole 2x2x4 slice. The times are simulated.
32 devices in a mesh: group: 1, node: 8 (over y, x, core), local: 4 (over z).
Axes of the slice: x: 2, y: 2, z: 4, core: 2. Of those that a mesh axis runs over, the one named last changes fastest.
Arguments:
- queries: bfloat16 [256, 64, 128], P(('group', 'node', 'local')), may hold values from -5 to 5
- key_cache: bfloat16 [256, 4, 96, 128], P(('group', 'node', 'local')), may hold values from -5 to 5
- value_cache: bfloat16 [256, 4, 96, 128], P(('group', 'node', 'local')), may hold values from -15 to 15
- fresh_token_keys: bfloat16 [256, 4, 128], P(('group', 'node', 'local')), may hold values from -5 to 5
- new_values: bfloat16 [256, 4, 128], P(('group', 'node', 'local')), may hold values from -15 to 15
- lengths: int32 [256], P(('group', 'node', 'local')), may hold values from 2 to 96, as said below
- hidden_rows: bfloat16 [256, 4096], P(('group', 'node', 'local')), may hold values from -100 to 100
- norm_gain: bfloat16 [4096], replicated, may hold values from 0.099609375 to 1.8984375
- expert_ids: int32 [256, 8], P(('group', 'node', 'local')), may hold values from 0 to 15, all different within a row; in each aligned block of 8 rows (0 to 7, 8 to 15, ...) at most 8 rows name the same one
- route_scores: float32 [256, 8], P(('group', 'node', 'local')), may hold values from 0.1 to 10
- gate_weight: bfloat16 [32, 4096, 768], P(('node', 'local')), may hold values from -0.09375 to 0.09375
- up_weight: bfloat16 [32, 4096, 768], P(('node', 'local')), may hold values from -0.09375 to 0.09375
- down_weight: bfloat16 [32, 768, 4096], P(('node', 'local')), may hold values from -0.4375 to 0.4375
Outputs:
- context: bfloat16 [256, 8192], P(('group', 'node', 'local'))
- weighted_expert_total: bfloat16 [256, 4096], P(('group', 'node', 'local'))
Inputs may be any that keep to these rules, and one draw needn't show every extreme that they name: `expert_ids`: each row names 8 different experts; among the 8 rows of one device no expert is named more than 8 times, and on some device some expert is named exactly 8 times. `lengths`: some request has all 96 slots filled.
All inputs are finite; a program needn't handle non-finite values.
Results may differ from a plain program's by a relative error of at most 0.0065.
Values may be sent and summed in bfloat16 or wider, within the bound.
No kernel may reach another device: no remote copies, remote signals or barrier semaphores. Data moves between devices by JAX's collectives and lax.ppermute only.
A program may use at most 128 MiB of HBM per device.

v0:
```python
import math

import jax
import jax.numpy as jnp
from jax import lax
from jax.sharding import PartitionSpec as P


def attend(queries, key_cache, value_cache, fresh_token_keys, new_values, lengths):
    request_count, head_count, head_width = queries.shape
    kv_heads = key_cache.shape[1]
    slot_count = key_cache.shape[2]
    grouped_queries = queries.reshape(request_count, kv_heads, head_count // kv_heads, head_width)
    inverse_scale = 1.0 / math.sqrt(head_width)
    scores = (
        jnp.einsum(
            "bkgd,bkpd->bkgp", grouped_queries, key_cache, preferred_element_type=jnp.float32
        )
        * inverse_scale
    )
    positions = jnp.arange(slot_count, dtype=jnp.int32)
    in_range = positions[None, :] < lengths[:, None]
    scores = jnp.where(in_range[:, None, None, :], scores, -jnp.inf)
    self_token_score = (
        jnp.einsum(
            "uxea,uxa->uxe", grouped_queries, fresh_token_keys, preferred_element_type=jnp.float32
        )
        * inverse_scale
    )
    highest = jnp.maximum(jnp.max(scores, axis=-1), self_token_score)
    exponent = jnp.exp(scores - highest[..., None])
    own_exponent = jnp.exp(self_token_score - highest)
    denominator = jnp.sum(exponent, axis=-1) + own_exponent
    probs = (exponent / denominator[..., None]).astype(jnp.bfloat16)
    own_prob = (own_exponent / denominator).astype(jnp.bfloat16)
    mixed = jnp.einsum("bkgp,bkpd->bkgd", probs, value_cache, preferred_element_type=jnp.float32)
    mixed = (
        mixed
        + own_prob.astype(jnp.float32)[..., None] * new_values.astype(jnp.float32)[:, :, None, :]
    )
    return mixed.reshape(request_count, head_count * head_width).astype(jnp.bfloat16)


def routed_expert_rows(arrived, gate_piece, up_piece, down_piece):
    flattened_tokens = arrived.reshape(-1, arrived.shape[-1])
    gate_proj = jnp.dot(flattened_tokens, gate_piece, preferred_element_type=jnp.float32)
    up_proj = jnp.dot(flattened_tokens, up_piece, preferred_element_type=jnp.float32)
    activated = (jax.nn.silu(gate_proj) * up_proj).astype(jnp.bfloat16)
    return jnp.dot(activated, down_piece, preferred_element_type=jnp.float32)


def per_device(
    queries,
    key_cache,
    value_cache,
    fresh_token_keys,
    new_values,
    lengths,
    hidden_rows,
    norm_gain,
    expert_ids,
    route_scores,
    gate_weight,
    up_weight,
    down_weight,
):
    context = attend(queries, key_cache, value_cache, fresh_token_keys, new_values, lengths)
    row_count, model_width = hidden_rows.shape
    top_count = expert_ids.shape[1]
    node_count = lax.axis_size("node")
    local_count = lax.axis_size("local")
    devices = node_count * local_count
    experts = devices // 2
    capacity = 2 * min(row_count // 2, max(1, top_count * row_count // experts))
    hidden_f32 = hidden_rows.astype(jnp.float32)
    mean_square = jnp.mean(hidden_f32 * hidden_f32, axis=1, keepdims=True)
    normed = (hidden_f32 * lax.rsqrt(mean_square + 1e-06) * norm_gain.astype(jnp.float32)).astype(
        jnp.bfloat16
    )
    gates = route_scores / jnp.sum(route_scores, axis=1, keepdims=True)
    flat_ids = expert_ids.reshape(-1)
    member = (flat_ids[:, None] == jnp.arange(experts, dtype=jnp.int32)[None, :]).astype(jnp.int32)
    earlier = jnp.cumsum(member, axis=0) - member
    slot_index = jnp.sum(earlier * member, axis=1)
    target_slot = (flat_ids * capacity + slot_index).reshape(row_count, top_count)
    slot_range = jnp.arange(experts * capacity, dtype=jnp.int32)
    matches = target_slot[:, :, None] == slot_range[None, None, :]
    collect = jnp.sum(jnp.where(matches, gates[:, :, None], 0.0), axis=1)
    spread = jnp.any(matches, axis=1).astype(jnp.bfloat16)
    outgoing = lax.dot_general(
        spread, normed, (((0,), (0,)), ((), ())), preferred_element_type=jnp.float32
    ).astype(jnp.bfloat16)
    gate_piece = gate_weight[0]
    up_piece = up_weight[0]
    down_piece = down_weight[0]
    doubled = jnp.repeat(outgoing.reshape(experts, capacity, model_width), 2, axis=0)
    arrived = lax.all_to_all(doubled, ("node", "local"), split_axis=0, concat_axis=0, tiled=True)
    partial_value = routed_expert_rows(arrived, gate_piece, up_piece, down_piece).reshape(
        devices, capacity, model_width
    )
    returned = lax.all_to_all(
        partial_value, ("node", "local"), split_axis=0, concat_axis=0, tiled=True
    )
    combined = jnp.sum(returned.reshape(experts, 2, capacity, model_width), axis=1)
    weighted_expert_total = jnp.dot(
        collect,
        combined.reshape(experts * capacity, model_width),
        precision=lax.Precision.HIGHEST,
        preferred_element_type=jnp.float32,
    ).astype(jnp.bfloat16)
    return (context, weighted_expert_total)


def solution(mesh):
    placed = (
        P(("group", "node", "local"), None, None),
        P(("group", "node", "local"), None, None, None),
        P(("group", "node", "local"), None, None, None),
        P(("group", "node", "local"), None, None),
        P(("group", "node", "local"), None, None),
        P(("group", "node", "local")),
        P(("group", "node", "local"), None),
        P(),
        P(("group", "node", "local"), None),
        P(("group", "node", "local"), None),
        P(("node", "local"), None, None),
        P(("node", "local"), None, None),
        P(("node", "local"), None, None),
    )
    return jax.shard_map(
        per_device,
        mesh=mesh,
        in_specs=placed,
        out_specs=(P(("group", "node", "local"), None), P(("group", "node", "local"), None)),
        check_vma=False,
    )
```

profile of v0, /device:TPU:0, one launch (start us, length us, event | category | flops | bytes accessed | tf_op | source)
XLA Modules:
  0.0 169.7 jit_solution(12951049820695238622)
XLA Ops:
  0.6 0.0 copy-start
  0.6 0.8 eq.28
  1.5 1.0 fusion.28
  2.5 0.7 convert_element_type.48
  3.2 0.1 fusion.37
  3.3 0.1 reduce_window_sum.11
  3.4 0.2 select_reduce_fusion.1
  3.5 0.1 reduce_sum.58
  3.6 0.7 multiply_add_fusion
  4.3 0.1 fusion.36
  4.4 0.0 copy-start.5
  4.4 1.5 fusion.6
  5.9 0.2 broadcast_in_dim.44
  6.2 0.0 slice-start.2
  6.2 0.0 slice-start
  6.2 54.6 %all_to_all.10 = bf16[32,8,4096]{2,1,0:T(8,128)(2,1)S(1)} all-to-all(bf16[32,8,4096]{2,1,0:T(8,128)(2,1)S(1)} %bitcast.53), channel_id=1, replica_groups=mesh['group'=1,'node'=8,'local'=4] {'node','local'}, dimensions={0} | all-to-all | bytes 4194304 | tf_op jit(solution)/shard_map/all_to_all | solution.py:97
  60.8 0.0 copy-done.5
  60.8 0.0 slice-start.3
  60.8 0.0 slice-start.1
  60.8 1.8 %fusion.4 = f32[256,768]{1,0:T(8,128)S(1)} fusion(bf16[1,4096,768]{2,1,0:T(8,128)(2,1)S(1)} %copy-done.5, bf16[32,8,4096]{2,1,0:T(8,128)(2,1)S(1)} %all_to_all.10), kind=kOutput, calls=%fused_computation.4 | convolution fusion | flops 1610612736 | bytes 9175040 | tf_op jit(solution)/shard_map/dot_general | solution.py:46
  62.6 0.0 slice-done.2
  62.6 0.0 slice-done.3
  62.7 1.8 %fusion.20 = bf16[32,8,768]{2,1,0:T(8,128)(2,1)S(1)} fusion(bf16[1,4096,768]{2,1,0:T(8,128)(2,1)S(1)} %bitcast.63, bf16[32,8,4096]{2,1,0:T(8,128)(2,1)S(1)} %all_to_all.10, f32[256,768]{1,0:T(8,128)S(1)} %fusion.4), kind=kOutput, calls=%fused_computation.15 | convolution fusion | flops 1611792384 | bytes 9568256 | tf_op jit(solution)/shard_map/dot_general | solution.py:47
  64.5 0.0 slice-done
  64.5 0.0 slice-done.1
  64.5 3.9 %fusion = f32[32,8,4096]{2,1,0:T(8,128)} fusion(bf16[32,8,768]{2,1,0:T(8,128)(2,1)S(1)} %fusion.20, bf16[1,768,4096]{2,1,0:T(8,128)(2,1)S(1)} %bitcast.55), kind=kOutput, calls=%fused_computation | convolution fusion | flops 1610612736 | bytes 10878976 | tf_op jit(solution)/shard_map/dot_general | solution.py:49
  68.4 0.0 copy-start.1
  68.4 0.0 copy-start.3
  68.4 4.6 %all-to-all-start.1 = ((f32[32,8,4096]{2,1,0:T(8,128)}), f32[32,8,4096]{2,1,0:T(8,128)}, u32[]{:S(2)}, u32[]{:S(2)}) async-start(f32[32,8,4096]{2,1,0:T(8,128)} %fusion), calls=%async_computation.1 | async-start | bytes 8388608 | tf_op jit(solution)/shard_map/all_to_all | solution.py:101
  73.0 0.0 copy-done.4
  73.0 0.0 copy-done.7
  73.1 0.1 iota_compare_fusion.2
  73.1 0.0 copy-done.2
  73.1 0.0 copy-done.6
  73.1 0.2 fusion.38
  73.3 0.0 copy-done.1
  73.3 0.6 fusion.42
  73.9 0.3 fusion.27
  74.3 0.0 copy-done
  74.3 0.4 fusion.26
  74.7 0.8 copy.21
  75.4 0.0 copy-done.3
  75.4 0.1 reduce_sum.59
  75.5 0.1 broadcast_divide_fusion
  75.6 0.1 select_reduce_fusion
  75.7 89.5 %all-to-all-done.1 = f32[32,8,4096]{2,1,0:T(8,128)} async-done(((f32[32,8,4096]{2,1,0:T(8,128)}), f32[32,8,4096]{2,1,0:T(8,128)}, u32[]{:S(2)}, u32[]{:S(2)}) %all-to-all-start.1) | async-done | bytes 4194336 | tf_op jit(solution)/shard_map/all_to_all | solution.py:101
  165.3 2.7 %bitcast_reduce_fusion = f32[16,8,4096]{2,1,0:T(8,128)S(1)} fusion(f32[32,8,4096]{2,1,0:T(8,128)} %all-to-all-done.1), kind=kLoop, calls=%fused_computation.9 | loop fusion | flops 524288 | bytes 6291456 | tf_op jit(solution)/shard_map/reduce_sum | solution.py:104
  167.9 1.7 %convolution_convert_fusion.1 = bf16[8,4096]{1,0:T(8,128)(2,1)} fusion(f32[8,128]{1,0:T(8,128)S(1)} %select_reduce_fusion, f32[16,8,4096]{2,1,0:T(8,128)S(1)} %bitcast_reduce_fusion), kind=kOutput, calls=%fused_computation.8 | convolution fusion | flops 50364416 | bytes 2166784 | tf_op jit(solution)/shard_map/dot_general | solution.py:105
  (10 shorter events, 0.1 us)
Async XLA Ops:
  0.6 73.6 %copy-start = (bf16[8,4,96,128]{3,2,1,0:T(8,128)(2,1)S(1)}, bf16[8,4,96,128]{3,2,1,0:T(8,128)(2,1)}, u32[]{:S(2)}) copy-start(bf16[8,4,96,128]{3,2,1,0:T(8,128)(2,1)} %param.15) | copy-start | bytes 2359300
  4.4 56.4 %copy-start.5 = (bf16[1,4096,768]{2,1,0:T(8,128)(2,1)S(1)}, bf16[1,4096,768]{2,1,0:T(8,128)(2,1)}, u32[]{:S(2)}) copy-start(bf16[1,4096,768]{2,1,0:T(8,128)(2,1)} %param.23) | copy-start | bytes 18874372
  6.2 56.5 %slice-start.2 = ((s8[6291456]{0:T(1024)(128)(4,1)}), s8[4194304]{0:T(1024)(128)(4,1)S(1)}, s32[]{:S(2)}) async-start(s8[6291456]{0:T(1024)(128)(4,1)} %bitcast.62), calls=%async_computation.4 | async-start | bytes 8388608
  6.2 58.3 %slice-start = ((s8[6291456]{0:T(1024)(128)(4,1)}), s8[2097152]{0:T(1024)(128)(4,1)S(1)}, s32[]{:S(2)}) async-start(s8[6291456]{0:T(1024)(128)(4,1)} %bitcast.54), calls=%async_computation.2 | async-start | bytes 4194304
  60.8 1.8 %slice-start.3 = ((s8[6291456]{0:T(1024)(128)(4,1)}), s8[2097152]{0:T(1024)(128)(4,1)S(1)}, s32[]{:S(2)}) async-start(s8[6291456]{0:T(1024)(128)(4,1)} %bitcast.62), calls=%async_computation.5 | async-start | bytes 4194304
  60.8 3.7 %slice-start.1 = ((s8[6291456]{0:T(1024)(128)(4,1)}), s8[4194304]{0:T(1024)(128)(4,1)S(1)}, s32[]{:S(2)}) async-start(s8[6291456]{0:T(1024)(128)(4,1)} %bitcast.54), calls=%async_computation.3 | async-start | bytes 8388608
  68.4 4.6 %copy-start.4 = (bf16[8,4,128]{2,1,0:T(4,128)(2,1)S(1)}, bf16[8,4,128]{2,1,0:T(4,128)(2,1)}, u32[]{:S(2)}) copy-start(bf16[8,4,128]{2,1,0:T(4,128)(2,1)} %param.17) | copy-start | bytes 24580
  68.4 4.7 %copy-start.7 = (s32[8]{0:T(128)S(1)}, s32[8]{0:T(128)}, u32[]{:S(2)}) copy-start(s32[8]{0:T(128)} %param.18) | copy-start | bytes 100
  68.4 4.7 %copy-start.2 = (bf16[8,64,128]{2,1,0:T(8,128)(2,1)S(1)}, bf16[8,64,128]{2,1,0:T(8,128)(2,1)}, u32[]{:S(2)}) copy-start(bf16[8,64,128]{2,1,0:T(8,128)(2,1)} %param.13) | copy-start | bytes 393220
  68.4 4.7 %copy-start.6 = (bf16[8,4,128]{2,1,0:T(4,128)(2,1)S(1)}, bf16[8,4,128]{2,1,0:T(4,128)(2,1)}, u32[]{:S(2)}) copy-start(bf16[8,4,128]{2,1,0:T(4,128)(2,1)} %param.16) | copy-start | bytes 24580
  68.4 4.9 %copy-start.1 = (bf16[8,4,96,128]{3,2,1,0:T(8,128)(2,1)S(1)}, bf16[8,4,96,128]{3,2,1,0:T(8,128)(2,1)}, u32[]{:S(2)}) copy-start(bf16[8,4,96,128]{3,2,1,0:T(8,128)(2,1)} %param.14) | copy-start | bytes 2359300
  68.4 7.0 %copy-start.3 = (f32[8,8]{1,0:T(8,128)S(1)}, f32[8,8]{1,0:T(8,128)}, u32[]{:S(2)}) copy-start(f32[8,8]{1,0:T(8,128)} %param.22) | copy-start | bytes 772
  68.4 96.8 %all-to-all-start.1 = ((f32[32,8,4096]{2,1,0:T(8,128)}), f32[32,8,4096]{2,1,0:T(8,128)}, u32[]{:S(2)}, u32[]{:S(2)}) async-start(f32[32,8,4096]{2,1,0:T(8,128)} %fusion), calls=%async_computation.1 | async-start | bytes 8388608 | tf_op jit(solution)/shard_map/all_to_all | solution.py:101
where the time goes:
time: 171 us; the launch traced here: 170 us
  waiting for transfers between devices  89.5 us (52%)
  blocking collectives  54.6 us (32%)
  matrix products  11.9 us (7%)
  other arithmetic  6.22 us (4%)
  starting transfers between devices  4.59 us (3%)
  local copies, waits for them, and re-layouts  1.97 us (1%)
    all_to_all x1, waiting for transfers between devices, per_device(): lax.all_to_all(partial_value, ('node', 'local'), split_axis=0, concat_axi...  89.5 us
    all_to_all x1, blocking collectives, per_device(): lax.all_to_all(doubled, ('node', 'local'), split_axis=0, concat_axis=0, t...  54.6 us
    all_to_all x1, starting transfers between devices, per_device(): lax.all_to_all(partial_value, ('node', 'local'), split_axis=0, concat_axi...  4.59 us
    dot_general x1, matrix products, routed_expert_rows(): return jnp.dot(activated, down_piece, preferred_element_type=jnp.float32)  3.86 us
  transfers between devices with their start and end apart: 1, of which 1 were waited for; matrix products, arithmetic and copies ran while one was open for 2% of the time, Pallas kernels for 0%

commit v1 on v0

--- a/solution.py
+++ b/solution.py
@@ -41,12 +41,47 @@
     return mixed.reshape(request_count, head_count * head_width).astype(jnp.bfloat16)
 
 
-def routed_expert_rows(arrived, gate_piece, up_piece, down_piece):
-    flattened_tokens = arrived.reshape(-1, arrived.shape[-1])
-    gate_proj = jnp.dot(flattened_tokens, gate_piece, preferred_element_type=jnp.float32)
-    up_proj = jnp.dot(flattened_tokens, up_piece, preferred_element_type=jnp.float32)
-    activated = (jax.nn.silu(gate_proj) * up_proj).astype(jnp.bfloat16)
-    return jnp.dot(activated, down_piece, preferred_element_type=jnp.float32)
+def exchange(rows, node_mask, local_mask):
+    nodes = lax.axis_size("node")
+    locals_ = lax.axis_size("local")
+    pairs = [
+        (n * locals_ + k, (n ^ node_mask) * locals_ + (k ^ local_mask))
+        for n in range(nodes)
+        for k in range(locals_)
+    ]
+    return lax.ppermute(rows, ("node", "local"), pairs)
+
+
+def gather_rows(rows):
+    nodes = lax.axis_size("node")
+    line = jnp.concatenate(
+        [rows] + [exchange(rows, 0, k) for k in range(1, lax.axis_size("local"))]
+    )
+    plane = jnp.concatenate([line] + [exchange(line, n, 0) for n in range(2, nodes, 2)])
+    return jnp.concatenate([plane, exchange(plane, 1, 0)])
+
+
+def scatter_sum(partial_rows):
+    nodes = lax.axis_size("node")
+    locals_ = lax.axis_size("local")
+    half = partial_rows.shape[0] // 2
+    arrived = exchange(partial_rows[half:].astype(jnp.bfloat16), 1, 0)
+    plane = partial_rows[:half] + arrived.astype(jnp.float32)
+    size = half // (nodes // 2)
+    packed = plane.astype(jnp.bfloat16)
+    line = plane[:size]
+    for step in range(1, nodes // 2):
+        line = line + exchange(
+            packed[step * size : (step + 1) * size], 2 * step, 0
+        ).astype(jnp.float32)
+    size = size // locals_
+    packed = line.astype(jnp.bfloat16)
+    total = line[:size]
+    for step in range(1, locals_):
+        total = total + exchange(
+            packed[step * size : (step + 1) * size], 0, step
+        ).astype(jnp.float32)
+    return total
 
 
 def per_device(
@@ -66,49 +101,41 @@
 ):
     context = attend(queries, key_cache, value_cache, fresh_token_keys, new_values, lengths)
     row_count, model_width = hidden_rows.shape
-    top_count = expert_ids.shape[1]
-    node_count = lax.axis_size("node")
-    local_count = lax.axis_size("local")
-    devices = node_count * local_count
-    experts = devices // 2
-    capacity = 2 * min(row_count // 2, max(1, top_count * row_count // experts))
+    experts = lax.axis_size("node") * lax.axis_size("local") // 2
     hidden_f32 = hidden_rows.astype(jnp.float32)
     mean_square = jnp.mean(hidden_f32 * hidden_f32, axis=1, keepdims=True)
     normed = (hidden_f32 * lax.rsqrt(mean_square + 1e-06) * norm_gain.astype(jnp.float32)).astype(
         jnp.bfloat16
     )
     gates = route_scores / jnp.sum(route_scores, axis=1, keepdims=True)
-    flat_ids = expert_ids.reshape(-1)
-    member = (flat_ids[:, None] == jnp.arange(experts, dtype=jnp.int32)[None, :]).astype(jnp.int32)
-    earlier = jnp.cumsum(member, axis=0) - member
-    slot_index = jnp.sum(earlier * member, axis=1)
-    target_slot = (flat_ids * capacity + slot_index).reshape(row_count, top_count)
-    slot_range = jnp.arange(experts * capacity, dtype=jnp.int32)
-    matches = target_slot[:, :, None] == slot_range[None, None, :]
-    collect = jnp.sum(jnp.where(matches, gates[:, :, None], 0.0), axis=1)
-    spread = jnp.any(matches, axis=1).astype(jnp.bfloat16)
-    outgoing = lax.dot_general(
-        spread, normed, (((0,), (0,)), ((), ())), preferred_element_type=jnp.float32
-    ).astype(jnp.bfloat16)
-    gate_piece = gate_weight[0]
-    up_piece = up_weight[0]
-    down_piece = down_weight[0]
-    doubled = jnp.repeat(outgoing.reshape(experts, capacity, model_width), 2, axis=0)
-    arrived = lax.all_to_all(doubled, ("node", "local"), split_axis=0, concat_axis=0, tiled=True)
-    partial_value = routed_expert_rows(arrived, gate_piece, up_piece, down_piece).reshape(
-        devices, capacity, model_width
+    chosen = expert_ids[:, :, None] == jnp.arange(experts, dtype=jnp.int32)[None, None, :]
+    table = jnp.sum(jnp.where(chosen, gates[:, :, None], 0.0), axis=1)
+    coarse = lax.reduce_precision(table, 8, 7)
+    extra = -(2 * experts) % 128
+    outgoing = jnp.concatenate(
+        [
+            normed,
+            coarse.astype(jnp.bfloat16),
+            (table - coarse).astype(jnp.bfloat16),
+            jnp.zeros((row_count, extra), jnp.bfloat16),
+        ],
+        axis=1,
     )
-    returned = lax.all_to_all(
-        partial_value, ("node", "local"), split_axis=0, concat_axis=0, tiled=True
+    arrived = gather_rows(outgoing)
+    tokens = arrived[:, :model_width]
+    own = (lax.axis_index("node") * lax.axis_size("local") + lax.axis_index("local")) // 2
+    column = jnp.arange(2 * experts + extra, dtype=jnp.int32) % experts
+    mine = (column == own) & (jnp.arange(2 * experts + extra) < 2 * experts)
+    weight = jnp.sum(
+        jnp.where(mine[None, :], arrived[:, model_width:].astype(jnp.float32), 0.0),
+        axis=1,
+        keepdims=True,
     )
-    combined = jnp.sum(returned.reshape(experts, 2, capacity, model_width), axis=1)
-    weighted_expert_total = jnp.dot(
-        collect,
-        combined.reshape(experts * capacity, model_width),
-        precision=lax.Precision.HIGHEST,
-        preferred_element_type=jnp.float32,
-    ).astype(jnp.bfloat16)
-    return (context, weighted_expert_total)
+    gate_proj = jnp.dot(tokens, gate_weight[0], preferred_element_type=jnp.float32)
+    up_proj = jnp.dot(tokens, up_weight[0], preferred_element_type=jnp.float32)
+    activated = (jax.nn.silu(gate_proj) * up_proj).astype(jnp.bfloat16)
+    partial_rows = weight * jnp.dot(activated, down_weight[0], preferred_element_type=jnp.float32)
+    return (context, scatter_sum(partial_rows).astype(jnp.bfloat16))
 
 
 def solution(mesh):

time: 171 us -> 86 us (0.50)
  blocking collectives: 54.6 us -> 0 us
  waiting for transfers between devices: 89.5 us -> 34.9 us
  starting transfers between devices: 4.59 us -> 17.4 us
  matrix products: 11.9 us -> 18.8 us
  local copies, waits for them, and re-layouts: 1.97 us -> 5.33 us
  other arithmetic: 6.22 us -> 8.29 us
    all_to_all x1 -> x0, waiting for transfers between devices: 89.5 us -> none  [per_device(): lax.all_to_all(partial_value, ('node', 'local'), split_axis=0, concat_axi...]
    all_to_all x1 -> x0, blocking collectives: 54.6 us -> none  [per_device(): lax.all_to_all(doubled, ('node', 'local'), split_axis=0, concat_axis=0, t...]
    ppermute x0 -> x14, waiting for transfers between devices: none -> 34.9 us  [exchange(): return lax.ppermute(rows, ('node', 'local'), pairs)]
    ppermute x0 -> x14, starting transfers between devices: none -> 17.4 us  [exchange(): return lax.ppermute(rows, ('node', 'local'), pairs)]
    dot_general x5 -> x2, matrix products: 10.7 us -> 17.7 us  [the longest x1 11.4 us: per_device(): jnp.dot(activated, down_weight[0], preferred_element_type=jnp.float32)]
    all_to_all x1 -> x0, starting transfers between devices: 4.59 us -> none  [per_device(): lax.all_to_all(partial_value, ('node', 'local'), split_axis=0, concat_axi...]
    convert_element_type x1 -> x5, other arithmetic: 0.07 us -> 3.65 us  [the longest x1 1.91 us: scatter_sum(): packed = plane.astype(jnp.bfloat16)]
    reduce_sum x3 -> x2, other arithmetic: 2.95 us -> 0.89 us  [the longest x1 0.78 us: per_device(): table = jnp.sum(jnp.where(chosen, gates[:, :, None], 0.0), axis=1)]
  transfers between devices with their start and end apart: 1 -> 14, of which waited for: 1 -> 9; matrix products, arithmetic and copies ran while one was open for 2% -> 3% of each run, Pallas kernels for 0% -> 0%
where the time goes in v1:
time: 86 us; the launch traced here: 85.6 us
  waiting for transfers between devices  34.9 us (41%)
  matrix products  18.8 us (22%)
  starting transfers between devices  17.4 us (20%)
  other arithmetic  8.29 us (10%)
  local copies, waits for them, and re-layouts  5.33 us (6%)
    ppermute x14, waiting for transfers between devices, exchange(): return lax.ppermute(rows, ('node', 'local'), pairs)  34.9 us
    ppermute x14, starting transfers between devices, exchange(): return lax.ppermute(rows, ('node', 'local'), pairs)  17.4 us
    dot_general x1, matrix products, per_device(): jnp.dot(activated, down_weight[0], preferred_element_type=jnp.float32)  11.4 us
    dot_general x1, matrix products, per_device(): up_proj = jnp.dot(tokens, up_weight[0], preferred_element_type=jnp.float32)  6.25 us
    unnamed x23, local copies, waits for them, and re-layouts  2.28 us
    convert_element_type x1, other arithmetic, scatter_sum(): packed = plane.astype(jnp.bfloat16)  1.91 us
    slice x1, local copies, waits for them, and re-layouts, scatter_sum(): arrived = exchange(partial_rows[half:].astype(jnp.bfloat16), 1, 0)  1.78 us
  transfers between devices with their start and end apart: 14, of which 9 were waited for; matrix products, arithmetic and copies ran while one was open for 3% of the time, Pallas kernels for 0%

profile of v1, /device:TPU:0, one launch (start us, length us, event | category | flops | bytes accessed | tf_op | source)
XLA Modules:
  0.0 85.6 jit_solution(1526212441852445429)
XLA Ops:
  0.6 0.0 copy-start
  0.6 0.9 %reduce_sum.47 = f32[8]{0:T(128)S(1)} reduce(f32[8,8]{1,0:T(8,128)} %param.22, f32[]{:T(128)} %constant.44.clone.1), dimensions={1}, to_apply=%region_3.4 | reduce | flops 56 | bytes 292 | tf_op jit(solution)/shard_map/reduce_sum | solution.py:110
  1.5 0.8 broadcast_divide_fusion
  2.3 0.8 select_reduce_fusion.1
  3.1 0.7 convert_element_type.77
  3.8 1.0 %fusion.25 = f32[8]{0:T(128)S(1)} fusion(bf16[8,4096]{1,0:T(8,128)(2,1)} %param.19), kind=kLoop, calls=%fused_computation.26 | loop fusion | flops 98296 | bytes 65568 | tf_op jit(solution)/shard_map/reduce_sum | solution.py:106
  4.8 0.9 %fusion.27 = bf16[8,4096]{1,0:T(8,128)(2,1)S(1)} fusion(bf16[8,4096]{1,0:T(8,128)(2,1)} %param.19, f32[4096]{0:T(1024)S(1)} %convert_element_type.77, f32[8]{0:T(128)S(1)} %add_rsqrt_fusion), kind=kLoop, calls=%fused_computation.28 | loop fusion | flops 131072 | bytes 147488 | tf_op jit(solution)/shard_map/convert_element_type | solution.py:107
  5.7 0.1 concatenate.14
  5.8 3.0 %collective-permute-start = (bf16[8,4224]{1,0:T(8,128)(2,1)S(1)}, bf16[8,4224]{1,0:T(8,128)(2,1)S(1)}, u32[]{:S(2)}, u32[]{:S(2)}) collective-permute-start(bf16[8,4224]{1,0:T(8,128)(2,1)S(1)} %concatenate.14), channel_id=1, source_target_pairs={{0,1},{1,0},{2,3},{3,2},{4,5},{5,4},{6,7},{7,6},{8,9},{9,8},{10,11... | collective-permute-start | bytes 202760 | tf_op jit(solution)/shard_map/ppermute | solution.py:52
  8.8 2.6 %collective-permute-start.1 = (bf16[8,4224]{1,0:T(8,128)(2,1)S(1)}, bf16[8,4224]{1,0:T(8,128)(2,1)S(1)}, u32[]{:S(2)}, u32[]{:S(2)}) collective-permute-start(bf16[8,4224]{1,0:T(8,128)(2,1)S(1)} %concatenate.14), channel_id=1, source_target_pairs={{0,2},{1,3},{2,0},{3,1},{4,6},{5,7},{6,4},{7,5},{8,10},{9,11},{10,... | collective-permute-start | bytes 202760 | tf_op jit(solution)/shard_map/ppermute | solution.py:52
  11.5 4.8 %collective-permute-done.1 = bf16[8,4224]{1,0:T(8,128)(2,1)S(1)} collective-permute-done((bf16[8,4224]{1,0:T(8,128)(2,1)S(1)}, bf16[8,4224]{1,0:T(8,128)(2,1)S(1)}, u32[]{:S(2)}, u32[]{:S(2)}) %collective-permute-start.1) | collective-permute-done | bytes 67616 | tf_op jit(solution)/shard_map/ppermute | solution.py:52
  16.2 1.4 %collective-permute-done.2 = bf16[8,4224]{1,0:T(8,128)(2,1)S(1)} collective-permute-done((bf16[8,4224]{1,0:T(8,128)(2,1)S(1)}, bf16[8,4224]{1,0:T(8,128)(2,1)S(1)}, u32[]{:S(2)}, u32[]{:S(2)}) %collective-permute-start.2) | collective-permute-done | bytes 67616 | tf_op jit(solution)/shard_map/ppermute | solution.py:52
  17.6 1.6 %collective-permute-start.3 = (bf16[32,4224]{1,0:T(8,128)(2,1)S(1)}, bf16[32,4224]{1,0:T(8,128)(2,1)S(1)}, u32[]{:S(2)}, u32[]{:S(2)}) collective-permute-start(bf16[32,4224]{1,0:T(8,128)(2,1)S(1)} %pad_maximum_fusion), channel_id=1, source_target_pairs={{0,8},{1,9},{2,10},{3,11},{4,12},{5,13},{6,14},{7,15},{8,0},{9,1},... | collective-permute-start | bytes 811016 | tf_op jit(solution)/shard_map/ppermute | solution.py:52
  19.2 1.5 %collective-permute-start.4 = (bf16[32,4224]{1,0:T(8,128)(2,1)S(1)}, bf16[32,4224]{1,0:T(8,128)(2,1)S(1)}, u32[]{:S(2)}, u32[]{:S(2)}) collective-permute-start(bf16[32,4224]{1,0:T(8,128)(2,1)S(1)} %pad_maximum_fusion), channel_id=1, source_target_pairs={{0,16},{1,17},{2,18},{3,19},{4,20},{5,21},{6,22},{7,23},{8,24},{9,... | collective-permute-start | bytes 811016 | tf_op jit(solution)/shard_map/ppermute | solution.py:52
  20.7 0.5 collective-permute-start.5
  21.3 5.9 %collective-permute-done.3 = bf16[32,4224]{1,0:T(8,128)(2,1)S(1)} collective-permute-done((bf16[32,4224]{1,0:T(8,128)(2,1)S(1)}, bf16[32,4224]{1,0:T(8,128)(2,1)S(1)}, u32[]{:S(2)}, u32[]{:S(2)}) %collective-permute-start.3) | collective-permute-done | bytes 270368 | tf_op jit(solution)/shard_map/ppermute | solution.py:52
  27.2 4.1 %collective-permute-done.4 = bf16[32,4224]{1,0:T(8,128)(2,1)S(1)} collective-permute-done((bf16[32,4224]{1,0:T(8,128)(2,1)S(1)}, bf16[32,4224]{1,0:T(8,128)(2,1)S(1)}, u32[]{:S(2)}, u32[]{:S(2)}) %collective-permute-start.4) | collective-permute-done | bytes 270368 | tf_op jit(solution)/shard_map/ppermute | solution.py:52
  31.3 1.3 %copy-done.3 = bf16[256,4224]{1,0:T(8,128)(2,1)} copy-done((bf16[256,4224]{1,0:T(8,128)(2,1)}, bf16[256,4224]{1,0:T(8,128)(2,1)S(1)}, u32[]{:S(2)}) %copy-start.3) | copy-done | bytes 2162712
  32.7 2.7 %collective-permute-done.6 = bf16[128,4224]{1,0:T(8,128)(2,1)S(1)} collective-permute-done((bf16[128,4224]{1,0:T(8,128)(2,1)S(1)}, bf16[128,4224]{1,0:T(8,128)(2,1)S(1)}, u32[]{:S(2)}, u32[]{:S(2)}) %collective-permute-start.6) | collective-permute-done | bytes 1081376 | tf_op jit(solution)/shard_map/ppermute | solution.py:52
  35.4 1.1 %constant_dynamic-update-slice_fusion.7 = bf16[256,4224]{1,0:T(8,128)(2,1)} fusion(bf16[256,4224]{1,0:T(8,128)(2,1)} %copy-done.3, bf16[128,4224]{1,0:T(8,128)(2,1)S(1)} %collective-permute-done.6), kind=kLoop, calls=%fused_computation.44 | loop fusion | bytes 2162688 | tf_op jit(solution)/shard_map/concatenate | solution.py:61
  36.4 6.2 %fusion.2 = f32[256,768]{1,0:T(8,128)} fusion(bf16[1,4096,768]{2,1,0:T(8,128)(2,1)} %param.24, bf16[256,4224]{1,0:T(8,128)(2,1)} %constant_dynamic-update-slice_fusion.7), kind=kOutput, calls=%fused_computation.2 | convolution fusion | flops 1610612736 | bytes 9175040 | tf_op jit(solution)/shard_map/dot_general | solution.py:135
  42.7 0.1 select_reduce_fusion
  42.8 0.0 copy-start.7
  42.8 0.0 copy-start.2
  42.8 11.4 %fusion.6 = f32[256,4096]{1,0:T(8,128)} fusion(bf16[1,768,4096]{2,1,0:T(8,128)(2,1)} %param.25, f32[256]{0:T(256)S(1)} %select_reduce_fusion, f32[256,768]{1,0:T(8,128)} %fusion.2, bf16[1,4096,768]{2,1,0:T(8,128)(2,1)} %param.23, bf16[256,4224]{1,0:T(8,128)(2,1)S(1)} %copy-done.4), kind=kOutput, calls=%fused_computation.6 | convolution fusion | flops 3223453696 | bytes 19661824 | tf_op jit(solution)/shard_map/dot_general | solution.py:137
  54.2 1.8 %slice.84 = bf16[128,4096]{1,0:T(8,128)(2,1)S(1)} slice(f32[256,4096]{1,0:T(8,128)} %fusion.6), slice={[128:256], [0:4096]} | slice | bytes 2097152 | tf_op jit(solution)/shard_map/slice | solution.py:68
  56.0 0.2 collective-permute-start.7
  56.3 0.1 iota_compare_fusion.1
  56.3 0.2 fusion.33
  56.5 0.6 fusion.44
  57.1 0.0 copy-start.5
  57.2 1.6 %collective-permute-done.7 = bf16[128,4096]{1,0:T(8,128)(2,1)S(1)} collective-permute-done((bf16[128,4096]{1,0:T(8,128)(2,1)S(1)}, bf16[128,4096]{1,0:T(8,128)(2,1)S(1)}, u32[]{:S(2)}, u32[]{:S(2)}) %collective-permute-start.7) | collective-permute-done | bytes 1048608 | tf_op jit(solution)/shard_map/ppermute | solution.py:52
  58.8 1.9 %fusion.41 = (bf16[128,4096]{1,0:T(8,128)(2,1)S(1)}, f32[128,4096]{1,0:T(8,128)S(1)}) fusion(bf16[128,4096]{1,0:T(8,128)(2,1)S(1)} %collective-permute-done.7, f32[256,4096]{1,0:T(8,128)} %fusion.6), kind=kLoop, calls=%fused_computation.71 | loop fusion | flops 1572864 | bytes 6291456 | tf_op jit(solution)/shard_map/convert_element_type | solution.py:71
  60.7 0.1 fusion.42
  60.8 1.6 %collective-permute-start.10 = (bf16[32,4096]{1,0:T(8,128)(2,1)S(1)}, bf16[32,4096]{1,0:T(8,128)(2,1)S(1)}, u32[]{:S(2)}, u32[]{:S(2)}) collective-permute-start(bf16[32,4096]{1,0:T(8,128)(2,1)S(1)} %get-tuple-element.7), channel_id=1, source_target_pairs={{0,24},{1,25},{2,26},{3,27},{4,28},{5,29},{6,30},{7,31},{8,16},{9,... | collective-permute-start | bytes 786440 | tf_op jit(solution)/shard_map/ppermute | solution.py:52
  62.3 1.5 %collective-permute-start.8 = (bf16[32,4096]{1,0:T(8,128)(2,1)S(1)}, bf16[32,4096]{1,0:T(8,128)(2,1)S(1)}, u32[]{:S(2)}, u32[]{:S(2)}) collective-permute-start(bf16[32,4096]{1,0:T(8,128)(2,1)S(1)} %get-tuple-element.6), channel_id=1, source_target_pairs={{0,8},{1,9},{2,10},{3,11},{4,12},{5,13},{6,14},{7,15},{8,0},{9,1},... | collective-permute-start | bytes 786440 | tf_op jit(solution)/shard_map/ppermute | solution.py:52
  63.8 0.5 collective-permute-start.9
  64.3 0.3 fusion.24
  64.6 6.3 %collective-permute-done.10 = bf16[32,4096]{1,0:T(8,128)(2,1)S(1)} collective-permute-done((bf16[32,4096]{1,0:T(8,128)(2,1)S(1)}, bf16[32,4096]{1,0:T(8,128)(2,1)S(1)}, u32[]{:S(2)}, u32[]{:S(2)}) %collective-permute-start.10) | collective-permute-done | bytes 262176 | tf_op jit(solution)/shard_map/ppermute | solution.py:52
  70.9 4.9 %collective-permute-done.8 = bf16[32,4096]{1,0:T(8,128)(2,1)S(1)} collective-permute-done((bf16[32,4096]{1,0:T(8,128)(2,1)S(1)}, bf16[32,4096]{1,0:T(8,128)(2,1)S(1)}, u32[]{:S(2)}, u32[]{:S(2)}) %collective-permute-start.8) | collective-permute-done | bytes 262176 | tf_op jit(solution)/shard_map/ppermute | solution.py:52
  75.8 0.1 fusion.39
  76.0 0.8 collective-permute-start.11
  76.8 1.5 %collective-permute-start.12 = (bf16[8,4096]{1,0:T(8,128)(2,1)S(1)}, bf16[8,4096]{1,0:T(8,128)(2,1)S(1)}, u32[]{:S(2)}, u32[]{:S(2)}) collective-permute-start(bf16[8,4096]{1,0:T(8,128)(2,1)S(1)} %get-tuple-element.17), channel_id=1, source_target_pairs={{0,2},{1,3},{2,0},{3,1},{4,6},{5,7},{6,4},{7,5},{8,10},{9,11},{10,... | collective-permute-start | bytes 196616 | tf_op jit(solution)/shard_map/ppermute | solution.py:52
  78.3 2.1 %collective-permute-start.13 = (bf16[8,4096]{1,0:T(8,128)(2,1)S(1)}, bf16[8,4096]{1,0:T(8,128)(2,1)S(1)}, u32[]{:S(2)}, u32[]{:S(2)}) collective-permute-start(bf16[8,4096]{1,0:T(8,128)(2,1)S(1)} %get-tuple-element.16), channel_id=1, source_target_pairs={{0,3},{1,2},{2,1},{3,0},{4,7},{5,6},{6,5},{7,4},{8,11},{9,10},{10,... | collective-permute-start | bytes 196616 | tf_op jit(solution)/shard_map/ppermute | solution.py:52
  80.4 0.4 fusion.12
  80.8 0.8 copy.21
  81.6 3.3 %collective-permute-done.12 = bf16[8,4096]{1,0:T(8,128)(2,1)S(1)} collective-permute-done((bf16[8,4096]{1,0:T(8,128)(2,1)S(1)}, bf16[8,4096]{1,0:T(8,128)(2,1)S(1)}, u32[]{:S(2)}, u32[]{:S(2)}) %collective-permute-start.12) | collective-permute-done | bytes 65568 | tf_op jit(solution)/shard_map/ppermute | solution.py:52
  84.9 0.7 fusion.30
  (34 shorter events, 0.3 us)
Async XLA Ops:
  0.6 79.8 %copy-start = (bf16[8,4,96,128]{3,2,1,0:T(8,128)(2,1)S(1)}, bf16[8,4,96,128]{3,2,1,0:T(8,128)(2,1)}, u32[]{:S(2)}) copy-start(bf16[8,4,96,128]{3,2,1,0:T(8,128)(2,1)} %param.15) | copy-start | bytes 2359300
  5.8 5.6 %collective-permute-start = (bf16[8,4224]{1,0:T(8,128)(2,1)S(1)}, bf16[8,4224]{1,0:T(8,128)(2,1)S(1)}, u32[]{:S(2)}, u32[]{:S(2)}) collective-permute-start(bf16[8,4224]{1,0:T(8,128)(2,1)S(1)} %concatenate.14), channel_id=1, source_target_pairs={{0,1},{1,0},{2,3},{3,2},{4,5},{5,4},{6,7},{7,6},{8,9},{9,8},{10,11... | collective-permute-start | bytes 202760 | tf_op jit(solution)/shard_map/ppermute | solution.py:52
  8.8 7.4 %collective-permute-start.1 = (bf16[8,4224]{1,0:T(8,128)(2,1)S(1)}, bf16[8,4224]{1,0:T(8,128)(2,1)S(1)}, u32[]{:S(2)}, u32[]{:S(2)}) collective-permute-start(bf16[8,4224]{1,0:T(8,128)(2,1)S(1)} %concatenate.14), channel_id=1, source_target_pairs={{0,2},{1,3},{2,0},{3,1},{4,6},{5,7},{6,4},{7,5},{8,10},{9,11},{10,... | collective-permute-start | bytes 202760 | tf_op jit(solution)/shard_map/ppermute | solution.py:52
  11.4 6.2 %collective-permute-start.2 = (bf16[8,4224]{1,0:T(8,128)(2,1)S(1)}, bf16[8,4224]{1,0:T(8,128)(2,1)S(1)}, u32[]{:S(2)}, u32[]{:S(2)}) collective-permute-start(bf16[8,4224]{1,0:T(8,128)(2,1)S(1)} %concatenate.14), channel_id=1, source_target_pairs={{0,3},{1,2},{2,1},{3,0},{4,7},{5,6},{6,5},{7,4},{8,11},{9,10},{10,... | collective-permute-start | bytes 202760 | tf_op jit(solution)/shard_map/ppermute | solution.py:52
  17.6 9.5 %collective-permute-start.3 = (bf16[32,4224]{1,0:T(8,128)(2,1)S(1)}, bf16[32,4224]{1,0:T(8,128)(2,1)S(1)}, u32[]{:S(2)}, u32[]{:S(2)}) collective-permute-start(bf16[32,4224]{1,0:T(8,128)(2,1)S(1)} %pad_maximum_fusion), channel_id=1, source_target_pairs={{0,8},{1,9},{2,10},{3,11},{4,12},{5,13},{6,14},{7,15},{8,0},{9,1},... | collective-permute-start | bytes 811016 | tf_op jit(solution)/shard_map/ppermute | solution.py:52
  19.2 12.0 %collective-permute-start.4 = (bf16[32,4224]{1,0:T(8,128)(2,1)S(1)}, bf16[32,4224]{1,0:T(8,128)(2,1)S(1)}, u32[]{:S(2)}, u32[]{:S(2)}) collective-permute-start(bf16[32,4224]{1,0:T(8,128)(2,1)S(1)} %pad_maximum_fusion), channel_id=1, source_target_pairs={{0,16},{1,17},{2,18},{3,19},{4,20},{5,21},{6,22},{7,23},{8,24},{9,... | collective-permute-start | bytes 811016 | tf_op jit(solution)/shard_map/ppermute | solution.py:52
  20.7 10.5 %collective-permute-start.5 = (bf16[32,4224]{1,0:T(8,128)(2,1)S(1)}, bf16[32,4224]{1,0:T(8,128)(2,1)S(1)}, u32[]{:S(2)}, u32[]{:S(2)}) collective-permute-start(bf16[32,4224]{1,0:T(8,128)(2,1)S(1)} %pad_maximum_fusion), channel_id=1, source_target_pairs={{0,24},{1,25},{2,26},{3,27},{4,28},{5,29},{6,30},{7,31},{8,16},{9,... | collective-permute-start | bytes 811016 | tf_op jit(solution)/shard_map/ppermute | solution.py:52
  31.3 1.3 %copy-start.3 = (bf16[256,4224]{1,0:T(8,128)(2,1)}, bf16[256,4224]{1,0:T(8,128)(2,1)S(1)}, u32[]{:S(2)}) copy-start(bf16[256,4224]{1,0:T(8,128)(2,1)S(1)} %get-tuple-element.10) | copy-start | bytes 6488068
  32.7 2.7 %collective-permute-start.6 = (bf16[128,4224]{1,0:T(8,128)(2,1)S(1)}, bf16[128,4224]{1,0:T(8,128)(2,1)S(1)}, u32[]{:S(2)}, u32[]{:S(2)}) collective-permute-start(bf16[128,4224]{1,0:T(8,128)(2,1)S(1)} %get-tuple-element.9), channel_id=1, source_target_pairs={{0,4},{1,5},{2,6},{3,7},{4,0},{5,1},{6,2},{7,3},{8,12},{9,13},{10,... | collective-permute-start | bytes 3244040 | tf_op jit(solution)/shard_map/ppermute | solution.py:52
  36.4 6.3 %copy-start.4 = (bf16[256,4224]{1,0:T(8,128)(2,1)S(1)}, bf16[256,4224]{1,0:T(8,128)(2,1)}, u32[]{:S(2)}) copy-start(bf16[256,4224]{1,0:T(8,128)(2,1)} %constant_dynamic-update-slice_fusion.7) | copy-start | bytes 6488068
  42.8 13.5 %copy-start.7 = (s32[8]{0:T(128)S(1)}, s32[8]{0:T(128)}, u32[]{:S(2)}) copy-start(s32[8]{0:T(128)} %param.18) | copy-start | bytes 100
  42.8 13.5 %copy-start.2 = (bf16[8,64,128]{2,1,0:T(8,128)(2,1)S(1)}, bf16[8,64,128]{2,1,0:T(8,128)(2,1)}, u32[]{:S(2)}) copy-start(bf16[8,64,128]{2,1,0:T(8,128)(2,1)} %param.13) | copy-start | bytes 393220
  42.8 13.5 %copy-start.6 = (bf16[8,4,128]{2,1,0:T(4,128)(2,1)S(1)}, bf16[8,4,128]{2,1,0:T(4,128)(2,1)}, u32[]{:S(2)}) copy-start(bf16[8,4,128]{2,1,0:T(4,128)(2,1)} %param.16) | copy-start | bytes 24580
  54.2 2.3 %copy-start.1 = (bf16[8,4,96,128]{3,2,1,0:T(8,128)(2,1)S(1)}, bf16[8,4,96,128]{3,2,1,0:T(8,128)(2,1)}, u32[]{:S(2)}) copy-start(bf16[8,4,96,128]{3,2,1,0:T(8,128)(2,1)} %param.14) | copy-start | bytes 2359300
  56.0 2.7 %collective-permute-start.7 = (bf16[128,4096]{1,0:T(8,128)(2,1)S(1)}, bf16[128,4096]{1,0:T(8,128)(2,1)S(1)}, u32[]{:S(2)}, u32[]{:S(2)}) collective-permute-start(bf16[128,4096]{1,0:T(8,128)(2,1)S(1)} %slice.84), channel_id=1, source_target_pairs={{0,4},{1,5},{2,6},{3,7},{4,0},{5,1},{6,2},{7,3},{8,12},{9,13},{10,... | collective-permute-start | bytes 3145736 | tf_op jit(solution)/shard_map/ppermute | solution.py:52
  57.1 7.5 %copy-start.5 = (bf16[8,4,128]{2,1,0:T(4,128)(2,1)S(1)}, bf16[8,4,128]{2,1,0:T(4,128)(2,1)}, u32[]{:S(2)}) copy-start(bf16[8,4,128]{2,1,0:T(4,128)(2,1)} %param.17) | copy-start | bytes 24580
  60.8 10.2 %collective-permute-start.10 = (bf16[32,4096]{1,0:T(8,128)(2,1)S(1)}, bf16[32,4096]{1,0:T(8,128)(2,1)S(1)}, u32[]{:S(2)}, u32[]{:S(2)}) collective-permute-start(bf16[32,4096]{1,0:T(8,128)(2,1)S(1)} %get-tuple-element.7), channel_id=1, source_target_pairs={{0,24},{1,25},{2,26},{3,27},{4,28},{5,29},{6,30},{7,31},{8,16},{9,... | collective-permute-start | bytes 786440 | tf_op jit(solution)/shard_map/ppermute | solution.py:52
  62.3 13.5 %collective-permute-start.8 = (bf16[32,4096]{1,0:T(8,128)(2,1)S(1)}, bf16[32,4096]{1,0:T(8,128)(2,1)S(1)}, u32[]{:S(2)}, u32[]{:S(2)}) collective-permute-start(bf16[32,4096]{1,0:T(8,128)(2,1)S(1)} %get-tuple-element.6), channel_id=1, source_target_pairs={{0,8},{1,9},{2,10},{3,11},{4,12},{5,13},{6,14},{7,15},{8,0},{9,1},... | collective-permute-start | bytes 786440 | tf_op jit(solution)/shard_map/ppermute | solution.py:52
  63.8 12.0 %collective-permute-start.9 = (bf16[32,4096]{1,0:T(8,128)(2,1)S(1)}, bf16[32,4096]{1,0:T(8,128)(2,1)S(1)}, u32[]{:S(2)}, u32[]{:S(2)}) collective-permute-start(bf16[32,4096]{1,0:T(8,128)(2,1)S(1)} %get-tuple-element.8), channel_id=1, source_target_pairs={{0,16},{1,17},{2,18},{3,19},{4,20},{5,21},{6,22},{7,23},{8,24},{9,... | collective-permute-start | bytes 786440 | tf_op jit(solution)/shard_map/ppermute | solution.py:52
  76.0 5.6 %collective-permute-start.11 = (bf16[8,4096]{1,0:T(8,128)(2,1)S(1)}, bf16[8,4096]{1,0:T(8,128)(2,1)S(1)}, u32[]{:S(2)}, u32[]{:S(2)}) collective-permute-start(bf16[8,4096]{1,0:T(8,128)(2,1)S(1)} %get-tuple-element.15), channel_id=1, source_target_pairs={{0,1},{1,0},{2,3},{3,2},{4,5},{5,4},{6,7},{7,6},{8,9},{9,8},{10,11... | collective-permute-start | bytes 196616 | tf_op jit(solution)/shard_map/ppermute | solution.py:52
  76.8 8.1 %collective-permute-start.12 = (bf16[8,4096]{1,0:T(8,128)(2,1)S(1)}, bf16[8,4096]{1,0:T(8,128)(2,1)S(1)}, u32[]{:S(2)}, u32[]{:S(2)}) collective-permute-start(bf16[8,4096]{1,0:T(8,128)(2,1)S(1)} %get-tuple-element.17), channel_id=1, source_target_pairs={{0,2},{1,3},{2,0},{3,1},{4,6},{5,7},{6,4},{7,5},{8,10},{9,11},{10,... | collective-permute-start | bytes 196616 | tf_op jit(solution)/shard_map/ppermute | solution.py:52
  78.3 6.6 %collective-permute-start.13 = (bf16[8,4096]{1,0:T(8,128)(2,1)S(1)}, bf16[8,4096]{1,0:T(8,128)(2,1)S(1)}, u32[]{:S(2)}, u32[]{:S(2)}) collective-permute-start(bf16[8,4096]{1,0:T(8,128)(2,1)S(1)} %get-tuple-element.16), channel_id=1, source_target_pairs={{0,3},{1,2},{2,1},{3,0},{4,7},{5,6},{6,5},{7,4},{8,11},{9,10},{10,... | collective-permute-start | bytes 196616 | tf_op jit(solution)/shard_map/ppermute | solution.py:52

commit v2 on v0

v2 whole, which is shorter than its diff:
```python
import functools
import math

import jax
import jax.numpy as jnp
from jax import lax
from jax.experimental import pallas as pl
from jax.experimental.pallas import tpu as pltpu
from jax.sharding import PartitionSpec as P


def attend(queries, key_cache, value_cache, fresh_token_keys, new_values, lengths):
    request_count, head_count, head_width = queries.shape
    kv_heads = key_cache.shape[1]
    slot_count = key_cache.shape[2]
    grouped_queries = queries.reshape(request_count, kv_heads, head_count // kv_heads, head_width)
    inverse_scale = 1.0 / math.sqrt(head_width)
    scores = (
        jnp.einsum(
            "bkgd,bkpd->bkgp", grouped_queries, key_cache, preferred_element_type=jnp.float32
        )
        * inverse_scale
    )
    positions = jnp.arange(slot_count, dtype=jnp.int32)
    in_range = positions[None, :] < lengths[:, None]
    scores = jnp.where(in_range[:, None, None, :], scores, -jnp.inf)
    self_token_score = (
        jnp.einsum(
            "uxea,uxa->uxe", grouped_queries, fresh_token_keys, preferred_element_type=jnp.float32
        )
        * inverse_scale
    )
    highest = jnp.maximum(jnp.max(scores, axis=-1), self_token_score)
    exponent = jnp.exp(scores - highest[..., None])
    own_exponent = jnp.exp(self_token_score - highest)
    denominator = jnp.sum(exponent, axis=-1) + own_exponent
    probs = (exponent / denominator[..., None]).astype(jnp.bfloat16)
    own_prob = (own_exponent / denominator).astype(jnp.bfloat16)
    mixed = jnp.einsum("bkgp,bkpd->bkgd", probs, value_cache, preferred_element_type=jnp.float32)
    mixed = (
        mixed
        + own_prob.astype(jnp.float32)[..., None] * new_values.astype(jnp.float32)[:, :, None, :]
    )
    return mixed.reshape(request_count, head_count * head_width).astype(jnp.bfloat16)


MIB = 1024 * 1024
TILE = 256
DOWN_TILE = 1024
LOAD_LIMIT = 34 * MIB


def whole(space):
    return pl.BlockSpec(memory_space=space)


def prepare_kernel(
    experts, hidden_hbm, gain_hbm, ids_hbm, scores_hbm, out_ref, hidden_ref, gain_ref, ids_ref, scores_ref, sems
):
    pairs = ((hidden_hbm, hidden_ref), (gain_hbm, gain_ref), (ids_hbm, ids_ref), (scores_hbm, scores_ref))
    copies = [pltpu.make_async_copy(a, b, sems.at[n]) for n, (a, b) in enumerate(pairs)]
    for copy in copies:
        copy.start()
    for copy in copies:
        copy.wait()
    width = hidden_ref.shape[1]
    hidden = hidden_ref[...].astype(jnp.float32)
    mean_square = jnp.mean(hidden * hidden, axis=1, keepdims=True)
    gain = gain_ref[...].astype(jnp.float32).reshape(1, width)
    out_ref[:, :width] = (hidden * lax.rsqrt(mean_square + 1e-06) * gain).astype(jnp.bfloat16)
    scores = scores_ref[...]
    gates = scores / jnp.sum(scores, axis=1, keepdims=True)
    ids = ids_ref[...]
    rows, extra = out_ref.shape[0], out_ref.shape[1] - width
    column = lax.broadcasted_iota(jnp.int32, (rows, extra), 1)
    expert = jnp.where(column < experts, column, column - experts)
    table = jnp.zeros((rows, extra), jnp.float32)
    for j in range(ids.shape[1]):
        table = table + jnp.where(ids[:, j : j + 1] == expert, gates[:, j : j + 1], 0.0)
    coarse = table.astype(jnp.bfloat16).astype(jnp.float32)
    parts = jnp.where(column < experts, coarse, jnp.where(column < 2 * experts, table - coarse, 0.0))
    out_ref[:, width:] = parts.astype(jnp.bfloat16)


def prepare(hidden_rows, norm_gain, expert_ids, route_scores, experts):
    rows, width = hidden_rows.shape
    extra = -(-2 * experts // 128) * 128
    args = (hidden_rows, norm_gain, expert_ids, route_scores)
    return pl.pallas_call(
        functools.partial(prepare_kernel, experts),
        out_shape=pltpu.VMEM((rows, width + extra), jnp.bfloat16),
        in_specs=[whole(pltpu.HBM)] * 4,
        out_specs=whole(pltpu.VMEM),
        scratch_shapes=[pltpu.VMEM(a.shape, a.dtype) for a in args] + [pltpu.SemaphoreType.DMA((4,))],
        compiler_params=pltpu.CompilerParams(vmem_limit_bytes=56 * MIB),
        name="prepare",
    )(*args)


def pack_kernel(tail, after, *refs):
    refs = refs[after:]
    out_ref, tail_ref = refs[-2:] if tail else (refs[-1], None)
    refs = refs[: -2 if tail else -1]
    start, inner = 0, 0
    for n, ref in enumerate(refs):
        out_ref[start : start + ref.shape[0], :] = ref[...]
        start += ref.shape[0]
        if n >= len(refs) - tail:
            tail_ref[inner : inner + ref.shape[0], :] = ref[...]
            inner += ref.shape[0]


def pack(pieces, tail=0, after=()):
    width, dtype = pieces[0].shape[1], pieces[0].dtype

    def out(pieces):
        return pltpu.VMEM((sum(piece.shape[0] for piece in pieces), width), dtype)

    vmem = whole(pltpu.VMEM)
    return pl.pallas_call(
        functools.partial(pack_kernel, tail, len(after)),
        out_shape=(out(pieces), out(pieces[-tail:])) if tail else out(pieces),
        in_specs=[whole(pl.ANY)] * len(after) + [vmem] * len(pieces),
        out_specs=(vmem, vmem) if tail else vmem,
        compiler_params=pltpu.CompilerParams(vmem_limit_bytes=MIB),
        name="pack",
    )(*after, *pieces)


def experts_kernel(experts, load, *refs):
    if load:
        own_ref, here_ref, there_ref = refs[:3]
        sources, (out_here, out_there), held, scratch = refs[3:6], refs[6:8], refs[8:11], refs[11:]
        rows_v, act_v, sems = scratch
    else:
        own_ref, here_ref, there_ref = refs[:3]
        held, (out_here, out_there), (rows_v, act_v) = refs[3:6], refs[6:8], refs[8:]
    gate_ref, up_ref, down_ref = held
    hidden, width = down_ref.shape
    cuts = [pl.ds(t, TILE) for t in range(0, hidden, TILE)]
    down_cuts = [pl.ds(t, DOWN_TILE) for t in range(0, width, DOWN_TILE)]
    copies, waits = [], iter(())
    if load:
        order = [(n, cut) for cut in cuts for n in (0, 1)] + [(2, cut) for cut in down_cuts]
        for k, (n, cut) in enumerate(order):
            copies.append(
                pltpu.make_async_copy(sources[n].at[0, :, cut], held[n].at[:, cut], sems.at[k])
            )
        for copy in copies:
            copy.start()
        waits = iter(copies)

    def arrive(count):
        for _ in range(count if load else 0):
            next(waits).wait()

    half = here_ref.shape[0]
    rows_v[:half, :] = here_ref[:, :width]
    rows_v[half:, :] = there_ref[:, :width]
    column = lax.broadcasted_iota(jnp.int32, (1, here_ref.shape[1] - width), 1)
    mine = (column == own_ref[0]) | (column == own_ref[0] + experts)

    def weights_of(ref):
        parts = jnp.where(mine, ref[:, width:].astype(jnp.float32), 0.0)
        return jnp.sum(parts, axis=1, keepdims=True)

    weight_here, weight_there = weights_of(here_ref), weights_of(there_ref)
    for cut in cuts:
        arrive(2)
        gate = jnp.dot(rows_v[...], gate_ref[:, cut], preferred_element_type=jnp.float32)
        up = jnp.dot(rows_v[...], up_ref[:, cut], preferred_element_type=jnp.float32)
        act_v[:, cut] = (gate / (1.0 + jnp.exp(-gate)) * up).astype(jnp.bfloat16)
    for cut in down_cuts:
        arrive(1)
        produced = jnp.dot(act_v[...], down_ref[:, cut], preferred_element_type=jnp.float32)
        out_here[:, cut] = (weight_here * produced[:half]).astype(jnp.bfloat16)
        out_there[:, cut] = (weight_there * produced[half:]).astype(jnp.bfloat16)


def expert_piece(here, there, own, experts, pieces, load):
    half = here.shape[0]
    hidden, width = pieces[2].shape[-2:]
    out = pltpu.VMEM((half, width), jnp.bfloat16)
    vmem = whole(pltpu.VMEM)
    held = [pltpu.VMEM(piece.shape[1:], piece.dtype) for piece in pieces] if load else []
    scratch = [
        pltpu.VMEM((2 * half, width), jnp.bfloat16),
        pltpu.VMEM((2 * half, hidden), jnp.bfloat16),
    ]
    if load:
        scratch.append(pltpu.SemaphoreType.DMA((2 * (hidden // TILE) + width // DOWN_TILE,)))
    limit = LOAD_LIMIT if load else 64 * half * 1024 + 4 * MIB
    return pl.pallas_call(
        functools.partial(experts_kernel, experts, load),
        out_shape=(out, out, *held),
        in_specs=[whole(pltpu.SMEM), vmem, vmem] + [whole(pltpu.HBM) if load else vmem] * 3,
        out_specs=(vmem,) * (2 + len(held)),
        scratch_shapes=scratch,
        compiler_params=pltpu.CompilerParams(vmem_limit_bytes=limit),
        cost_estimate=pl.CostEstimate(
            flops=12 * half * width * hidden,
            bytes_accessed=6 * width * hidden if load else 0,
            transcendentals=2 * half * hidden,
        ),
        name="expert_piece",
    )(own.reshape(1), here, there, *pieces)


def exchange(rows, node_mask, local_mask):
    nodes = lax.axis_size("node")
    locals_ = lax.axis_size("local")
    pairs = [
        (n * locals_ + k, (n ^ node_mask) * locals_ + (k ^ local_mask))
        for n in range(nodes)
        for k in range(locals_)
    ]
    return lax.ppermute(rows, ("node", "local"), pairs)


def masks():
    far = list(range(2, lax.axis_size("local"))) + [1]
    return far, [lax.axis_size("node") - 2] + list(range(2, lax.axis_size("node") - 2, 2))


def gather_first(rows):
    far, plane = masks()
    line = [exchange(rows, 0, k) for k in far]
    beside = [exchange(rows, n, 0) for n in plane]
    return pack([rows] + beside + line, tail=len(far))


def gather_second(line, after):
    return pack([exchange(line, n, 0) for n in masks()[1]], after=(after,))


def scatter_sum(first, first_other, second, second_other, count):
    far, plane = masks()
    lines = len(far) * count
    cut = first.shape[0] - lines

    def f32(x):
        return x.astype(jnp.float32)

    def block(x, size, i):
        return x[i * size : (i + 1) * size]

    sums = f32(first) + f32(exchange(first_other, 1, 0))
    beside = sums[count:cut].astype(jnp.bfloat16)
    own, line = sums[:count], sums[cut:]
    for i, n in enumerate(plane):
        own = own + f32(exchange(block(beside, count, i), n, 0))
    sums = (f32(second) + f32(exchange(second_other, 1, 0))).astype(jnp.bfloat16)
    sums, own = lax.optimization_barrier((sums, own))
    for i, n in enumerate(plane):
        line = line + f32(exchange(block(sums, lines, i), n, 0))
    line = line.astype(jnp.bfloat16)
    for i, k in enumerate(far):
        own = own + f32(exchange(block(line, count, i), 0, k))
    return own.astype(jnp.bfloat16)


def per_device(
    queries,
    key_cache,
    value_cache,
    fresh_token_keys,
    new_values,
    lengths,
    hidden_rows,
    norm_gain,
    expert_ids,
    route_scores,
    gate_weight,
    up_weight,
    down_weight,
):
    context = attend(queries, key_cache, value_cache, fresh_token_keys, new_values, lengths)
    experts = lax.axis_size("node") * lax.axis_size("local") // 2
    own = (lax.axis_index("node") * lax.axis_size("local") + lax.axis_index("local")) // 2
    outgoing = prepare(hidden_rows, norm_gain, expert_ids, route_scores, experts)
    pieces = (gate_weight, up_weight, down_weight)
    first, line = gather_first(outgoing)
    first, first_other, *pieces = expert_piece(first, exchange(first, 1, 0), own, experts, pieces, True)
    second, first_other = lax.optimization_barrier((gather_second(line, first), first_other))
    second, second_other = expert_piece(
        second, exchange(second, 1, 0), own, experts, pieces, False
    )
    total = scatter_sum(first, first_other, second, second_other, hidden_rows.shape[0])
    return (context, total)


def solution(mesh):
    placed = (
        P(("group", "node", "local"), None, None),
        P(("group", "node", "local"), None, None, None),
        P(("group", "node", "local"), None, None, None),
        P(("group", "node", "local"), None, None),
        P(("group", "node", "local"), None, None),
        P(("group", "node", "local")),
        P(("group", "node", "local"), None),
        P(),
        P(("group", "node", "local"), None),
        P(("group", "node", "local"), None),
        P(("node", "local"), None, None),
        P(("node", "local"), None, None),
        P(("node", "local"), None, None),
    )
    return jax.shard_map(
        per_device,
        mesh=mesh,
        in_specs=placed,
        out_specs=(P(("group", "node", "local"), None), P(("group", "node", "local"), None)),
        check_vma=False,
    )
```

time: 171 us -> 62.2 us (0.36)
  waiting for transfers between devices: 89.5 us -> 20.3 us
  blocking collectives: 54.6 us -> 0 us
  starting transfers between devices: 4.59 us -> 24.1 us
  Pallas kernels: 0 us -> 11.5 us
  matrix products: 11.9 us -> 2.37 us
  other arithmetic: 6.22 us -> 2.1 us
    all_to_all x1 -> x0, waiting for transfers between devices: 89.5 us -> none  [per_device(): lax.all_to_all(partial_value, ('node', 'local'), split_axis=0, concat_axi...]
    all_to_all x1 -> x0, blocking collectives: 54.6 us -> none  [per_device(): lax.all_to_all(doubled, ('node', 'local'), split_axis=0, concat_axis=0, t...]
    ppermute x0 -> x22, starting transfers between devices: none -> 24.1 us  [exchange(): return lax.ppermute(rows, ('node', 'local'), pairs)]
    ppermute x0 -> x22, waiting for transfers between devices: none -> 20.3 us  [exchange(): return lax.ppermute(rows, ('node', 'local'), pairs)]
    pallas_call x0 -> x5, Pallas kernels: none -> 11.5 us  [the longest x2 10.3 us: expert_piece(): pl.pallas_call(functools.partial(experts_kernel, experts, load), out_shap...]
    dot_general x5 -> x0, matrix products: 10.7 us -> none  [the longest x1 3.86 us: routed_expert_rows(): return jnp.dot(activated, down_piece, preferred_element_type=jnp.float32)]
    all_to_all x1 -> x0, starting transfers between devices: 4.59 us -> none  [per_device(): lax.all_to_all(partial_value, ('node', 'local'), split_axis=0, concat_axi...]
    reduce_sum x5 -> x0, other arithmetic: 4.06 us -> none  [the longest x1 2.68 us: per_device(): jnp.sum(returned.reshape(experts, 2, capacity, model_width), axis=1)]
  transfers between devices with their start and end apart: 1 -> 22, of which waited for: 1 -> 12; matrix products, arithmetic and copies ran while one was open for 2% -> 7% of each run, Pallas kernels for 0% -> 17%
where the time goes in v2:
time: 62.2 us; the launch traced here: 62.1 us
  starting transfers between devices  24.1 us (39%)
  waiting for transfers between devices  20.3 us (33%)
  Pallas kernels  11.5 us (18%)
  matrix products  2.37 us (4%)
  other arithmetic  2.1 us (3%)
  between operations  0.86 us (1%)
  local copies, waits for them, and re-layouts  0.85 us (1%)
    ppermute x22, starting transfers between devices, exchange(): return lax.ppermute(rows, ('node', 'local'), pairs)  24.1 us
    ppermute x22, waiting for transfers between devices, exchange(): return lax.ppermute(rows, ('node', 'local'), pairs)  20.3 us
    pallas_call x2, Pallas kernels, expert_piece(): pl.pallas_call(functools.partial(experts_kernel, experts, load), out_shap...  10.3 us
    dot_general x1, matrix products, attend(): jnp.einsum('bkgd,bkpd->bkgp', grouped_queries, key_cache, preferred_eleme...  1.81 us
  transfers between devices with their start and end apart: 22, of which 12 were waited for; matrix products, arithmetic and copies ran while one was open for 7% of the time, Pallas kernels for 17%

profile of v2, /device:TPU:0, one launch (start us, length us, event | category | flops | bytes accessed | tf_op | source)
XLA Modules:
  0.0 62.1 jit_solution(7128479464126117960)
XLA Ops:
  0.6 1.1 %prepare.1.refs_0_ = bf16[8,4224]{1,0:T(8,128)(2,1)S(1)} custom-call(bf16[8,4096]{1,0:T(8,128)(2,1)} %hidden_hbm.1, bf16[4096]{0:T(1024)(128)(2,1)} %gain_hbm.1, s32[8,8]{1,0:T(8,128)} %ids_hbm.1, f32[8,8]{1,0:T(8,128)} %scores_hbm.1), custom_call_target="tpu_custom_call" | custom-call | tf_op jit(solution)/shard_map/prepare/pallas_call | solution.py:89
  1.8 4.0 %collective-permute-start = (bf16[8,4224]{1,0:T(8,128)(2,1)S(1)}, bf16[8,4224]{1,0:T(8,128)(2,1)S(1)}, u32[]{:S(2)}, u32[]{:S(2)}) collective-permute-start(bf16[8,4224]{1,0:T(8,128)(2,1)S(1)} %prepare.1.refs_0_), channel_id=1, source_target_pairs={{0,24},{1,25},{2,26},{3,27},{4,28},{5,29},{6,30},{7,31},{8,16},{9,... | collective-permute-start | bytes 202760 | tf_op jit(solution)/shard_map/ppermute | solution.py:217
  5.8 0.5 collective-permute-start.1
  6.3 0.1 collective-permute-start.2
  6.4 3.0 %collective-permute-start.3 = (bf16[8,4224]{1,0:T(8,128)(2,1)S(1)}, bf16[8,4224]{1,0:T(8,128)(2,1)S(1)}, u32[]{:S(2)}, u32[]{:S(2)}) collective-permute-start(bf16[8,4224]{1,0:T(8,128)(2,1)S(1)} %prepare.1.refs_0_), channel_id=1, source_target_pairs={{0,2},{1,3},{2,0},{3,1},{4,6},{5,7},{6,4},{7,5},{8,10},{9,11},{10,... | collective-permute-start | bytes 202760 | tf_op jit(solution)/shard_map/ppermute | solution.py:217
  9.4 1.3 %collective-permute-start.4 = (bf16[8,4224]{1,0:T(8,128)(2,1)S(1)}, bf16[8,4224]{1,0:T(8,128)(2,1)S(1)}, u32[]{:S(2)}, u32[]{:S(2)}) collective-permute-start(bf16[8,4224]{1,0:T(8,128)(2,1)S(1)} %prepare.1.refs_0_), channel_id=1, source_target_pairs={{0,3},{1,2},{2,1},{3,0},{4,7},{5,6},{6,5},{7,4},{8,11},{9,10},{10,... | collective-permute-start | bytes 202760 | tf_op jit(solution)/shard_map/ppermute | solution.py:217
  10.7 0.2 collective-permute-start.5
  11.0 0.8 %collective-permute-done.3.refs_4_ = bf16[8,4224]{1,0:T(8,128)(2,1)S(1)} collective-permute-done((bf16[8,4224]{1,0:T(8,128)(2,1)S(1)}, bf16[8,4224]{1,0:T(8,128)(2,1)S(1)}, u32[]{:S(2)}, u32[]{:S(2)}) %collective-permute-start.3) | collective-permute-done | bytes 67616 | tf_op jit(solution)/shard_map/ppermute | solution.py:217
  11.8 3.8 %collective-permute-done.4.refs_5_ = bf16[8,4224]{1,0:T(8,128)(2,1)S(1)} collective-permute-done((bf16[8,4224]{1,0:T(8,128)(2,1)S(1)}, bf16[8,4224]{1,0:T(8,128)(2,1)S(1)}, u32[]{:S(2)}, u32[]{:S(2)}) %collective-permute-start.4) | collective-permute-done | bytes 67616 | tf_op jit(solution)/shard_map/ppermute | solution.py:217
  15.6 0.2 collective-permute-done.5.refs_6_
  15.8 0.1 collective-permute-start.6
  15.9 0.7 %iota_compare_fusion = pred[8,96]{1,0:T(8,128)(4,1)S(1)} fusion(s32[8]{0:T(128)} %param.18), kind=kLoop, calls=%fused_computation.26 | loop fusion | flops 768 | bytes 800 | tf_op jit(solution)/shard_map/lt | solution.py:25
  16.6 2.4 %collective-permute-start.7 = (bf16[24,4224]{1,0:T(8,128)(2,1)S(1)}, bf16[24,4224]{1,0:T(8,128)(2,1)S(1)}, u32[]{:S(2)}, u32[]{:S(2)}) collective-permute-start(bf16[24,4224]{1,0:T(8,128)(2,1)S(1)} %get-tuple-element.17), channel_id=1, source_target_pairs={{0,24},{1,25},{2,26},{3,27},{4,28},{5,29},{6,30},{7,31},{8,16},{9,... | collective-permute-start | bytes 608264 | tf_op jit(solution)/shard_map/ppermute | solution.py:217
  19.1 0.5 collective-permute-start.8
  19.6 0.5 collective-permute-start.9
  20.1 1.8 %fusion.18 = (f32[8,4,16]{2,1,0:T(4,128)S(1)}, f32[8,4,16,96]{3,2,1,0:T(8,128)S(1)}) fusion(bf16[8,4,16,128]{3,2,1,0:T(8,128)(2,1)} %bitcast.16, bf16[8,4,96,128]{3,2,1,0:T(8,128)(2,1)} %param.14, pred[8,96]{1,0:T(8,128)(4,1)S(1)} %iota_compare_fusion), kind=kOutput, calls=%fused_computation.32 | convolution fusion | flops 12729856 | bytes 1116928 | tf_op jit(solution)/shard_map/bkgd,bkpd->bkgp/dot_general | solution.py:19
  22.0 7.3 %expert_piece.2 = (bf16[56,4096]{1,0:T(8,128)(2,1)S(1)}, bf16[56,4096]{1,0:T(8,128)(2,1)S(1)}, bf16[4096,768]{1,0:T(8,128)(2,1)S(1)}, bf16[4096,768]{1,0:T(8,128)(2,1)S(1)}, bf16[768,4096]{1,0:T(8,128)(2,1)S(1)}) custom-call(s32[1]{0:T(128)} %bitcast.4.refs_0_, bf16[56,4224]{1,0:T(8,128)(2,1)S(1)} %get-tuple-element.15.refs_1_, ...), custom_call_target="tpu_custom_call" | custom-call | flops 2113929216 | bytes 18874368 | tf_op jit(solution)/shard_map/expert_piece/pallas_call | solution.py:193
  29.2 0.1 collective-permute-done.8.refs_2_
  29.4 0.1 collective-permute-start.12
  29.5 0.2 fusion.10
  29.8 0.3 fusion.5
  30.0 0.5 collective-permute-start.10
  30.6 0.7 %collective-permute-done.12 = bf16[56,4096]{1,0:T(8,128)(2,1)S(1)} collective-permute-done((bf16[56,4096]{1,0:T(8,128)(2,1)S(1)}, bf16[56,4096]{1,0:T(8,128)(2,1)S(1)}, u32[]{:S(2)}, u32[]{:S(2)}) %collective-permute-start.12) | collective-permute-done | bytes 458784 | tf_op jit(solution)/shard_map/ppermute | solution.py:217
  31.3 0.1 fusion.14
  31.5 2.4 %collective-permute-start.13 = (bf16[8,4096]{1,0:T(8,128)(2,1)S(1)}, bf16[8,4096]{1,0:T(8,128)(2,1)S(1)}, u32[]{:S(2)}, u32[]{:S(2)}) collective-permute-start(bf16[8,4096]{1,0:T(8,128)(2,1)S(1)} %get-tuple-element.33), channel_id=1, source_target_pairs={{0,24},{1,25},{2,26},{3,27},{4,28},{5,29},{6,30},{7,31},{8,16},{9,... | collective-permute-start | bytes 196616 | tf_op jit(solution)/shard_map/ppermute | solution.py:217
  33.9 0.5 collective-permute-start.14
  34.4 0.6 collective-permute-start.15
  35.0 3.0 %expert_piece.3 = (bf16[72,4096]{1,0:T(8,128)(2,1)S(1)}, bf16[72,4096]{1,0:T(8,128)(2,1)S(1)}) custom-call(s32[1]{0:T(128)} %bitcast.4.refs_0_, bf16[72,4224]{1,0:T(8,128)(2,1)S(1)} %pack.3.refs_1_, bf16[72,4224]{1,0:T(8,128)(2,1)S(1)} %collective-permute-done.10.refs_2_, bf16[4096,768]{1,0:T(8,128)(2,1)S(1)} %get-tuple-element.20.refs_3_, ...), custom_call_target="tpu_custom_call" | custom-call | flops 2717908992 | tf_op jit(solution)/shard_map/expert_piece/pallas_call | solution.py:193
  38.0 0.1 collective-permute-start.11
  38.1 0.0 collective-permute-done.14
  38.1 0.5 collective-permute-done.15
  38.7 1.4 %collective-permute-done.11 = bf16[72,4096]{1,0:T(8,128)(2,1)S(1)} collective-permute-done((bf16[72,4096]{1,0:T(8,128)(2,1)S(1)}, bf16[72,4096]{1,0:T(8,128)(2,1)S(1)}, u32[]{:S(2)}, u32[]{:S(2)}) %collective-permute-start.11) | collective-permute-done | bytes 589856 | tf_op jit(solution)/shard_map/ppermute | solution.py:217
  40.1 0.1 add_convert_fusion
  40.3 2.4 %collective-permute-start.16 = (bf16[24,4096]{1,0:T(8,128)(2,1)S(1)}, bf16[24,4096]{1,0:T(8,128)(2,1)S(1)}, u32[]{:S(2)}, u32[]{:S(2)}) collective-permute-start(bf16[24,4096]{1,0:T(8,128)(2,1)S(1)} %get-tuple-element.30), channel_id=1, source_target_pairs={{0,24},{1,25},{2,26},{3,27},{4,28},{5,29},{6,30},{7,31},{8,16},{9,... | collective-permute-start | bytes 589832 | tf_op jit(solution)/shard_map/ppermute | solution.py:217
  42.7 0.5 collective-permute-start.17
  43.2 0.6 collective-permute-start.18
  43.9 5.2 %collective-permute-done.16 = bf16[24,4096]{1,0:T(8,128)(2,1)S(1)} collective-permute-done((bf16[24,4096]{1,0:T(8,128)(2,1)S(1)}, bf16[24,4096]{1,0:T(8,128)(2,1)S(1)}, u32[]{:S(2)}, u32[]{:S(2)}) %collective-permute-start.16) | collective-permute-done | bytes 196640 | tf_op jit(solution)/shard_map/ppermute | solution.py:217
  49.1 3.4 %collective-permute-done.17 = bf16[24,4096]{1,0:T(8,128)(2,1)S(1)} collective-permute-done((bf16[24,4096]{1,0:T(8,128)(2,1)S(1)}, bf16[24,4096]{1,0:T(8,128)(2,1)S(1)}, u32[]{:S(2)}, u32[]{:S(2)}) %collective-permute-start.17) | collective-permute-done | bytes 196640 | tf_op jit(solution)/shard_map/ppermute | solution.py:217
  52.4 0.1 fusion.4
  52.6 2.0 %collective-permute-start.19 = (bf16[8,4096]{1,0:T(8,128)(2,1)S(1)}, bf16[8,4096]{1,0:T(8,128)(2,1)S(1)}, u32[]{:S(2)}, u32[]{:S(2)}) collective-permute-start(bf16[8,4096]{1,0:T(8,128)(2,1)S(1)} %get-tuple-element.36), channel_id=1, source_target_pairs={{0,2},{1,3},{2,0},{3,1},{4,6},{5,7},{6,4},{7,5},{8,10},{9,11},{10,... | collective-permute-start | bytes 196616 | tf_op jit(solution)/shard_map/ppermute | solution.py:217
  54.5 0.9 %collective-permute-start.20 = (bf16[8,4096]{1,0:T(8,128)(2,1)S(1)}, bf16[8,4096]{1,0:T(8,128)(2,1)S(1)}, u32[]{:S(2)}, u32[]{:S(2)}) collective-permute-start(bf16[8,4096]{1,0:T(8,128)(2,1)S(1)} %get-tuple-element.38), channel_id=1, source_target_pairs={{0,3},{1,2},{2,1},{3,0},{4,7},{5,6},{6,5},{7,4},{8,11},{9,10},{10,... | collective-permute-start | bytes 196616 | tf_op jit(solution)/shard_map/ppermute | solution.py:217
  55.4 0.7 %collective-permute-start.21 = (bf16[8,4096]{1,0:T(8,128)(2,1)S(1)}, bf16[8,4096]{1,0:T(8,128)(2,1)S(1)}, u32[]{:S(2)}, u32[]{:S(2)}) collective-permute-start(bf16[8,4096]{1,0:T(8,128)(2,1)S(1)} %get-tuple-element.37), channel_id=1, source_target_pairs={{0,1},{1,0},{2,3},{3,2},{4,5},{5,4},{6,7},{7,6},{8,9},{9,8},{10,11... | collective-permute-start | bytes 196616 | tf_op jit(solution)/shard_map/ppermute | solution.py:217
  56.1 0.4 fusion.1
  56.5 0.8 %copy.21 = bf16[1,8,64,128]{3,1,2,0:T(8,128)(2,1)} copy(bf16[1,8,64,128]{3,2,1,0:T(8,128)(2,1)S(1)} %bitcast.15) | data formatting | bytes 262144
  57.2 2.5 %collective-permute-done.19 = bf16[8,4096]{1,0:T(8,128)(2,1)S(1)} collective-permute-done((bf16[8,4096]{1,0:T(8,128)(2,1)S(1)}, bf16[8,4096]{1,0:T(8,128)(2,1)S(1)}, u32[]{:S(2)}, u32[]{:S(2)}) %collective-permute-start.19) | collective-permute-done | bytes 65568 | tf_op jit(solution)/shard_map/ppermute | solution.py:217
  59.7 1.2 %collective-permute-done.20 = bf16[8,4096]{1,0:T(8,128)(2,1)S(1)} collective-permute-done((bf16[8,4096]{1,0:T(8,128)(2,1)S(1)}, bf16[8,4096]{1,0:T(8,128)(2,1)S(1)}, u32[]{:S(2)}, u32[]{:S(2)}) %collective-permute-start.20) | collective-permute-done | bytes 65568 | tf_op jit(solution)/shard_map/ppermute | solution.py:217
  60.9 0.5 collective-permute-done.21
  61.4 0.7 %add_convert_fusion.1 = bf16[8,4096]{1,0:T(8,128)(2,1)} fusion(bf16[8,4096]{1,0:T(8,128)(2,1)S(1)} %collective-permute-done.21, bf16[8,4096]{1,0:T(8,128)(2,1)S(1)} %collective-permute-done.20, f32[8,4096]{1,0:T(8,128)S(1)} %fusion.7, bf16[8,4096]{1,0:T(8,128)(2,1)S(1)} %collective-permute-done.19), kind=kLoop, calls=%fused_computation.17 | loop fusion | flops 229376 | bytes 393216 | tf_op jit(solution)/shard_map/convert_element_type | solution.py:259
  (26 shorter events, 0.3 us)
Async XLA Ops:
  0.6 55.5 %copy-start = (bf16[8,4,96,128]{3,2,1,0:T(8,128)(2,1)S(1)}, bf16[8,4,96,128]{3,2,1,0:T(8,128)(2,1)}, u32[]{:S(2)}) copy-start(bf16[8,4,96,128]{3,2,1,0:T(8,128)(2,1)} %param.15) | copy-start | bytes 2359300
  1.8 8.9 %collective-permute-start = (bf16[8,4224]{1,0:T(8,128)(2,1)S(1)}, bf16[8,4224]{1,0:T(8,128)(2,1)S(1)}, u32[]{:S(2)}, u32[]{:S(2)}) collective-permute-start(bf16[8,4224]{1,0:T(8,128)(2,1)S(1)} %prepare.1.refs_0_), channel_id=1, source_target_pairs={{0,24},{1,25},{2,26},{3,27},{4,28},{5,29},{6,30},{7,31},{8,16},{9,... | collective-permute-start | bytes 202760 | tf_op jit(solution)/shard_map/ppermute | solution.py:217
  5.8 5.2 %collective-permute-start.1 = (bf16[8,4224]{1,0:T(8,128)(2,1)S(1)}, bf16[8,4224]{1,0:T(8,128)(2,1)S(1)}, u32[]{:S(2)}, u32[]{:S(2)}) collective-permute-start(bf16[8,4224]{1,0:T(8,128)(2,1)S(1)} %prepare.1.refs_0_), channel_id=1, source_target_pairs={{0,8},{1,9},{2,10},{3,11},{4,12},{5,13},{6,14},{7,15},{8,0},{9,1},... | collective-permute-start | bytes 202760 | tf_op jit(solution)/shard_map/ppermute | solution.py:217
  6.3 4.7 %collective-permute-start.2 = (bf16[8,4224]{1,0:T(8,128)(2,1)S(1)}, bf16[8,4224]{1,0:T(8,128)(2,1)S(1)}, u32[]{:S(2)}, u32[]{:S(2)}) collective-permute-start(bf16[8,4224]{1,0:T(8,128)(2,1)S(1)} %prepare.1.refs_0_), channel_id=1, source_target_pairs={{0,16},{1,17},{2,18},{3,19},{4,20},{5,21},{6,22},{7,23},{8,24},{9,... | collective-permute-start | bytes 202760 | tf_op jit(solution)/shard_map/ppermute | solution.py:217
  6.4 5.4 %collective-permute-start.3 = (bf16[8,4224]{1,0:T(8,128)(2,1)S(1)}, bf16[8,4224]{1,0:T(8,128)(2,1)S(1)}, u32[]{:S(2)}, u32[]{:S(2)}) collective-permute-start(bf16[8,4224]{1,0:T(8,128)(2,1)S(1)} %prepare.1.refs_0_), channel_id=1, source_target_pairs={{0,2},{1,3},{2,0},{3,1},{4,6},{5,7},{6,4},{7,5},{8,10},{9,11},{10,... | collective-permute-start | bytes 202760 | tf_op jit(solution)/shard_map/ppermute | solution.py:217
  9.4 6.2 %collective-permute-start.4 = (bf16[8,4224]{1,0:T(8,128)(2,1)S(1)}, bf16[8,4224]{1,0:T(8,128)(2,1)S(1)}, u32[]{:S(2)}, u32[]{:S(2)}) collective-permute-start(bf16[8,4224]{1,0:T(8,128)(2,1)S(1)} %prepare.1.refs_0_), channel_id=1, source_target_pairs={{0,3},{1,2},{2,1},{3,0},{4,7},{5,6},{6,5},{7,4},{8,11},{9,10},{10,... | collective-permute-start | bytes 202760 | tf_op jit(solution)/shard_map/ppermute | solution.py:217
  10.7 5.0 %collective-permute-start.5 = (bf16[8,4224]{1,0:T(8,128)(2,1)S(1)}, bf16[8,4224]{1,0:T(8,128)(2,1)S(1)}, u32[]{:S(2)}, u32[]{:S(2)}) collective-permute-start(bf16[8,4224]{1,0:T(8,128)(2,1)S(1)} %prepare.1.refs_0_), channel_id=1, source_target_pairs={{0,1},{1,0},{2,3},{3,2},{4,5},{5,4},{6,7},{7,6},{8,9},{9,8},{10,11... | collective-permute-start | bytes 202760 | tf_op jit(solution)/shard_map/ppermute | solution.py:217
  15.8 6.1 %collective-permute-start.6 = (bf16[56,4224]{1,0:T(8,128)(2,1)S(1)}, bf16[56,4224]{1,0:T(8,128)(2,1)S(1)}, u32[]{:S(2)}, u32[]{:S(2)}) collective-permute-start(bf16[56,4224]{1,0:T(8,128)(2,1)S(1)} %get-tuple-element.15.refs_1_), channel_id=1, source_target_pairs={{0,4},{1,5},{2,6},{3,7},{4,0},{5,1},{6,2},{7,3},{8,12},{9,13},{10,... | collective-permute-start | bytes 1419272 | tf_op jit(solution)/shard_map/ppermute | solution.py:217
  16.6 12.6 %collective-permute-start.7 = (bf16[24,4224]{1,0:T(8,128)(2,1)S(1)}, bf16[24,4224]{1,0:T(8,128)(2,1)S(1)}, u32[]{:S(2)}, u32[]{:S(2)}) collective-permute-start(bf16[24,4224]{1,0:T(8,128)(2,1)S(1)} %get-tuple-element.17), channel_id=1, source_target_pairs={{0,24},{1,25},{2,26},{3,27},{4,28},{5,29},{6,30},{7,31},{8,16},{9,... | collective-permute-start | bytes 608264 | tf_op jit(solution)/shard_map/ppermute | solution.py:217
  19.1 10.3 %collective-permute-start.8 = (bf16[24,4224]{1,0:T(8,128)(2,1)S(1)}, bf16[24,4224]{1,0:T(8,128)(2,1)S(1)}, u32[]{:S(2)}, u32[]{:S(2)}) collective-permute-start(bf16[24,4224]{1,0:T(8,128)(2,1)S(1)} %get-tuple-element.17), channel_id=1, source_target_pairs={{0,8},{1,9},{2,10},{3,11},{4,12},{5,13},{6,14},{7,15},{8,0},{9,1},... | collective-permute-start | bytes 608264 | tf_op jit(solution)/shard_map/ppermute | solution.py:217
  19.6 9.8 %collective-permute-start.9 = (bf16[24,4224]{1,0:T(8,128)(2,1)S(1)}, bf16[24,4224]{1,0:T(8,128)(2,1)S(1)}, u32[]{:S(2)}, u32[]{:S(2)}) collective-permute-start(bf16[24,4224]{1,0:T(8,128)(2,1)S(1)} %get-tuple-element.17), channel_id=1, source_target_pairs={{0,16},{1,17},{2,18},{3,19},{4,20},{5,21},{6,22},{7,23},{8,24},{9,... | collective-permute-start | bytes 608264 | tf_op jit(solution)/shard_map/ppermute | solution.py:217
  21.9 7.6 %copy-start.1 = (bf16[8,64,128]{2,1,0:T(8,128)(2,1)S(1)}, bf16[8,64,128]{2,1,0:T(8,128)(2,1)}, u32[]{:S(2)}) copy-start(bf16[8,64,128]{2,1,0:T(8,128)(2,1)} %param.13) | copy-start | bytes 393220
  21.9 7.6 %copy-start.3 = (bf16[8,4,128]{2,1,0:T(4,128)(2,1)S(1)}, bf16[8,4,128]{2,1,0:T(4,128)(2,1)}, u32[]{:S(2)}) copy-start(bf16[8,4,128]{2,1,0:T(4,128)(2,1)} %param.16) | copy-start | bytes 24580
  22.0 7.8 %copy-start.2 = (bf16[8,4,128]{2,1,0:T(4,128)(2,1)S(1)}, bf16[8,4,128]{2,1,0:T(4,128)(2,1)}, u32[]{:S(2)}) copy-start(bf16[8,4,128]{2,1,0:T(4,128)(2,1)} %param.17) | copy-start | bytes 24580
  29.4 1.9 %collective-permute-start.12 = (bf16[56,4096]{1,0:T(8,128)(2,1)S(1)}, bf16[56,4096]{1,0:T(8,128)(2,1)S(1)}, u32[]{:S(2)}, u32[]{:S(2)}) collective-permute-start(bf16[56,4096]{1,0:T(8,128)(2,1)S(1)} %get-tuple-element.25), channel_id=1, source_target_pairs={{0,4},{1,5},{2,6},{3,7},{4,0},{5,1},{6,2},{7,3},{8,12},{9,13},{10,... | collective-permute-start | bytes 1376264 | tf_op jit(solution)/shard_map/ppermute | solution.py:217
  30.0 5.0 %collective-permute-start.10 = (bf16[72,4224]{1,0:T(8,128)(2,1)S(1)}, bf16[72,4224]{1,0:T(8,128)(2,1)S(1)}, u32[]{:S(2)}, u32[]{:S(2)}) collective-permute-start(bf16[72,4224]{1,0:T(8,128)(2,1)S(1)} %pack.3.refs_1_), channel_id=1, source_target_pairs={{0,4},{1,5},{2,6},{3,7},{4,0},{5,1},{6,2},{7,3},{8,12},{9,13},{10,... | collective-permute-start | bytes 1824776 | tf_op jit(solution)/shard_map/ppermute | solution.py:217
  31.5 6.7 %collective-permute-start.13 = (bf16[8,4096]{1,0:T(8,128)(2,1)S(1)}, bf16[8,4096]{1,0:T(8,128)(2,1)S(1)}, u32[]{:S(2)}, u32[]{:S(2)}) collective-permute-start(bf16[8,4096]{1,0:T(8,128)(2,1)S(1)} %get-tuple-element.33), channel_id=1, source_target_pairs={{0,24},{1,25},{2,26},{3,27},{4,28},{5,29},{6,30},{7,31},{8,16},{9,... | collective-permute-start | bytes 196616 | tf_op jit(solution)/shard_map/ppermute | solution.py:217
  33.9 4.3 %collective-permute-start.14 = (bf16[8,4096]{1,0:T(8,128)(2,1)S(1)}, bf16[8,4096]{1,0:T(8,128)(2,1)S(1)}, u32[]{:S(2)}, u32[]{:S(2)}) collective-permute-start(bf16[8,4096]{1,0:T(8,128)(2,1)S(1)} %get-tuple-element.35), channel_id=1, source_target_pairs={{0,8},{1,9},{2,10},{3,11},{4,12},{5,13},{6,14},{7,15},{8,0},{9,1},... | collective-permute-start | bytes 196616 | tf_op jit(solution)/shard_map/ppermute | solution.py:217
  34.4 4.3 %collective-permute-start.15 = (bf16[8,4096]{1,0:T(8,128)(2,1)S(1)}, bf16[8,4096]{1,0:T(8,128)(2,1)S(1)}, u32[]{:S(2)}, u32[]{:S(2)}) collective-permute-start(bf16[8,4096]{1,0:T(8,128)(2,1)S(1)} %get-tuple-element.34), channel_id=1, source_target_pairs={{0,16},{1,17},{2,18},{3,19},{4,20},{5,21},{6,22},{7,23},{8,24},{9,... | collective-permute-start | bytes 196616 | tf_op jit(solution)/shard_map/ppermute | solution.py:217
  38.0 2.1 %collective-permute-start.11 = (bf16[72,4096]{1,0:T(8,128)(2,1)S(1)}, bf16[72,4096]{1,0:T(8,128)(2,1)S(1)}, u32[]{:S(2)}, u32[]{:S(2)}) collective-permute-start(bf16[72,4096]{1,0:T(8,128)(2,1)S(1)} %get-tuple-element.24), channel_id=1, source_target_pairs={{0,4},{1,5},{2,6},{3,7},{4,0},{5,1},{6,2},{7,3},{8,12},{9,13},{10,... | collective-permute-start | bytes 1769480 | tf_op jit(solution)/shard_map/ppermute | solution.py:217
  40.3 8.8 %collective-permute-start.16 = (bf16[24,4096]{1,0:T(8,128)(2,1)S(1)}, bf16[24,4096]{1,0:T(8,128)(2,1)S(1)}, u32[]{:S(2)}, u32[]{:S(2)}) collective-permute-start(bf16[24,4096]{1,0:T(8,128)(2,1)S(1)} %get-tuple-element.30), channel_id=1, source_target_pairs={{0,24},{1,25},{2,26},{3,27},{4,28},{5,29},{6,30},{7,31},{8,16},{9,... | collective-permute-start | bytes 589832 | tf_op jit(solution)/shard_map/ppermute | solution.py:217
  42.7 9.7 %collective-permute-start.17 = (bf16[24,4096]{1,0:T(8,128)(2,1)S(1)}, bf16[24,4096]{1,0:T(8,128)(2,1)S(1)}, u32[]{:S(2)}, u32[]{:S(2)}) collective-permute-start(bf16[24,4096]{1,0:T(8,128)(2,1)S(1)} %get-tuple-element.32), channel_id=1, source_target_pairs={{0,8},{1,9},{2,10},{3,11},{4,12},{5,13},{6,14},{7,15},{8,0},{9,1},... | collective-permute-start | bytes 589832 | tf_op jit(solution)/shard_map/ppermute | solution.py:217
  43.2 9.2 %collective-permute-start.18 = (bf16[24,4096]{1,0:T(8,128)(2,1)S(1)}, bf16[24,4096]{1,0:T(8,128)(2,1)S(1)}, u32[]{:S(2)}, u32[]{:S(2)}) collective-permute-start(bf16[24,4096]{1,0:T(8,128)(2,1)S(1)} %get-tuple-element.31), channel_id=1, source_target_pairs={{0,16},{1,17},{2,18},{3,19},{4,20},{5,21},{6,22},{7,23},{8,24},{9,... | collective-permute-start | bytes 589832 | tf_op jit(solution)/shard_map/ppermute | solution.py:217
  52.6 7.2 %collective-permute-start.19 = (bf16[8,4096]{1,0:T(8,128)(2,1)S(1)}, bf16[8,4096]{1,0:T(8,128)(2,1)S(1)}, u32[]{:S(2)}, u32[]{:S(2)}) collective-permute-start(bf16[8,4096]{1,0:T(8,128)(2,1)S(1)} %get-tuple-element.36), channel_id=1, source_target_pairs={{0,2},{1,3},{2,0},{3,1},{4,6},{5,7},{6,4},{7,5},{8,10},{9,11},{10,... | collective-permute-start | bytes 196616 | tf_op jit(solution)/shard_map/ppermute | solution.py:217
  54.5 6.4 %collective-permute-start.20 = (bf16[8,4096]{1,0:T(8,128)(2,1)S(1)}, bf16[8,4096]{1,0:T(8,128)(2,1)S(1)}, u32[]{:S(2)}, u32[]{:S(2)}) collective-permute-start(bf16[8,4096]{1,0:T(8,128)(2,1)S(1)} %get-tuple-element.38), channel_id=1, source_target_pairs={{0,3},{1,2},{2,1},{3,0},{4,7},{5,6},{6,5},{7,4},{8,11},{9,10},{10,... | collective-permute-start | bytes 196616 | tf_op jit(solution)/shard_map/ppermute | solution.py:217
  55.4 6.0 %collective-permute-start.21 = (bf16[8,4096]{1,0:T(8,128)(2,1)S(1)}, bf16[8,4096]{1,0:T(8,128)(2,1)S(1)}, u32[]{:S(2)}, u32[]{:S(2)}) collective-permute-start(bf16[8,4096]{1,0:T(8,128)(2,1)S(1)} %get-tuple-element.37), channel_id=1, source_target_pairs={{0,1},{1,0},{2,3},{3,2},{4,5},{5,4},{6,7},{7,6},{8,9},{9,8},{10,11... | collective-permute-start | bytes 196616 | tf_op jit(solution)/shard_map/ppermute | solution.py:217

commit v3 on v2

v3 whole, which is shorter than its diff:
```python
import functools
import math

import jax
import jax.numpy as jnp
from jax import lax
from jax.experimental import pallas as pl
from jax.experimental.pallas import tpu as pltpu
from jax.sharding import PartitionSpec as P


MIB = 1024 * 1024
TILE = 256
DOWN_TILE = 1024
ATTEND_LIMIT = 12 * MIB


def whole(space):
    return pl.BlockSpec(memory_space=space)


def in_hbm(array):
    return pltpu.with_memory_space_constraint(array, pltpu.HBM)


def prepare_kernel(
    experts, hidden_hbm, gain_hbm, ids_hbm, scores_hbm, out_ref, hidden_ref, gain_ref, ids_ref, scores_ref, sems
):
    pairs = ((hidden_hbm, hidden_ref), (gain_hbm, gain_ref), (ids_hbm, ids_ref), (scores_hbm, scores_ref))
    copies = [pltpu.make_async_copy(a, b, sems.at[n]) for n, (a, b) in enumerate(pairs)]
    for copy in copies:
        copy.start()
    for copy in copies:
        copy.wait()
    width = hidden_ref.shape[1]
    hidden = hidden_ref[...].astype(jnp.float32)
    mean_square = jnp.mean(hidden * hidden, axis=1, keepdims=True)
    gain = gain_ref[...].astype(jnp.float32).reshape(1, width)
    out_ref[:, :width] = (hidden * lax.rsqrt(mean_square + 1e-06) * gain).astype(jnp.bfloat16)
    scores = scores_ref[...]
    gates = scores / jnp.sum(scores, axis=1, keepdims=True)
    ids = ids_ref[...]
    rows, extra = out_ref.shape[0], out_ref.shape[1] - width
    column = lax.broadcasted_iota(jnp.int32, (rows, extra), 1)
    expert = jnp.where(column < experts, column, column - experts)
    table = jnp.zeros((rows, extra), jnp.float32)
    for j in range(ids.shape[1]):
        table = table + jnp.where(ids[:, j : j + 1] == expert, gates[:, j : j + 1], 0.0)
    coarse = table.astype(jnp.bfloat16).astype(jnp.float32)
    parts = jnp.where(column < experts, coarse, jnp.where(column < 2 * experts, table - coarse, 0.0))
    out_ref[:, width:] = parts.astype(jnp.bfloat16)


def prepare(hidden_rows, norm_gain, expert_ids, route_scores, experts):
    rows, width = hidden_rows.shape
    extra = -(-2 * experts // 128) * 128
    args = (hidden_rows, norm_gain, expert_ids, route_scores)
    return pl.pallas_call(
        functools.partial(prepare_kernel, experts),
        out_shape=pltpu.VMEM((rows, width + extra), jnp.bfloat16),
        in_specs=[whole(pltpu.HBM)] * 4,
        out_specs=whole(pltpu.VMEM),
        scratch_shapes=[pltpu.VMEM(a.shape, a.dtype) for a in args] + [pltpu.SemaphoreType.DMA((4,))],
        compiler_params=pltpu.CompilerParams(vmem_limit_bytes=2 * MIB),
        name="prepare",
    )(*[in_hbm(a) for a in args])


def attend_kernel(
    kv_heads,
    inverse_scale,
    lengths_hbm,
    queries_hbm,
    keys_hbm,
    values_hbm,
    fresh_hbm,
    new_hbm,
    out_ref,
    lengths_ref,
    queries_v,
    keys_v,
    values_v,
    fresh_v,
    new_v,
    mixed_v,
    sems,
):
    requests, slots, width = keys_hbm.shape
    context = slots // kv_heads
    heads = queries_hbm.shape[1]
    group = heads // kv_heads
    pairs = [
        (queries_hbm, queries_v),
        (keys_hbm, keys_v.at[:, pl.ds(0, slots), :]),
        (values_hbm, values_v.at[:, pl.ds(0, slots), :]),
        (fresh_hbm, fresh_v),
        (new_hbm, new_v),
        (lengths_hbm, lengths_ref),
    ]
    copies = [pltpu.make_async_copy(a, b, sems.at[n]) for n, (a, b) in enumerate(pairs)]
    for copy in copies:
        copy.start()
    total = keys_v.shape[1]
    row_group = lax.broadcasted_iota(jnp.int32, (heads, total), 0) // group
    slot = lax.broadcasted_iota(jnp.int32, (heads, total), 1)
    offset = slot - row_group * context
    is_new = slot == slots + row_group
    empty = jnp.zeros((total - slots - kv_heads, width), jnp.float32)
    for copy in copies:
        copy.wait()
    for b in range(requests):
        for cache, token in ((keys_v, fresh_v), (values_v, new_v)):
            tail = jnp.concatenate([token[b].astype(jnp.float32), empty])
            cache[b, slots:, :] = tail.astype(jnp.bfloat16)
    scores = [
        lax.dot_general(
            queries_v[b], keys_v[b], (((1,), (1,)), ((), ())), preferred_element_type=jnp.float32
        )
        for b in range(requests)
    ]
    probs = []
    for b in range(requests):
        valid = (offset >= 0) & (offset < lengths_ref[b]) & (slot < slots) | is_new
        score = jnp.where(valid, scores[b] * inverse_scale, -1e30)
        exponent = jnp.exp(score - jnp.max(score, axis=1, keepdims=True))
        probs.append((exponent / jnp.sum(exponent, axis=1, keepdims=True)).astype(jnp.bfloat16))
    for b in range(requests):
        mixed_v[b * heads : (b + 1) * heads, :] = jnp.dot(
            probs[b], values_v[b], preferred_element_type=jnp.float32
        )
    for h in range(heads):
        rows = mixed_v[pl.ds(h, requests, stride=heads), :]
        out_ref[:, h * width : (h + 1) * width] = rows.astype(jnp.bfloat16)


def attend(queries, key_cache, value_cache, fresh_token_keys, new_values, lengths):
    requests, heads, width = queries.shape
    kv_heads, context = key_cache.shape[1:3]
    slots = kv_heads * context
    total = -(-(slots + kv_heads) // 128) * 128
    cache = pltpu.VMEM((requests, total, width), jnp.bfloat16)
    token = pltpu.VMEM(fresh_token_keys.shape, jnp.bfloat16)
    vmem = whole(pltpu.VMEM)
    return pl.pallas_call(
        functools.partial(attend_kernel, kv_heads, 1.0 / math.sqrt(width)),
        out_shape=jax.ShapeDtypeStruct((requests, heads * width), jnp.bfloat16),
        in_specs=[whole(pltpu.HBM)] * 6,
        out_specs=vmem,
        scratch_shapes=[
            pltpu.SMEM(lengths.shape, jnp.int32),
            pltpu.VMEM(queries.shape, jnp.bfloat16),
            cache,
            cache,
            token,
            token,
            pltpu.VMEM((requests * heads, width), jnp.float32),
            pltpu.SemaphoreType.DMA((6,)),
        ],
        compiler_params=pltpu.CompilerParams(vmem_limit_bytes=ATTEND_LIMIT),
        cost_estimate=pl.CostEstimate(
            flops=12 * 10**9,
            bytes_accessed=4 * key_cache.size,
            transcendentals=requests * heads * total,
        ),
        name="attend",
    )(
        in_hbm(lengths),
        in_hbm(queries),
        in_hbm(key_cache.reshape(requests, slots, width)),
        in_hbm(value_cache.reshape(requests, slots, width)),
        in_hbm(fresh_token_keys),
        in_hbm(new_values),
    )


def pack_kernel(tail, after, *refs):
    refs = refs[after:]
    out_ref, tail_ref = refs[-2:] if tail else (refs[-1], None)
    refs = refs[: -2 if tail else -1]
    start, inner = 0, 0
    for n, ref in enumerate(refs):
        out_ref[start : start + ref.shape[0], :] = ref[...]
        start += ref.shape[0]
        if n >= len(refs) - tail:
            tail_ref[inner : inner + ref.shape[0], :] = ref[...]
            inner += ref.shape[0]


def pack(pieces, tail=0, after=()):
    width, dtype = pieces[0].shape[1], pieces[0].dtype

    def out(pieces):
        return pltpu.VMEM((sum(piece.shape[0] for piece in pieces), width), dtype)

    vmem = whole(pltpu.VMEM)
    return pl.pallas_call(
        functools.partial(pack_kernel, tail, len(after)),
        out_shape=(out(pieces), out(pieces[-tail:])) if tail else out(pieces),
        in_specs=[whole(pl.ANY)] * len(after) + [vmem] * len(pieces),
        out_specs=(vmem, vmem) if tail else vmem,
        compiler_params=pltpu.CompilerParams(vmem_limit_bytes=MIB),
        name="pack",
    )(*after, *pieces)


def experts_kernel(
    experts, after, here_ref, there_ref, gate_ref, up_ref, down_ref, *refs
):
    out_here, out_there, rows_v, act_v = refs[after:]
    hidden, width = down_ref.shape
    cuts = [pl.ds(t, TILE) for t in range(0, hidden, TILE)]
    down_cuts = [pl.ds(t, DOWN_TILE) for t in range(0, width, DOWN_TILE)]
    half = here_ref.shape[0]
    rows_v[:half, :] = here_ref[:, :width]
    rows_v[half:, :] = there_ref[:, :width]
    column = lax.broadcasted_iota(jnp.int32, (1, here_ref.shape[1] - width), 1)
    own = (lax.axis_index("node") * lax.axis_size("local") + lax.axis_index("local")) // 2
    mine = (column == own) | (column == own + experts)

    def weights_of(ref):
        parts = jnp.where(mine, ref[:, width:].astype(jnp.float32), 0.0)
        return jnp.sum(parts, axis=1, keepdims=True)

    weight_here, weight_there = weights_of(here_ref), weights_of(there_ref)
    for cut in cuts:
        gate = jnp.dot(rows_v[...], gate_ref[:, cut], preferred_element_type=jnp.float32)
        up = jnp.dot(rows_v[...], up_ref[:, cut], preferred_element_type=jnp.float32)
        act_v[:, cut] = (gate / (1.0 + jnp.exp(-gate)) * up).astype(jnp.bfloat16)
    for cut in down_cuts:
        produced = jnp.dot(act_v[...], down_ref[:, cut], preferred_element_type=jnp.float32)
        out_here[:, cut] = (weight_here * produced[:half]).astype(jnp.bfloat16)
        out_there[:, cut] = (weight_there * produced[half:]).astype(jnp.bfloat16)


def expert_piece(here, there, experts, pieces, after=()):
    half = here.shape[0]
    hidden, width = pieces[2].shape
    out = pltpu.VMEM((half, width), jnp.bfloat16)
    vmem = whole(pltpu.VMEM)
    return pl.pallas_call(
        functools.partial(experts_kernel, experts, len(after)),
        out_shape=(out, out),
        in_specs=[vmem] * 5 + [whole(pl.ANY)] * len(after),
        out_specs=(vmem, vmem),
        scratch_shapes=[
            pltpu.VMEM((2 * half, width), jnp.bfloat16),
            pltpu.VMEM((2 * half, hidden), jnp.bfloat16),
        ],
        compiler_params=pltpu.CompilerParams(vmem_limit_bytes=64 * half * 1024 + 4 * MIB),
        cost_estimate=pl.CostEstimate(
            flops=12 * half * width * hidden, bytes_accessed=0, transcendentals=2 * half * hidden
        ),
        name="expert_piece",
    )(here, there, *pieces, *after)


def exchange(rows, node_mask, local_mask):
    nodes = lax.axis_size("node")
    locals_ = lax.axis_size("local")
    pairs = [
        (n * locals_ + k, (n ^ node_mask) * locals_ + (k ^ local_mask))
        for n in range(nodes)
        for k in range(locals_)
    ]
    return lax.ppermute(rows, ("node", "local"), pairs)


def masks():
    locals_, nodes = lax.axis_size("local"), lax.axis_size("node")
    near, far = list(range(locals_ // 2)), list(range(locals_ // 2, locals_))
    return near, far, [nodes - 2] + list(range(2, nodes - 2, 2))


def gather_plane(line, after=()):
    return pack([line] + [exchange(line, n, 0) for n in masks()[2]], after=after)


def f32(x):
    return x.astype(jnp.float32)


def block(x, size, i):
    return x[i * size : (i + 1) * size]


def core_sum(here, there):
    return f32(here) + f32(exchange(there, 1, 0))


def plane_sum(sums):
    plane = masks()[2]
    size = sums.shape[0] // (1 + len(plane))
    line, packed = sums[:size], sums.astype(jnp.bfloat16)
    for i, n in enumerate(plane):
        line = line + f32(exchange(block(packed, size, i + 1), n, 0))
    return line


def per_device(
    queries,
    key_cache,
    value_cache,
    fresh_token_keys,
    new_values,
    lengths,
    hidden_rows,
    norm_gain,
    expert_ids,
    route_scores,
    gate_weight,
    up_weight,
    down_weight,
):
    context = attend(queries, key_cache, value_cache, fresh_token_keys, new_values, lengths)
    experts = lax.axis_size("node") * lax.axis_size("local") // 2
    count = hidden_rows.shape[0]
    near, far, _ = masks()
    rows = prepare(hidden_rows, norm_gain, expert_ids, route_scores, experts)
    line = {k: exchange(rows, 0, k) for k in near[1:] + far}
    second = pack([line[k] for k in far], after=(in_hbm(context),))
    first = gather_plane(pack([rows] + [line[k] for k in near[1:]]), after=(second,))
    pieces = (gate_weight[0], up_weight[0], down_weight[0])
    first, first_other = expert_piece(first, exchange(first, 1, 0), experts, pieces)
    second = gather_plane(second, after=(first,))
    second, first_other = lax.optimization_barrier((second, first_other))
    second, second_other = expert_piece(
        second, exchange(second, 1, 0), experts, pieces
    )
    line = plane_sum(core_sum(first, first_other))
    total, packed = line[:count], line.astype(jnp.bfloat16)
    line = plane_sum(core_sum(second, second_other)).astype(jnp.bfloat16)
    for i, k in enumerate(far):
        total = total + f32(exchange(block(line, count, i), 0, k))
    for i, k in enumerate(near[1:]):
        total = total + f32(exchange(block(packed, count, i + 1), 0, k))
    total = total.astype(jnp.bfloat16)
    return (context, total)


def solution(mesh):
    placed = (
        P(("group", "node", "local"), None, None),
        P(("group", "node", "local"), None, None, None),
        P(("group", "node", "local"), None, None, None),
        P(("group", "node", "local"), None, None),
        P(("group", "node", "local"), None, None),
        P(("group", "node", "local")),
        P(("group", "node", "local"), None),
        P(),
        P(("group", "node", "local"), None),
        P(("group", "node", "local"), None),
        P(("node", "local"), None, None),
        P(("node", "local"), None, None),
        P(("node", "local"), None, None),
    )
    return jax.shard_map(
        per_device,
        mesh=mesh,
        in_specs=placed,
        out_specs=(P(("group", "node", "local"), None), P(("group", "node", "local"), None)),
        check_vma=False,
    )
```

time: 62.2 us -> 58 us (0.932)
  starting transfers between devices: 24.1 us -> 26.6 us
  matrix products: 2.37 us -> 0 us
  Pallas kernels: 11.5 us -> 9.89 us
  other arithmetic: 2.1 us -> 1.05 us
  waiting for transfers between devices: 20.3 us -> 19.4 us
  local copies, waits for them, and re-layouts: 0.85 us -> 0.09 us
    ppermute x22, starting transfers between devices: 24.1 us -> 26.6 us  [exchange(): return lax.ppermute(rows, ('node', 'local'), pairs)]
    dot_general x3 -> x0, matrix products: 2.37 us -> none  [the longest x1 1.81 us: attend(): jnp.einsum('bkgd,bkpd->bkgp', grouped_queries, key_cache, preferred_eleme...]
    pallas_call x2 -> x3, Pallas kernels: 10.3 us -> 8.72 us  [the longest x2 5.39 us: expert_piece(): pl.pallas_call(functools.partial(experts_kernel, experts, len(after)), ou...]
    ppermute x22, waiting for transfers between devices: 20.3 us -> 19.4 us  [exchange(): return lax.ppermute(rows, ('node', 'local'), pairs)]
    unnamed x9 -> x6, local copies, waits for them, and re-layouts: 0.78 us -> 0.01 us
    lt x1 -> x0, other arithmetic: 0.73 us -> none  [attend(): in_range = positions[None, :] < lengths[:, None]]
  transfers between devices with their start and end apart: 22 -> 22, of which waited for: 12 -> 12; matrix products, arithmetic and copies ran while one was open for 7% -> 1% of each run, Pallas kernels for 17% -> 10%
where the time goes in v3:
time: 58 us; the launch traced here: 57.8 us
  starting transfers between devices  26.6 us (46%)
  waiting for transfers between devices  19.4 us (33%)
  Pallas kernels  9.89 us (17%)
  other arithmetic  1.05 us (2%)
  between operations  0.81 us (1%)
    ppermute x22, starting transfers between devices, exchange(): return lax.ppermute(rows, ('node', 'local'), pairs)  26.6 us
    ppermute x22, waiting for transfers between devices, exchange(): return lax.ppermute(rows, ('node', 'local'), pairs)  19.4 us
    pallas_call x2, Pallas kernels, expert_piece(): pl.pallas_call(functools.partial(experts_kernel, experts, len(after)), ou...  5.39 us
    pallas_call x1, Pallas kernels, attend(): pl.pallas_call(functools.partial(attend_kernel, kv_heads, 1.0 / math.sqrt...  3.33 us
  transfers between devices with their start and end apart: 22, of which 12 were waited for; matrix products, arithmetic and copies ran while one was open for 1% of the time, Pallas kernels for 10%

profile of v3, /device:TPU:0, one launch (start us, length us, event | category | flops | bytes accessed | tf_op | source)
XLA Modules:
  0.0 57.8 jit_solution(578930692786360535)
XLA Ops:
  0.6 1.1 %prepare.1.refs_0_ = bf16[8,4224]{1,0:T(8,128)(2,1)S(1)} custom-call(bf16[8,4096]{1,0:T(8,128)(2,1)} %hidden_hbm.1, bf16[4096]{0:T(1024)(128)(2,1)} %gain_hbm.1, s32[8,8]{1,0:T(8,128)} %ids_hbm.1, f32[8,8]{1,0:T(8,128)} %scores_hbm.1), custom_call_target="tpu_custom_call" | custom-call | tf_op jit(solution)/shard_map/prepare/pallas_call | solution.py:58
  1.7 3.1 %collective-permute-start.2 = (bf16[8,4224]{1,0:T(8,128)(2,1)S(1)}, bf16[8,4224]{1,0:T(8,128)(2,1)S(1)}, u32[]{:S(2)}, u32[]{:S(2)}) collective-permute-start(bf16[8,4224]{1,0:T(8,128)(2,1)S(1)} %prepare.1.refs_0_), channel_id=1, source_target_pairs={{0,1},{1,0},{2,3},{3,2},{4,5},{5,4},{6,7},{7,6},{8,9},{9,8},{10,11... | collective-permute-start | bytes 202760 | tf_op jit(solution)/shard_map/ppermute | solution.py:265
  4.8 2.5 %collective-permute-start.1 = (bf16[8,4224]{1,0:T(8,128)(2,1)S(1)}, bf16[8,4224]{1,0:T(8,128)(2,1)S(1)}, u32[]{:S(2)}, u32[]{:S(2)}) collective-permute-start(bf16[8,4224]{1,0:T(8,128)(2,1)S(1)} %prepare.1.refs_0_), channel_id=1, source_target_pairs={{0,3},{1,2},{2,1},{3,0},{4,7},{5,6},{6,5},{7,4},{8,11},{9,10},{10,... | collective-permute-start | bytes 202760 | tf_op jit(solution)/shard_map/ppermute | solution.py:265
  7.3 0.1 collective-permute-start
  7.4 0.0 collective-permute-done.2.refs_1_
  7.4 1.7 %collective-permute-start.5 = (bf16[16,4224]{1,0:T(8,128)(2,1)S(1)}, bf16[16,4224]{1,0:T(8,128)(2,1)S(1)}, u32[]{:S(2)}, u32[]{:S(2)}) collective-permute-start(bf16[16,4224]{1,0:T(8,128)(2,1)S(1)} %pack.5.refs_1_), channel_id=1, source_target_pairs={{0,16},{1,17},{2,18},{3,19},{4,20},{5,21},{6,22},{7,23},{8,24},{9,... | collective-permute-start | bytes 405512 | tf_op jit(solution)/shard_map/ppermute | solution.py:265
  9.1 1.5 %collective-permute-start.4 = (bf16[16,4224]{1,0:T(8,128)(2,1)S(1)}, bf16[16,4224]{1,0:T(8,128)(2,1)S(1)}, u32[]{:S(2)}, u32[]{:S(2)}) collective-permute-start(bf16[16,4224]{1,0:T(8,128)(2,1)S(1)} %pack.5.refs_1_), channel_id=1, source_target_pairs={{0,8},{1,9},{2,10},{3,11},{4,12},{5,13},{6,14},{7,15},{8,0},{9,1},... | collective-permute-start | bytes 405512 | tf_op jit(solution)/shard_map/ppermute | solution.py:265
  10.6 0.4 collective-permute-start.3
  11.0 3.3 %attend.1.refs_0_ = bf16[8,8192]{1,0:T(8,128)(2,1)} custom-call(s32[8]{0:T(128)} %lengths_hbm.1, bf16[8,64,128]{2,1,0:T(8,128)(2,1)} %queries_hbm.1, bf16[8,384,128]{2,1,0:T(8,128)(2,1)} %bitcast.11, bf16[8,384,128]{2,1,0:T(8,128)(2,1)} %bitcast.12, bf16[8,4,128]{2,1,0:T(4,128)(2,1)} %fresh_hbm.1, bf16[8,4,128]{2,1,0:T(4,128)(2,1)} %new_hbm.1), custom_call_target="tpu_custom_call" | custom-call | flops 12000000000 | bytes 1572864 | tf_op jit(solution)/shard_map/attend/pallas_call | solution.py:144
  14.3 0.0 collective-permute-done.1.refs_2_
  14.3 0.0 collective-permute-done.refs_1_
  14.3 0.0 collective-permute-done.5.refs_4_
  14.4 0.6 collective-permute-done.4.refs_3_
  14.9 1.9 %collective-permute-done.3.refs_2_ = bf16[16,4224]{1,0:T(8,128)(2,1)S(1)} collective-permute-done((bf16[16,4224]{1,0:T(8,128)(2,1)S(1)}, bf16[16,4224]{1,0:T(8,128)(2,1)S(1)}, u32[]{:S(2)}, u32[]{:S(2)}) %collective-permute-start.3) | collective-permute-done | bytes 135200 | tf_op jit(solution)/shard_map/ppermute | solution.py:265
  16.9 0.1 collective-permute-start.6
  17.0 1.1 %collective-permute-start.9 = (bf16[16,4224]{1,0:T(8,128)(2,1)S(1)}, bf16[16,4224]{1,0:T(8,128)(2,1)S(1)}, u32[]{:S(2)}, u32[]{:S(2)}) collective-permute-start(bf16[16,4224]{1,0:T(8,128)(2,1)S(1)} %pack.4.refs_0_.refs_1_), channel_id=1, source_target_pairs={{0,16},{1,17},{2,18},{3,19},{4,20},{5,21},{6,22},{7,23},{8,24},{9,... | collective-permute-start | bytes 405512 | tf_op jit(solution)/shard_map/ppermute | solution.py:265
  18.0 1.5 %collective-permute-start.8 = (bf16[16,4224]{1,0:T(8,128)(2,1)S(1)}, bf16[16,4224]{1,0:T(8,128)(2,1)S(1)}, u32[]{:S(2)}, u32[]{:S(2)}) collective-permute-start(bf16[16,4224]{1,0:T(8,128)(2,1)S(1)} %pack.4.refs_0_.refs_1_), channel_id=1, source_target_pairs={{0,8},{1,9},{2,10},{3,11},{4,12},{5,13},{6,14},{7,15},{8,0},{9,1},... | collective-permute-start | bytes 405512 | tf_op jit(solution)/shard_map/ppermute | solution.py:265
  19.5 1.0 %collective-permute-start.7 = (bf16[16,4224]{1,0:T(8,128)(2,1)S(1)}, bf16[16,4224]{1,0:T(8,128)(2,1)S(1)}, u32[]{:S(2)}, u32[]{:S(2)}) collective-permute-start(bf16[16,4224]{1,0:T(8,128)(2,1)S(1)} %pack.4.refs_0_.refs_1_), channel_id=1, source_target_pairs={{0,24},{1,25},{2,26},{3,27},{4,28},{5,29},{6,30},{7,31},{8,16},{9,... | collective-permute-start | bytes 405512 | tf_op jit(solution)/shard_map/ppermute | solution.py:265
  20.5 0.0 collective-permute-done.6.there_ref
  20.5 2.7 %expert_piece.2 = (bf16[64,4096]{1,0:T(8,128)(2,1)S(1)}, bf16[64,4096]{1,0:T(8,128)(2,1)S(1)}) custom-call(bf16[64,4224]{1,0:T(8,128)(2,1)S(1)} %pack.6.here_ref, bf16[64,4224]{1,0:T(8,128)(2,1)S(1)} %collective-permute-done.6.there_ref, bf16[4096,768]{1,0:T(8,128)(2,1)S(1)} %bitcast.5, bf16[4096,768]{1,0:T(8,128)(2,1)S(1)} %bitcast.7, ...), custom_call_target="tpu_custom_call" | custom-call | flops 2415919104 | tf_op jit(solution)/shard_map/expert_piece/pallas_call | solution.py:240
  23.3 1.2 %collective-permute-done.8.refs_3_ = bf16[16,4224]{1,0:T(8,128)(2,1)S(1)} collective-permute-done((bf16[16,4224]{1,0:T(8,128)(2,1)S(1)}, bf16[16,4224]{1,0:T(8,128)(2,1)S(1)}, u32[]{:S(2)}, u32[]{:S(2)}) %collective-permute-start.8) | collective-permute-done | bytes 135200 | tf_op jit(solution)/shard_map/ppermute | solution.py:265
  24.5 2.6 %collective-permute-done.7.refs_2_ = bf16[16,4224]{1,0:T(8,128)(2,1)S(1)} collective-permute-done((bf16[16,4224]{1,0:T(8,128)(2,1)S(1)}, bf16[16,4224]{1,0:T(8,128)(2,1)S(1)}, u32[]{:S(2)}, u32[]{:S(2)}) %collective-permute-start.7) | collective-permute-done | bytes 135200 | tf_op jit(solution)/shard_map/ppermute | solution.py:265
  27.1 0.1 collective-permute-start.10
  27.2 0.5 collective-permute-start.14
  27.7 1.4 %collective-permute-done.10 = bf16[64,4096]{1,0:T(8,128)(2,1)S(1)} collective-permute-done((bf16[64,4096]{1,0:T(8,128)(2,1)S(1)}, bf16[64,4096]{1,0:T(8,128)(2,1)S(1)}, u32[]{:S(2)}, u32[]{:S(2)}) %collective-permute-start.10) | collective-permute-done | bytes 524320 | tf_op jit(solution)/shard_map/ppermute | solution.py:265
  29.1 0.1 fusion.8
  29.2 0.6 %collective-permute-done.14.there_ref = bf16[64,4224]{1,0:T(8,128)(2,1)S(1)} collective-permute-done((bf16[64,4224]{1,0:T(8,128)(2,1)S(1)}, bf16[64,4224]{1,0:T(8,128)(2,1)S(1)}, u32[]{:S(2)}, u32[]{:S(2)}) %collective-permute-start.14) | collective-permute-done | bytes 540704 | tf_op jit(solution)/shard_map/ppermute | solution.py:265
  29.8 2.7 %expert_piece.3 = (bf16[64,4096]{1,0:T(8,128)(2,1)S(1)}, bf16[64,4096]{1,0:T(8,128)(2,1)S(1)}) custom-call(bf16[64,4224]{1,0:T(8,128)(2,1)S(1)} %pack.7.here_ref, bf16[64,4224]{1,0:T(8,128)(2,1)S(1)} %collective-permute-done.14.there_ref, bf16[4096,768]{1,0:T(8,128)(2,1)S(1)} %bitcast.6, bf16[4096,768]{1,0:T(8,128)(2,1)S(1)} %bitcast.8, ...), custom_call_target="tpu_custom_call" | custom-call | flops 2415919104 | tf_op jit(solution)/shard_map/expert_piece/pallas_call | solution.py:240
  32.5 0.2 collective-permute-start.15
  32.8 2.0 %collective-permute-start.11 = (bf16[16,4096]{1,0:T(8,128)(2,1)S(1)}, bf16[16,4096]{1,0:T(8,128)(2,1)S(1)}, u32[]{:S(2)}, u32[]{:S(2)}) collective-permute-start(bf16[16,4096]{1,0:T(8,128)(2,1)S(1)} %get-tuple-element.21), channel_id=1, source_target_pairs={{0,24},{1,25},{2,26},{3,27},{4,28},{5,29},{6,30},{7,31},{8,16},{9,... | collective-permute-start | bytes 393224 | tf_op jit(solution)/shard_map/ppermute | solution.py:265
  34.8 0.5 collective-permute-start.13
  35.3 1.1 %collective-permute-start.12 = (bf16[16,4096]{1,0:T(8,128)(2,1)S(1)}, bf16[16,4096]{1,0:T(8,128)(2,1)S(1)}, u32[]{:S(2)}, u32[]{:S(2)}) collective-permute-start(bf16[16,4096]{1,0:T(8,128)(2,1)S(1)} %get-tuple-element.23), channel_id=1, source_target_pairs={{0,8},{1,9},{2,10},{3,11},{4,12},{5,13},{6,14},{7,15},{8,0},{9,1},... | collective-permute-start | bytes 393224 | tf_op jit(solution)/shard_map/ppermute | solution.py:265
  36.3 0.1 fusion.9
  36.5 2.0 %collective-permute-start.16 = (bf16[16,4096]{1,0:T(8,128)(2,1)S(1)}, bf16[16,4096]{1,0:T(8,128)(2,1)S(1)}, u32[]{:S(2)}, u32[]{:S(2)}) collective-permute-start(bf16[16,4096]{1,0:T(8,128)(2,1)S(1)} %get-tuple-element.18), channel_id=1, source_target_pairs={{0,24},{1,25},{2,26},{3,27},{4,28},{5,29},{6,30},{7,31},{8,16},{9,... | collective-permute-start | bytes 393224 | tf_op jit(solution)/shard_map/ppermute | solution.py:265
  38.5 0.5 collective-permute-start.18
  39.0 1.1 %collective-permute-done.11 = bf16[16,4096]{1,0:T(8,128)(2,1)S(1)} collective-permute-done((bf16[16,4096]{1,0:T(8,128)(2,1)S(1)}, bf16[16,4096]{1,0:T(8,128)(2,1)S(1)}, u32[]{:S(2)}, u32[]{:S(2)}) %collective-permute-start.11) | collective-permute-done | bytes 131104 | tf_op jit(solution)/shard_map/ppermute | solution.py:265
  40.1 1.0 %collective-permute-start.17 = (bf16[16,4096]{1,0:T(8,128)(2,1)S(1)}, bf16[16,4096]{1,0:T(8,128)(2,1)S(1)}, u32[]{:S(2)}, u32[]{:S(2)}) collective-permute-start(bf16[16,4096]{1,0:T(8,128)(2,1)S(1)} %get-tuple-element.20), channel_id=1, source_target_pairs={{0,8},{1,9},{2,10},{3,11},{4,12},{5,13},{6,14},{7,15},{8,0},{9,1},... | collective-permute-start | bytes 393224 | tf_op jit(solution)/shard_map/ppermute | solution.py:265
  41.1 1.9 %collective-permute-done.13 = bf16[16,4096]{1,0:T(8,128)(2,1)S(1)} collective-permute-done((bf16[16,4096]{1,0:T(8,128)(2,1)S(1)}, bf16[16,4096]{1,0:T(8,128)(2,1)S(1)}, u32[]{:S(2)}, u32[]{:S(2)}) %collective-permute-start.13) | collective-permute-done | bytes 131104 | tf_op jit(solution)/shard_map/ppermute | solution.py:265
  43.0 0.1 fusion.4
  43.0 1.8 %collective-permute-start.21 = (bf16[8,4096]{1,0:T(8,128)(2,1)S(1)}, bf16[8,4096]{1,0:T(8,128)(2,1)S(1)}, u32[]{:S(2)}, u32[]{:S(2)}) collective-permute-start(bf16[8,4096]{1,0:T(8,128)(2,1)S(1)} %slice.80), channel_id=1, source_target_pairs={{0,1},{1,0},{2,3},{3,2},{4,5},{5,4},{6,7},{7,6},{8,9},{9,8},{10,11... | collective-permute-start | bytes 196616 | tf_op jit(solution)/shard_map/ppermute | solution.py:265
  44.8 0.9 %collective-permute-done.16 = bf16[16,4096]{1,0:T(8,128)(2,1)S(1)} collective-permute-done((bf16[16,4096]{1,0:T(8,128)(2,1)S(1)}, bf16[16,4096]{1,0:T(8,128)(2,1)S(1)}, u32[]{:S(2)}, u32[]{:S(2)}) %collective-permute-start.16) | collective-permute-done | bytes 131104 | tf_op jit(solution)/shard_map/ppermute | solution.py:265
  45.7 2.2 %collective-permute-done.18 = bf16[16,4096]{1,0:T(8,128)(2,1)S(1)} collective-permute-done((bf16[16,4096]{1,0:T(8,128)(2,1)S(1)}, bf16[16,4096]{1,0:T(8,128)(2,1)S(1)}, u32[]{:S(2)}, u32[]{:S(2)}) %collective-permute-start.18) | collective-permute-done | bytes 131104 | tf_op jit(solution)/shard_map/ppermute | solution.py:265
  47.9 0.1 fusion.2
  48.0 3.0 %collective-permute-start.19 = (bf16[8,4096]{1,0:T(8,128)(2,1)S(1)}, bf16[8,4096]{1,0:T(8,128)(2,1)S(1)}, u32[]{:S(2)}, u32[]{:S(2)}) collective-permute-start(bf16[8,4096]{1,0:T(8,128)(2,1)S(1)} %get-tuple-element.24), channel_id=1, source_target_pairs={{0,2},{1,3},{2,0},{3,1},{4,6},{5,7},{6,4},{7,5},{8,10},{9,11},{10,... | collective-permute-start | bytes 196616 | tf_op jit(solution)/shard_map/ppermute | solution.py:265
  51.0 1.2 %collective-permute-start.20 = (bf16[8,4096]{1,0:T(8,128)(2,1)S(1)}, bf16[8,4096]{1,0:T(8,128)(2,1)S(1)}, u32[]{:S(2)}, u32[]{:S(2)}) collective-permute-start(bf16[8,4096]{1,0:T(8,128)(2,1)S(1)} %get-tuple-element.25), channel_id=1, source_target_pairs={{0,3},{1,2},{2,1},{3,0},{4,7},{5,6},{6,5},{7,4},{8,11},{9,10},{10,... | collective-permute-start | bytes 196616 | tf_op jit(solution)/shard_map/ppermute | solution.py:265
  52.2 2.8 %collective-permute-done.19 = bf16[8,4096]{1,0:T(8,128)(2,1)S(1)} collective-permute-done((bf16[8,4096]{1,0:T(8,128)(2,1)S(1)}, bf16[8,4096]{1,0:T(8,128)(2,1)S(1)}, u32[]{:S(2)}, u32[]{:S(2)}) %collective-permute-start.19) | collective-permute-done | bytes 65568 | tf_op jit(solution)/shard_map/ppermute | solution.py:265
  55.0 2.2 %collective-permute-done.20 = bf16[8,4096]{1,0:T(8,128)(2,1)S(1)} collective-permute-done((bf16[8,4096]{1,0:T(8,128)(2,1)S(1)}, bf16[8,4096]{1,0:T(8,128)(2,1)S(1)}, u32[]{:S(2)}, u32[]{:S(2)}) %collective-permute-start.20) | collective-permute-done | bytes 65568 | tf_op jit(solution)/shard_map/ppermute | solution.py:265
  57.1 0.7 %fusion.7 = bf16[8,4096]{1,0:T(8,128)(2,1)} fusion(f32[16,4096]{1,0:T(8,128)S(1)} %fusion.4, bf16[8,4096]{1,0:T(8,128)(2,1)S(1)} %collective-permute-done.21, bf16[8,4096]{1,0:T(8,128)(2,1)S(1)} %collective-permute-done.20, bf16[8,4096]{1,0:T(8,128)(2,1)S(1)} %collective-permute-done.19), kind=kLoop, calls=%fused_computation.13 | loop fusion | flops 229376 | bytes 393216 | tf_op jit(solution)/shard_map/convert_element_type | solution.py:336
  (19 shorter events, 0.2 us)
Async XLA Ops:
  1.7 5.7 %collective-permute-start.2 = (bf16[8,4224]{1,0:T(8,128)(2,1)S(1)}, bf16[8,4224]{1,0:T(8,128)(2,1)S(1)}, u32[]{:S(2)}, u32[]{:S(2)}) collective-permute-start(bf16[8,4224]{1,0:T(8,128)(2,1)S(1)} %prepare.1.refs_0_), channel_id=1, source_target_pairs={{0,1},{1,0},{2,3},{3,2},{4,5},{5,4},{6,7},{7,6},{8,9},{9,8},{10,11... | collective-permute-start | bytes 202760 | tf_op jit(solution)/shard_map/ppermute | solution.py:265
  4.8 9.5 %collective-permute-start.1 = (bf16[8,4224]{1,0:T(8,128)(2,1)S(1)}, bf16[8,4224]{1,0:T(8,128)(2,1)S(1)}, u32[]{:S(2)}, u32[]{:S(2)}) collective-permute-start(bf16[8,4224]{1,0:T(8,128)(2,1)S(1)} %prepare.1.refs_0_), channel_id=1, source_target_pairs={{0,3},{1,2},{2,1},{3,0},{4,7},{5,6},{6,5},{7,4},{8,11},{9,10},{10,... | collective-permute-start | bytes 202760 | tf_op jit(solution)/shard_map/ppermute | solution.py:265
  7.3 7.0 %collective-permute-start = (bf16[8,4224]{1,0:T(8,128)(2,1)S(1)}, bf16[8,4224]{1,0:T(8,128)(2,1)S(1)}, u32[]{:S(2)}, u32[]{:S(2)}) collective-permute-start(bf16[8,4224]{1,0:T(8,128)(2,1)S(1)} %prepare.1.refs_0_), channel_id=1, source_target_pairs={{0,2},{1,3},{2,0},{3,1},{4,6},{5,7},{6,4},{7,5},{8,10},{9,11},{10,... | collective-permute-start | bytes 202760 | tf_op jit(solution)/shard_map/ppermute | solution.py:265
  7.4 6.9 %collective-permute-start.5 = (bf16[16,4224]{1,0:T(8,128)(2,1)S(1)}, bf16[16,4224]{1,0:T(8,128)(2,1)S(1)}, u32[]{:S(2)}, u32[]{:S(2)}) collective-permute-start(bf16[16,4224]{1,0:T(8,128)(2,1)S(1)} %pack.5.refs_1_), channel_id=1, source_target_pairs={{0,16},{1,17},{2,18},{3,19},{4,20},{5,21},{6,22},{7,23},{8,24},{9,... | collective-permute-start | bytes 405512 | tf_op jit(solution)/shard_map/ppermute | solution.py:265
  9.1 5.8 %collective-permute-start.4 = (bf16[16,4224]{1,0:T(8,128)(2,1)S(1)}, bf16[16,4224]{1,0:T(8,128)(2,1)S(1)}, u32[]{:S(2)}, u32[]{:S(2)}) collective-permute-start(bf16[16,4224]{1,0:T(8,128)(2,1)S(1)} %pack.5.refs_1_), channel_id=1, source_target_pairs={{0,8},{1,9},{2,10},{3,11},{4,12},{5,13},{6,14},{7,15},{8,0},{9,1},... | collective-permute-start | bytes 405512 | tf_op jit(solution)/shard_map/ppermute | solution.py:265
  10.6 6.2 %collective-permute-start.3 = (bf16[16,4224]{1,0:T(8,128)(2,1)S(1)}, bf16[16,4224]{1,0:T(8,128)(2,1)S(1)}, u32[]{:S(2)}, u32[]{:S(2)}) collective-permute-start(bf16[16,4224]{1,0:T(8,128)(2,1)S(1)} %pack.5.refs_1_), channel_id=1, source_target_pairs={{0,24},{1,25},{2,26},{3,27},{4,28},{5,29},{6,30},{7,31},{8,16},{9,... | collective-permute-start | bytes 405512 | tf_op jit(solution)/shard_map/ppermute | solution.py:265
  11.0 9.6 %copy-start = (bf16[1,4096,768]{2,1,0:T(8,128)(2,1)S(1)}, bf16[1,4096,768]{2,1,0:T(8,128)(2,1)}, u32[]{:S(2)}) copy-start(bf16[1,4096,768]{2,1,0:T(8,128)(2,1)} %param.23) | copy-start | bytes 18874372
  11.0 9.6 %copy-start.1 = (bf16[1,4096,768]{2,1,0:T(8,128)(2,1)S(1)}, bf16[1,4096,768]{2,1,0:T(8,128)(2,1)}, u32[]{:S(2)}) copy-start(bf16[1,4096,768]{2,1,0:T(8,128)(2,1)} %param.24) | copy-start | bytes 18874372
  11.0 9.6 %copy-start.2 = (bf16[1,768,4096]{2,1,0:T(8,128)(2,1)S(1)}, bf16[1,768,4096]{2,1,0:T(8,128)(2,1)}, u32[]{:S(2)}) copy-start(bf16[1,768,4096]{2,1,0:T(8,128)(2,1)} %param.25) | copy-start | bytes 18874372
  16.9 3.6 %collective-permute-start.6 = (bf16[64,4224]{1,0:T(8,128)(2,1)S(1)}, bf16[64,4224]{1,0:T(8,128)(2,1)S(1)}, u32[]{:S(2)}, u32[]{:S(2)}) collective-permute-start(bf16[64,4224]{1,0:T(8,128)(2,1)S(1)} %pack.6.here_ref), channel_id=1, source_target_pairs={{0,4},{1,5},{2,6},{3,7},{4,0},{5,1},{6,2},{7,3},{8,12},{9,13},{10,... | collective-permute-start | bytes 1622024 | tf_op jit(solution)/shard_map/ppermute | solution.py:265
  17.0 6.3 %collective-permute-start.9 = (bf16[16,4224]{1,0:T(8,128)(2,1)S(1)}, bf16[16,4224]{1,0:T(8,128)(2,1)S(1)}, u32[]{:S(2)}, u32[]{:S(2)}) collective-permute-start(bf16[16,4224]{1,0:T(8,128)(2,1)S(1)} %pack.4.refs_0_.refs_1_), channel_id=1, source_target_pairs={{0,16},{1,17},{2,18},{3,19},{4,20},{5,21},{6,22},{7,23},{8,24},{9,... | collective-permute-start | bytes 405512 | tf_op jit(solution)/shard_map/ppermute | solution.py:265
  18.0 6.4 %collective-permute-start.8 = (bf16[16,4224]{1,0:T(8,128)(2,1)S(1)}, bf16[16,4224]{1,0:T(8,128)(2,1)S(1)}, u32[]{:S(2)}, u32[]{:S(2)}) collective-permute-start(bf16[16,4224]{1,0:T(8,128)(2,1)S(1)} %pack.4.refs_0_.refs_1_), channel_id=1, source_target_pairs={{0,8},{1,9},{2,10},{3,11},{4,12},{5,13},{6,14},{7,15},{8,0},{9,1},... | collective-permute-start | bytes 405512 | tf_op jit(solution)/shard_map/ppermute | solution.py:265
  19.5 7.5 %collective-permute-start.7 = (bf16[16,4224]{1,0:T(8,128)(2,1)S(1)}, bf16[16,4224]{1,0:T(8,128)(2,1)S(1)}, u32[]{:S(2)}, u32[]{:S(2)}) collective-permute-start(bf16[16,4224]{1,0:T(8,128)(2,1)S(1)} %pack.4.refs_0_.refs_1_), channel_id=1, source_target_pairs={{0,24},{1,25},{2,26},{3,27},{4,28},{5,29},{6,30},{7,31},{8,16},{9,... | collective-permute-start | bytes 405512 | tf_op jit(solution)/shard_map/ppermute | solution.py:265
  27.1 2.0 %collective-permute-start.10 = (bf16[64,4096]{1,0:T(8,128)(2,1)S(1)}, bf16[64,4096]{1,0:T(8,128)(2,1)S(1)}, u32[]{:S(2)}, u32[]{:S(2)}) collective-permute-start(bf16[64,4096]{1,0:T(8,128)(2,1)S(1)} %get-tuple-element.10), channel_id=1, source_target_pairs={{0,4},{1,5},{2,6},{3,7},{4,0},{5,1},{6,2},{7,3},{8,12},{9,13},{10,... | collective-permute-start | bytes 1572872 | tf_op jit(solution)/shard_map/ppermute | solution.py:265
  27.2 2.7 %collective-permute-start.14 = (bf16[64,4224]{1,0:T(8,128)(2,1)S(1)}, bf16[64,4224]{1,0:T(8,128)(2,1)S(1)}, u32[]{:S(2)}, u32[]{:S(2)}) collective-permute-start(bf16[64,4224]{1,0:T(8,128)(2,1)S(1)} %pack.7.here_ref), channel_id=1, source_target_pairs={{0,4},{1,5},{2,6},{3,7},{4,0},{5,1},{6,2},{7,3},{8,12},{9,13},{10,... | collective-permute-start | bytes 1622024 | tf_op jit(solution)/shard_map/ppermute | solution.py:265
  32.5 3.8 %collective-permute-start.15 = (bf16[64,4096]{1,0:T(8,128)(2,1)S(1)}, bf16[64,4096]{1,0:T(8,128)(2,1)S(1)}, u32[]{:S(2)}, u32[]{:S(2)}) collective-permute-start(bf16[64,4096]{1,0:T(8,128)(2,1)S(1)} %get-tuple-element.13), channel_id=1, source_target_pairs={{0,4},{1,5},{2,6},{3,7},{4,0},{5,1},{6,2},{7,3},{8,12},{9,13},{10,... | collective-permute-start | bytes 1572872 | tf_op jit(solution)/shard_map/ppermute | solution.py:265
  32.8 7.3 %collective-permute-start.11 = (bf16[16,4096]{1,0:T(8,128)(2,1)S(1)}, bf16[16,4096]{1,0:T(8,128)(2,1)S(1)}, u32[]{:S(2)}, u32[]{:S(2)}) collective-permute-start(bf16[16,4096]{1,0:T(8,128)(2,1)S(1)} %get-tuple-element.21), channel_id=1, source_target_pairs={{0,24},{1,25},{2,26},{3,27},{4,28},{5,29},{6,30},{7,31},{8,16},{9,... | collective-permute-start | bytes 393224 | tf_op jit(solution)/shard_map/ppermute | solution.py:265
  34.8 8.2 %collective-permute-start.13 = (bf16[16,4096]{1,0:T(8,128)(2,1)S(1)}, bf16[16,4096]{1,0:T(8,128)(2,1)S(1)}, u32[]{:S(2)}, u32[]{:S(2)}) collective-permute-start(bf16[16,4096]{1,0:T(8,128)(2,1)S(1)} %get-tuple-element.22), channel_id=1, source_target_pairs={{0,16},{1,17},{2,18},{3,19},{4,20},{5,21},{6,22},{7,23},{8,24},{9,... | collective-permute-start | bytes 393224 | tf_op jit(solution)/shard_map/ppermute | solution.py:265
  35.3 7.7 %collective-permute-start.12 = (bf16[16,4096]{1,0:T(8,128)(2,1)S(1)}, bf16[16,4096]{1,0:T(8,128)(2,1)S(1)}, u32[]{:S(2)}, u32[]{:S(2)}) collective-permute-start(bf16[16,4096]{1,0:T(8,128)(2,1)S(1)} %get-tuple-element.23), channel_id=1, source_target_pairs={{0,8},{1,9},{2,10},{3,11},{4,12},{5,13},{6,14},{7,15},{8,0},{9,1},... | collective-permute-start | bytes 393224 | tf_op jit(solution)/shard_map/ppermute | solution.py:265
  36.5 9.2 %collective-permute-start.16 = (bf16[16,4096]{1,0:T(8,128)(2,1)S(1)}, bf16[16,4096]{1,0:T(8,128)(2,1)S(1)}, u32[]{:S(2)}, u32[]{:S(2)}) collective-permute-start(bf16[16,4096]{1,0:T(8,128)(2,1)S(1)} %get-tuple-element.18), channel_id=1, source_target_pairs={{0,24},{1,25},{2,26},{3,27},{4,28},{5,29},{6,30},{7,31},{8,16},{9,... | collective-permute-start | bytes 393224 | tf_op jit(solution)/shard_map/ppermute | solution.py:265
  38.5 9.4 %collective-permute-start.18 = (bf16[16,4096]{1,0:T(8,128)(2,1)S(1)}, bf16[16,4096]{1,0:T(8,128)(2,1)S(1)}, u32[]{:S(2)}, u32[]{:S(2)}) collective-permute-start(bf16[16,4096]{1,0:T(8,128)(2,1)S(1)} %get-tuple-element.19), channel_id=1, source_target_pairs={{0,16},{1,17},{2,18},{3,19},{4,20},{5,21},{6,22},{7,23},{8,24},{9,... | collective-permute-start | bytes 393224 | tf_op jit(solution)/shard_map/ppermute | solution.py:265
  40.1 7.9 %collective-permute-start.17 = (bf16[16,4096]{1,0:T(8,128)(2,1)S(1)}, bf16[16,4096]{1,0:T(8,128)(2,1)S(1)}, u32[]{:S(2)}, u32[]{:S(2)}) collective-permute-start(bf16[16,4096]{1,0:T(8,128)(2,1)S(1)} %get-tuple-element.20), channel_id=1, source_target_pairs={{0,8},{1,9},{2,10},{3,11},{4,12},{5,13},{6,14},{7,15},{8,0},{9,1},... | collective-permute-start | bytes 393224 | tf_op jit(solution)/shard_map/ppermute | solution.py:265
  43.0 9.1 %collective-permute-start.21 = (bf16[8,4096]{1,0:T(8,128)(2,1)S(1)}, bf16[8,4096]{1,0:T(8,128)(2,1)S(1)}, u32[]{:S(2)}, u32[]{:S(2)}) collective-permute-start(bf16[8,4096]{1,0:T(8,128)(2,1)S(1)} %slice.80), channel_id=1, source_target_pairs={{0,1},{1,0},{2,3},{3,2},{4,5},{5,4},{6,7},{7,6},{8,9},{9,8},{10,11... | collective-permute-start | bytes 196616 | tf_op jit(solution)/shard_map/ppermute | solution.py:265
  48.0 6.9 %collective-permute-start.19 = (bf16[8,4096]{1,0:T(8,128)(2,1)S(1)}, bf16[8,4096]{1,0:T(8,128)(2,1)S(1)}, u32[]{:S(2)}, u32[]{:S(2)}) collective-permute-start(bf16[8,4096]{1,0:T(8,128)(2,1)S(1)} %get-tuple-element.24), channel_id=1, source_target_pairs={{0,2},{1,3},{2,0},{3,1},{4,6},{5,7},{6,4},{7,5},{8,10},{9,11},{10,... | collective-permute-start | bytes 196616 | tf_op jit(solution)/shard_map/ppermute | solution.py:265
  51.0 6.1 %collective-permute-start.20 = (bf16[8,4096]{1,0:T(8,128)(2,1)S(1)}, bf16[8,4096]{1,0:T(8,128)(2,1)S(1)}, u32[]{:S(2)}, u32[]{:S(2)}) collective-permute-start(bf16[8,4096]{1,0:T(8,128)(2,1)S(1)} %get-tuple-element.25), channel_id=1, source_target_pairs={{0,3},{1,2},{2,1},{3,0},{4,7},{5,6},{6,5},{7,4},{8,11},{9,10},{10,... | collective-permute-start | bytes 196616 | tf_op jit(solution)/shard_map/ppermute | solution.py:265

commit v4 on v3

--- a/solution.py
+++ b/solution.py
@@ -321,16 +321,22 @@
     first = gather_plane(pack([rows] + [line[k] for k in near[1:]]), after=(second,))
     pieces = (gate_weight[0], up_weight[0], down_weight[0])
     first, first_other = expert_piece(first, exchange(first, 1, 0), experts, pieces)
-    second = gather_plane(second, after=(first,))
-    second, first_other = lax.optimization_barrier((second, first_other))
-    second, second_other = expert_piece(
-        second, exchange(second, 1, 0), experts, pieces
-    )
-    line = plane_sum(core_sum(first, first_other))
-    total, packed = line[:count], line.astype(jnp.bfloat16)
-    line = plane_sum(core_sum(second, second_other)).astype(jnp.bfloat16)
+    second = gather_plane(second)
+    second_other = exchange(second, 1, 0)
+    second, second_other = expert_piece(second, second_other, experts, pieces, (first,))
+    plane = masks()[2]
+    sums = core_sum(second, second_other)
+    size = sums.shape[0] // (1 + len(plane))
+    packed, farther = sums.astype(jnp.bfloat16), sums[:size]
+    arrived = [exchange(block(packed, size, i + 1), n, 0) for i, n in enumerate(plane)]
+    arrived[1], nearer = lax.optimization_barrier((arrived[1], core_sum(first, first_other)))
+    for piece in arrived:
+        farther = farther + f32(piece)
+    farther = farther.astype(jnp.bfloat16)
+    nearer = plane_sum(nearer)
+    total, packed = nearer[:count], nearer.astype(jnp.bfloat16)
     for i, k in enumerate(far):
-        total = total + f32(exchange(block(line, count, i), 0, k))
+        total = total + f32(exchange(block(farther, count, i), 0, k))
     for i, k in enumerate(near[1:]):
         total = total + f32(exchange(block(packed, count, i + 1), 0, k))
     total = total.astype(jnp.bfloat16)

time: 58 us -> 54.8 us (0.945)
  waiting for transfers between devices: 19.4 us -> 16.9 us
  starting transfers between devices: 26.6 us -> 25.8 us
    ppermute x22, waiting for transfers between devices: 19.4 us -> 16.9 us  [exchange(): return lax.ppermute(rows, ('node', 'local'), pairs)]
    ppermute x22, starting transfers between devices: 26.6 us -> 25.8 us  [exchange(): return lax.ppermute(rows, ('node', 'local'), pairs)]
  transfers between devices with their start and end apart: 22 -> 22, of which waited for: 12 -> 11; matrix products, arithmetic and copies ran while one was open for 1% -> 1% of each run, Pallas kernels for 10% -> 11%
where the time goes in v4:
time: 54.8 us; the launch traced here: 54.6 us
  starting transfers between devices  25.8 us (47%)
  waiting for transfers between devices  16.9 us (31%)
  Pallas kernels  9.89 us (18%)
  other arithmetic  1.07 us (2%)
  between operations  0.9 us (2%)
    ppermute x22, starting transfers between devices, exchange(): return lax.ppermute(rows, ('node', 'local'), pairs)  25.8 us
    ppermute x22, waiting for transfers between devices, exchange(): return lax.ppermute(rows, ('node', 'local'), pairs)  16.9 us
    pallas_call x2, Pallas kernels, expert_piece(): pl.pallas_call(functools.partial(experts_kernel, experts, len(after)), ou...  5.39 us
    pallas_call x1, Pallas kernels, attend(): pl.pallas_call(functools.partial(attend_kernel, kv_heads, 1.0 / math.sqrt...  3.33 us
  transfers between devices with their start and end apart: 22, of which 11 were waited for; matrix products, arithmetic and copies ran while one was open for 1% of the time, Pallas kernels for 11%

profile of v4, /device:TPU:0, one launch (start us, length us, event | category | flops | bytes accessed | tf_op | source)
XLA Modules:
  0.0 54.6 jit_solution(5315729047268638391)
XLA Ops:
  0.6 1.1 %prepare.1.refs_0_ = bf16[8,4224]{1,0:T(8,128)(2,1)S(1)} custom-call(bf16[8,4096]{1,0:T(8,128)(2,1)} %hidden_hbm.1, bf16[4096]{0:T(1024)(128)(2,1)} %gain_hbm.1, s32[8,8]{1,0:T(8,128)} %ids_hbm.1, f32[8,8]{1,0:T(8,128)} %scores_hbm.1), custom_call_target="tpu_custom_call" | custom-call | tf_op jit(solution)/shard_map/prepare/pallas_call | solution.py:58
  1.7 3.1 %collective-permute-start.6 = (bf16[8,4224]{1,0:T(8,128)(2,1)S(1)}, bf16[8,4224]{1,0:T(8,128)(2,1)S(1)}, u32[]{:S(2)}, u32[]{:S(2)}) collective-permute-start(bf16[8,4224]{1,0:T(8,128)(2,1)S(1)} %prepare.1.refs_0_), channel_id=1, source_target_pairs={{0,1},{1,0},{2,3},{3,2},{4,5},{5,4},{6,7},{7,6},{8,9},{9,8},{10,11... | collective-permute-start | bytes 202760 | tf_op jit(solution)/shard_map/ppermute | solution.py:265
  4.8 2.6 %collective-permute-start = (bf16[8,4224]{1,0:T(8,128)(2,1)S(1)}, bf16[8,4224]{1,0:T(8,128)(2,1)S(1)}, u32[]{:S(2)}, u32[]{:S(2)}) collective-permute-start(bf16[8,4224]{1,0:T(8,128)(2,1)S(1)} %prepare.1.refs_0_), channel_id=1, source_target_pairs={{0,2},{1,3},{2,0},{3,1},{4,6},{5,7},{6,4},{7,5},{8,10},{9,11},{10,... | collective-permute-start | bytes 202760 | tf_op jit(solution)/shard_map/ppermute | solution.py:265
  7.4 0.0 collective-permute-done.6.refs_1_
  7.4 2.7 %collective-permute-start.7 = (bf16[16,4224]{1,0:T(8,128)(2,1)S(1)}, bf16[16,4224]{1,0:T(8,128)(2,1)S(1)}, u32[]{:S(2)}, u32[]{:S(2)}) collective-permute-start(bf16[16,4224]{1,0:T(8,128)(2,1)S(1)} %pack.6.refs_1_), channel_id=1, source_target_pairs={{0,24},{1,25},{2,26},{3,27},{4,28},{5,29},{6,30},{7,31},{8,16},{9,... | collective-permute-start | bytes 405512 | tf_op jit(solution)/shard_map/ppermute | solution.py:265
  10.1 0.5 collective-permute-start.8
  10.7 0.3 collective-permute-start.9
  11.0 0.0 slice-start.3
  11.0 0.0 slice-start.5
  11.0 3.3 %attend.1.refs_0_ = bf16[8,8192]{1,0:T(8,128)(2,1)} custom-call(s32[8]{0:T(128)} %lengths_hbm.1, bf16[8,64,128]{2,1,0:T(8,128)(2,1)} %queries_hbm.1, bf16[8,384,128]{2,1,0:T(8,128)(2,1)} %bitcast.17, bf16[8,384,128]{2,1,0:T(8,128)(2,1)} %bitcast.18, bf16[8,4,128]{2,1,0:T(4,128)(2,1)} %fresh_hbm.1, bf16[8,4,128]{2,1,0:T(4,128)(2,1)} %new_hbm.1), custom_call_target="tpu_custom_call" | custom-call | flops 12000000000 | bytes 1572864 | tf_op jit(solution)/shard_map/attend/pallas_call | solution.py:144
  14.3 0.0 collective-permute-done.refs_1_
  14.4 0.3 collective-permute-done.7.refs_2_
  14.7 1.4 %collective-permute-done.8.refs_3_ = bf16[16,4224]{1,0:T(8,128)(2,1)S(1)} collective-permute-done((bf16[16,4224]{1,0:T(8,128)(2,1)S(1)}, bf16[16,4224]{1,0:T(8,128)(2,1)S(1)}, u32[]{:S(2)}, u32[]{:S(2)}) %collective-permute-start.8) | collective-permute-done | bytes 135200 | tf_op jit(solution)/shard_map/ppermute | solution.py:265
  16.1 0.0 collective-permute-done.9.refs_4_
  16.1 0.1 collective-permute-start.10
  16.2 2.4 %collective-permute-start.2 = (bf16[16,4224]{1,0:T(8,128)(2,1)S(1)}, bf16[16,4224]{1,0:T(8,128)(2,1)S(1)}, u32[]{:S(2)}, u32[]{:S(2)}) collective-permute-start(bf16[16,4224]{1,0:T(8,128)(2,1)S(1)} %pack.4.refs_0_), channel_id=1, source_target_pairs={{0,24},{1,25},{2,26},{3,27},{4,28},{5,29},{6,30},{7,31},{8,16},{9,... | collective-permute-start | bytes 405512 | tf_op jit(solution)/shard_map/ppermute | solution.py:265
  18.7 0.5 collective-permute-start.3
  19.2 0.6 %collective-permute-start.4 = (bf16[16,4224]{1,0:T(8,128)(2,1)S(1)}, bf16[16,4224]{1,0:T(8,128)(2,1)S(1)}, u32[]{:S(2)}, u32[]{:S(2)}) collective-permute-start(bf16[16,4224]{1,0:T(8,128)(2,1)S(1)} %pack.4.refs_0_), channel_id=1, source_target_pairs={{0,16},{1,17},{2,18},{3,19},{4,20},{5,21},{6,22},{7,23},{8,24},{9,... | collective-permute-start | bytes 405512 | tf_op jit(solution)/shard_map/ppermute | solution.py:265
  19.8 3.8 %collective-permute-done.2.refs_1_ = bf16[16,4224]{1,0:T(8,128)(2,1)S(1)} collective-permute-done((bf16[16,4224]{1,0:T(8,128)(2,1)S(1)}, bf16[16,4224]{1,0:T(8,128)(2,1)S(1)}, u32[]{:S(2)}, u32[]{:S(2)}) %collective-permute-start.2) | collective-permute-done | bytes 135200 | tf_op jit(solution)/shard_map/ppermute | solution.py:265
  23.6 2.5 %collective-permute-done.3.refs_2_ = bf16[16,4224]{1,0:T(8,128)(2,1)S(1)} collective-permute-done((bf16[16,4224]{1,0:T(8,128)(2,1)S(1)}, bf16[16,4224]{1,0:T(8,128)(2,1)S(1)}, u32[]{:S(2)}, u32[]{:S(2)}) %collective-permute-start.3) | collective-permute-done | bytes 135200 | tf_op jit(solution)/shard_map/ppermute | solution.py:265
  26.1 0.0 collective-permute-done.4.refs_3_
  26.1 0.1 collective-permute-start.5
  26.3 2.7 %expert_piece.2 = (bf16[64,4096]{1,0:T(8,128)(2,1)S(1)}, bf16[64,4096]{1,0:T(8,128)(2,1)S(1)}) custom-call(bf16[64,4224]{1,0:T(8,128)(2,1)S(1)} %pack.7.here_ref, bf16[64,4224]{1,0:T(8,128)(2,1)S(1)} %collective-permute-done.10.there_ref, bf16[4096,768]{1,0:T(8,128)(2,1)S(1)} %bitcast.7, bf16[4096,768]{1,0:T(8,128)(2,1)S(1)} %bitcast.11, ...), custom_call_target="tpu_custom_call" | custom-call | flops 2415919104 | tf_op jit(solution)/shard_map/expert_piece/pallas_call | solution.py:240
  29.0 0.0 collective-permute-done.5.there_ref
  29.0 2.7 %expert_piece.3 = (bf16[64,4096]{1,0:T(8,128)(2,1)S(1)}, bf16[64,4096]{1,0:T(8,128)(2,1)S(1)}) custom-call(bf16[64,4224]{1,0:T(8,128)(2,1)S(1)} %pack.5.here_ref, bf16[64,4224]{1,0:T(8,128)(2,1)S(1)} %collective-permute-done.5.there_ref, bf16[4096,768]{1,0:T(8,128)(2,1)S(1)} %bitcast.8, bf16[4096,768]{1,0:T(8,128)(2,1)S(1)} %bitcast.12, ...), custom_call_target="tpu_custom_call" | custom-call | flops 2415919104 | tf_op jit(solution)/shard_map/expert_piece/pallas_call | solution.py:240
  31.7 0.5 collective-permute-start.11
  32.2 0.1 collective-permute-start.13
  32.3 1.5 %collective-permute-done.11 = bf16[64,4096]{1,0:T(8,128)(2,1)S(1)} collective-permute-done((bf16[64,4096]{1,0:T(8,128)(2,1)S(1)}, bf16[64,4096]{1,0:T(8,128)(2,1)S(1)}, u32[]{:S(2)}, u32[]{:S(2)}) %collective-permute-start.11) | collective-permute-done | bytes 524320 | tf_op jit(solution)/shard_map/ppermute | solution.py:265
  33.8 0.1 convert_add_fusion.1
  33.9 1.6 %collective-permute-start.12 = (bf16[16,4096]{1,0:T(8,128)(2,1)S(1)}, bf16[16,4096]{1,0:T(8,128)(2,1)S(1)}, u32[]{:S(2)}, u32[]{:S(2)}) collective-permute-start(bf16[16,4096]{1,0:T(8,128)(2,1)S(1)} %get-tuple-element.18), channel_id=1, source_target_pairs={{0,8},{1,9},{2,10},{3,11},{4,12},{5,13},{6,14},{7,15},{8,0},{9,1},... | collective-permute-start | bytes 393224 | tf_op jit(solution)/shard_map/ppermute | solution.py:265
  35.5 1.4 %collective-permute-start.18 = (bf16[16,4096]{1,0:T(8,128)(2,1)S(1)}, bf16[16,4096]{1,0:T(8,128)(2,1)S(1)}, u32[]{:S(2)}, u32[]{:S(2)}) collective-permute-start(bf16[16,4096]{1,0:T(8,128)(2,1)S(1)} %get-tuple-element.17), channel_id=1, source_target_pairs={{0,16},{1,17},{2,18},{3,19},{4,20},{5,21},{6,22},{7,23},{8,24},{9,... | collective-permute-start | bytes 393224 | tf_op jit(solution)/shard_map/ppermute | solution.py:265
  36.9 0.6 %collective-permute-start.17 = (bf16[16,4096]{1,0:T(8,128)(2,1)S(1)}, bf16[16,4096]{1,0:T(8,128)(2,1)S(1)}, u32[]{:S(2)}, u32[]{:S(2)}) collective-permute-start(bf16[16,4096]{1,0:T(8,128)(2,1)S(1)} %get-tuple-element.16), channel_id=1, source_target_pairs={{0,24},{1,25},{2,26},{3,27},{4,28},{5,29},{6,30},{7,31},{8,16},{9,... | collective-permute-start | bytes 393224 | tf_op jit(solution)/shard_map/ppermute | solution.py:265
  37.5 0.1 convert_add_fusion
  37.6 2.5 %collective-permute-done.12 = bf16[16,4096]{1,0:T(8,128)(2,1)S(1)} collective-permute-done((bf16[16,4096]{1,0:T(8,128)(2,1)S(1)}, bf16[16,4096]{1,0:T(8,128)(2,1)S(1)}, u32[]{:S(2)}, u32[]{:S(2)}) %collective-permute-start.12) | collective-permute-done | bytes 131104 | tf_op jit(solution)/shard_map/ppermute | solution.py:265
  40.1 0.1 convert_element_type.59
  40.2 1.5 %collective-permute-start.16 = (bf16[16,4096]{1,0:T(8,128)(2,1)S(1)}, bf16[16,4096]{1,0:T(8,128)(2,1)S(1)}, u32[]{:S(2)}, u32[]{:S(2)}) collective-permute-start(bf16[16,4096]{1,0:T(8,128)(2,1)S(1)} %get-tuple-element.20), channel_id=1, source_target_pairs={{0,16},{1,17},{2,18},{3,19},{4,20},{5,21},{6,22},{7,23},{8,24},{9,... | collective-permute-start | bytes 393224 | tf_op jit(solution)/shard_map/ppermute | solution.py:265
  41.7 1.7 %collective-permute-start.15 = (bf16[16,4096]{1,0:T(8,128)(2,1)S(1)}, bf16[16,4096]{1,0:T(8,128)(2,1)S(1)}, u32[]{:S(2)}, u32[]{:S(2)}) collective-permute-start(bf16[16,4096]{1,0:T(8,128)(2,1)S(1)} %get-tuple-element.21), channel_id=1, source_target_pairs={{0,8},{1,9},{2,10},{3,11},{4,12},{5,13},{6,14},{7,15},{8,0},{9,1},... | collective-permute-start | bytes 393224 | tf_op jit(solution)/shard_map/ppermute | solution.py:265
  43.4 0.4 collective-permute-start.14
  43.8 0.2 collective-permute-done.18
  44.0 0.1 fusion.2
  44.1 3.9 %collective-permute-start.20 = (bf16[8,4096]{1,0:T(8,128)(2,1)S(1)}, bf16[8,4096]{1,0:T(8,128)(2,1)S(1)}, u32[]{:S(2)}, u32[]{:S(2)}) collective-permute-start(bf16[8,4096]{1,0:T(8,128)(2,1)S(1)} %get-tuple-element.23), channel_id=1, source_target_pairs={{0,3},{1,2},{2,1},{3,0},{4,7},{5,6},{6,5},{7,4},{8,11},{9,10},{10,... | collective-permute-start | bytes 196616 | tf_op jit(solution)/shard_map/ppermute | solution.py:265
  48.0 0.4 collective-permute-done.16
  48.4 1.1 %collective-permute-done.14 = bf16[16,4096]{1,0:T(8,128)(2,1)S(1)} collective-permute-done((bf16[16,4096]{1,0:T(8,128)(2,1)S(1)}, bf16[16,4096]{1,0:T(8,128)(2,1)S(1)}, u32[]{:S(2)}, u32[]{:S(2)}) %collective-permute-start.14) | collective-permute-done | bytes 131104 | tf_op jit(solution)/shard_map/ppermute | solution.py:265
  49.5 0.1 convert_add_fusion.2
  49.6 1.2 %collective-permute-start.21 = (bf16[8,4096]{1,0:T(8,128)(2,1)S(1)}, bf16[8,4096]{1,0:T(8,128)(2,1)S(1)}, u32[]{:S(2)}, u32[]{:S(2)}) collective-permute-start(bf16[8,4096]{1,0:T(8,128)(2,1)S(1)} %slice.75), channel_id=1, source_target_pairs={{0,1},{1,0},{2,3},{3,2},{4,5},{5,4},{6,7},{7,6},{8,9},{9,8},{10,11... | collective-permute-start | bytes 196616 | tf_op jit(solution)/shard_map/ppermute | solution.py:265
  50.8 2.4 %collective-permute-done.19 = bf16[8,4096]{1,0:T(8,128)(2,1)S(1)} collective-permute-done((bf16[8,4096]{1,0:T(8,128)(2,1)S(1)}, bf16[8,4096]{1,0:T(8,128)(2,1)S(1)}, u32[]{:S(2)}, u32[]{:S(2)}) %collective-permute-start.19) | collective-permute-done | bytes 65568 | tf_op jit(solution)/shard_map/ppermute | solution.py:265
  53.2 0.7 %collective-permute-done.21 = bf16[8,4096]{1,0:T(8,128)(2,1)S(1)} collective-permute-done((bf16[8,4096]{1,0:T(8,128)(2,1)S(1)}, bf16[8,4096]{1,0:T(8,128)(2,1)S(1)}, u32[]{:S(2)}, u32[]{:S(2)}) %collective-permute-start.21) | collective-permute-done | bytes 65568 | tf_op jit(solution)/shard_map/ppermute | solution.py:265
  53.9 0.7 %fusion.5 = bf16[8,4096]{1,0:T(8,128)(2,1)} fusion(f32[16,4096]{1,0:T(8,128)S(1)} %convert_add_fusion.2, bf16[8,4096]{1,0:T(8,128)(2,1)S(1)} %collective-permute-done.21, bf16[8,4096]{1,0:T(8,128)(2,1)S(1)} %collective-permute-done.20, bf16[8,4096]{1,0:T(8,128)(2,1)S(1)} %collective-permute-done.19), kind=kLoop, calls=%fused_computation.11 | loop fusion | flops 229376 | bytes 393216 | tf_op jit(solution)/shard_map/convert_element_type | solution.py:342
  (29 shorter events, 0.2 us)
Async XLA Ops:
  1.7 5.7 %collective-permute-start.6 = (bf16[8,4224]{1,0:T(8,128)(2,1)S(1)}, bf16[8,4224]{1,0:T(8,128)(2,1)S(1)}, u32[]{:S(2)}, u32[]{:S(2)}) collective-permute-start(bf16[8,4224]{1,0:T(8,128)(2,1)S(1)} %prepare.1.refs_0_), channel_id=1, source_target_pairs={{0,1},{1,0},{2,3},{3,2},{4,5},{5,4},{6,7},{7,6},{8,9},{9,8},{10,11... | collective-permute-start | bytes 202760 | tf_op jit(solution)/shard_map/ppermute | solution.py:265
  4.8 9.5 %collective-permute-start = (bf16[8,4224]{1,0:T(8,128)(2,1)S(1)}, bf16[8,4224]{1,0:T(8,128)(2,1)S(1)}, u32[]{:S(2)}, u32[]{:S(2)}) collective-permute-start(bf16[8,4224]{1,0:T(8,128)(2,1)S(1)} %prepare.1.refs_0_), channel_id=1, source_target_pairs={{0,2},{1,3},{2,0},{3,1},{4,6},{5,7},{6,4},{7,5},{8,10},{9,11},{10,... | collective-permute-start | bytes 202760 | tf_op jit(solution)/shard_map/ppermute | solution.py:265
  7.4 7.0 %collective-permute-start.1 = (bf16[8,4224]{1,0:T(8,128)(2,1)S(1)}, bf16[8,4224]{1,0:T(8,128)(2,1)S(1)}, u32[]{:S(2)}, u32[]{:S(2)}) collective-permute-start(bf16[8,4224]{1,0:T(8,128)(2,1)S(1)} %prepare.1.refs_0_), channel_id=1, source_target_pairs={{0,3},{1,2},{2,1},{3,0},{4,7},{5,6},{6,5},{7,4},{8,11},{9,10},{10,... | collective-permute-start | bytes 202760 | tf_op jit(solution)/shard_map/ppermute | solution.py:265
  7.4 7.3 %collective-permute-start.7 = (bf16[16,4224]{1,0:T(8,128)(2,1)S(1)}, bf16[16,4224]{1,0:T(8,128)(2,1)S(1)}, u32[]{:S(2)}, u32[]{:S(2)}) collective-permute-start(bf16[16,4224]{1,0:T(8,128)(2,1)S(1)} %pack.6.refs_1_), channel_id=1, source_target_pairs={{0,24},{1,25},{2,26},{3,27},{4,28},{5,29},{6,30},{7,31},{8,16},{9,... | collective-permute-start | bytes 405512 | tf_op jit(solution)/shard_map/ppermute | solution.py:265
  10.1 6.0 %collective-permute-start.8 = (bf16[16,4224]{1,0:T(8,128)(2,1)S(1)}, bf16[16,4224]{1,0:T(8,128)(2,1)S(1)}, u32[]{:S(2)}, u32[]{:S(2)}) collective-permute-start(bf16[16,4224]{1,0:T(8,128)(2,1)S(1)} %pack.6.refs_1_), channel_id=1, source_target_pairs={{0,8},{1,9},{2,10},{3,11},{4,12},{5,13},{6,14},{7,15},{8,0},{9,1},... | collective-permute-start | bytes 405512 | tf_op jit(solution)/shard_map/ppermute | solution.py:265
  10.7 5.4 %collective-permute-start.9 = (bf16[16,4224]{1,0:T(8,128)(2,1)S(1)}, bf16[16,4224]{1,0:T(8,128)(2,1)S(1)}, u32[]{:S(2)}, u32[]{:S(2)}) collective-permute-start(bf16[16,4224]{1,0:T(8,128)(2,1)S(1)} %pack.6.refs_1_), channel_id=1, source_target_pairs={{0,16},{1,17},{2,18},{3,19},{4,20},{5,21},{6,22},{7,23},{8,24},{9,... | collective-permute-start | bytes 405512 | tf_op jit(solution)/shard_map/ppermute | solution.py:265
  11.0 15.2 %slice-start = ((s8[6291456]{0:T(1024)(128)(4,1)}), s8[4194304]{0:T(1024)(128)(4,1)S(1)}, s32[]{:S(2)}) async-start(s8[6291456]{0:T(1024)(128)(4,1)} %bitcast.5), calls=%async_computation | async-start | bytes 8388608
  11.0 15.2 %slice-start.2 = ((s8[6291456]{0:T(1024)(128)(4,1)}), s8[4194304]{0:T(1024)(128)(4,1)S(1)}, s32[]{:S(2)}) async-start(s8[6291456]{0:T(1024)(128)(4,1)} %bitcast.9), calls=%async_computation.2 | async-start | bytes 8388608
  11.0 15.2 %slice-start.4 = ((s8[6291456]{0:T(1024)(128)(4,1)}), s8[4194304]{0:T(1024)(128)(4,1)S(1)}, s32[]{:S(2)}) async-start(s8[6291456]{0:T(1024)(128)(4,1)} %bitcast.13), calls=%async_computation.4 | async-start | bytes 8388608
  11.0 15.2 %slice-start.1 = ((s8[6291456]{0:T(1024)(128)(4,1)}), s8[2097152]{0:T(1024)(128)(4,1)S(1)}, s32[]{:S(2)}) async-start(s8[6291456]{0:T(1024)(128)(4,1)} %bitcast.5), calls=%async_computation.1 | async-start | bytes 4194304
  11.0 15.3 %slice-start.3 = ((s8[6291456]{0:T(1024)(128)(4,1)}), s8[2097152]{0:T(1024)(128)(4,1)S(1)}, s32[]{:S(2)}) async-start(s8[6291456]{0:T(1024)(128)(4,1)} %bitcast.9), calls=%async_computation.3 | async-start | bytes 4194304
  11.0 15.3 %slice-start.5 = ((s8[6291456]{0:T(1024)(128)(4,1)}), s8[2097152]{0:T(1024)(128)(4,1)S(1)}, s32[]{:S(2)}) async-start(s8[6291456]{0:T(1024)(128)(4,1)} %bitcast.13), calls=%async_computation.5 | async-start | bytes 4194304
  16.1 10.0 %collective-permute-start.10 = (bf16[64,4224]{1,0:T(8,128)(2,1)S(1)}, bf16[64,4224]{1,0:T(8,128)(2,1)S(1)}, u32[]{:S(2)}, u32[]{:S(2)}) collective-permute-start(bf16[64,4224]{1,0:T(8,128)(2,1)S(1)} %pack.7.here_ref), channel_id=1, source_target_pairs={{0,4},{1,5},{2,6},{3,7},{4,0},{5,1},{6,2},{7,3},{8,12},{9,13},{10,... | collective-permute-start | bytes 1622024 | tf_op jit(solution)/shard_map/ppermute | solution.py:265
  16.2 7.3 %collective-permute-start.2 = (bf16[16,4224]{1,0:T(8,128)(2,1)S(1)}, bf16[16,4224]{1,0:T(8,128)(2,1)S(1)}, u32[]{:S(2)}, u32[]{:S(2)}) collective-permute-start(bf16[16,4224]{1,0:T(8,128)(2,1)S(1)} %pack.4.refs_0_), channel_id=1, source_target_pairs={{0,24},{1,25},{2,26},{3,27},{4,28},{5,29},{6,30},{7,31},{8,16},{9,... | collective-permute-start | bytes 405512 | tf_op jit(solution)/shard_map/ppermute | solution.py:265
  18.7 7.4 %collective-permute-start.3 = (bf16[16,4224]{1,0:T(8,128)(2,1)S(1)}, bf16[16,4224]{1,0:T(8,128)(2,1)S(1)}, u32[]{:S(2)}, u32[]{:S(2)}) collective-permute-start(bf16[16,4224]{1,0:T(8,128)(2,1)S(1)} %pack.4.refs_0_), channel_id=1, source_target_pairs={{0,8},{1,9},{2,10},{3,11},{4,12},{5,13},{6,14},{7,15},{8,0},{9,1},... | collective-permute-start | bytes 405512 | tf_op jit(solution)/shard_map/ppermute | solution.py:265
  19.2 6.9 %collective-permute-start.4 = (bf16[16,4224]{1,0:T(8,128)(2,1)S(1)}, bf16[16,4224]{1,0:T(8,128)(2,1)S(1)}, u32[]{:S(2)}, u32[]{:S(2)}) collective-permute-start(bf16[16,4224]{1,0:T(8,128)(2,1)S(1)} %pack.4.refs_0_), channel_id=1, source_target_pairs={{0,16},{1,17},{2,18},{3,19},{4,20},{5,21},{6,22},{7,23},{8,24},{9,... | collective-permute-start | bytes 405512 | tf_op jit(solution)/shard_map/ppermute | solution.py:265
  26.1 2.9 %collective-permute-start.5 = (bf16[64,4224]{1,0:T(8,128)(2,1)S(1)}, bf16[64,4224]{1,0:T(8,128)(2,1)S(1)}, u32[]{:S(2)}, u32[]{:S(2)}) collective-permute-start(bf16[64,4224]{1,0:T(8,128)(2,1)S(1)} %pack.5.here_ref), channel_id=1, source_target_pairs={{0,4},{1,5},{2,6},{3,7},{4,0},{5,1},{6,2},{7,3},{8,12},{9,13},{10,... | collective-permute-start | bytes 1622024 | tf_op jit(solution)/shard_map/ppermute | solution.py:265
  31.7 2.1 %collective-permute-start.11 = (bf16[64,4096]{1,0:T(8,128)(2,1)S(1)}, bf16[64,4096]{1,0:T(8,128)(2,1)S(1)}, u32[]{:S(2)}, u32[]{:S(2)}) collective-permute-start(bf16[64,4096]{1,0:T(8,128)(2,1)S(1)} %get-tuple-element.10), channel_id=1, source_target_pairs={{0,4},{1,5},{2,6},{3,7},{4,0},{5,1},{6,2},{7,3},{8,12},{9,13},{10,... | collective-permute-start | bytes 1572872 | tf_op jit(solution)/shard_map/ppermute | solution.py:265
  32.2 5.3 %collective-permute-start.13 = (bf16[64,4096]{1,0:T(8,128)(2,1)S(1)}, bf16[64,4096]{1,0:T(8,128)(2,1)S(1)}, u32[]{:S(2)}, u32[]{:S(2)}) collective-permute-start(bf16[64,4096]{1,0:T(8,128)(2,1)S(1)} %get-tuple-element.11), channel_id=1, source_target_pairs={{0,4},{1,5},{2,6},{3,7},{4,0},{5,1},{6,2},{7,3},{8,12},{9,13},{10,... | collective-permute-start | bytes 1572872 | tf_op jit(solution)/shard_map/ppermute | solution.py:265
  33.9 6.2 %collective-permute-start.12 = (bf16[16,4096]{1,0:T(8,128)(2,1)S(1)}, bf16[16,4096]{1,0:T(8,128)(2,1)S(1)}, u32[]{:S(2)}, u32[]{:S(2)}) collective-permute-start(bf16[16,4096]{1,0:T(8,128)(2,1)S(1)} %get-tuple-element.18), channel_id=1, source_target_pairs={{0,8},{1,9},{2,10},{3,11},{4,12},{5,13},{6,14},{7,15},{8,0},{9,1},... | collective-permute-start | bytes 393224 | tf_op jit(solution)/shard_map/ppermute | solution.py:265
  35.5 8.5 %collective-permute-start.18 = (bf16[16,4096]{1,0:T(8,128)(2,1)S(1)}, bf16[16,4096]{1,0:T(8,128)(2,1)S(1)}, u32[]{:S(2)}, u32[]{:S(2)}) collective-permute-start(bf16[16,4096]{1,0:T(8,128)(2,1)S(1)} %get-tuple-element.17), channel_id=1, source_target_pairs={{0,16},{1,17},{2,18},{3,19},{4,20},{5,21},{6,22},{7,23},{8,24},{9,... | collective-permute-start | bytes 393224 | tf_op jit(solution)/shard_map/ppermute | solution.py:265
  36.9 7.1 %collective-permute-start.17 = (bf16[16,4096]{1,0:T(8,128)(2,1)S(1)}, bf16[16,4096]{1,0:T(8,128)(2,1)S(1)}, u32[]{:S(2)}, u32[]{:S(2)}) collective-permute-start(bf16[16,4096]{1,0:T(8,128)(2,1)S(1)} %get-tuple-element.16), channel_id=1, source_target_pairs={{0,24},{1,25},{2,26},{3,27},{4,28},{5,29},{6,30},{7,31},{8,16},{9,... | collective-permute-start | bytes 393224 | tf_op jit(solution)/shard_map/ppermute | solution.py:265
  40.2 8.2 %collective-permute-start.16 = (bf16[16,4096]{1,0:T(8,128)(2,1)S(1)}, bf16[16,4096]{1,0:T(8,128)(2,1)S(1)}, u32[]{:S(2)}, u32[]{:S(2)}) collective-permute-start(bf16[16,4096]{1,0:T(8,128)(2,1)S(1)} %get-tuple-element.20), channel_id=1, source_target_pairs={{0,16},{1,17},{2,18},{3,19},{4,20},{5,21},{6,22},{7,23},{8,24},{9,... | collective-permute-start | bytes 393224 | tf_op jit(solution)/shard_map/ppermute | solution.py:265
  41.7 6.7 %collective-permute-start.15 = (bf16[16,4096]{1,0:T(8,128)(2,1)S(1)}, bf16[16,4096]{1,0:T(8,128)(2,1)S(1)}, u32[]{:S(2)}, u32[]{:S(2)}) collective-permute-start(bf16[16,4096]{1,0:T(8,128)(2,1)S(1)} %get-tuple-element.21), channel_id=1, source_target_pairs={{0,8},{1,9},{2,10},{3,11},{4,12},{5,13},{6,14},{7,15},{8,0},{9,1},... | collective-permute-start | bytes 393224 | tf_op jit(solution)/shard_map/ppermute | solution.py:265
  43.4 6.1 %collective-permute-start.14 = (bf16[16,4096]{1,0:T(8,128)(2,1)S(1)}, bf16[16,4096]{1,0:T(8,128)(2,1)S(1)}, u32[]{:S(2)}, u32[]{:S(2)}) collective-permute-start(bf16[16,4096]{1,0:T(8,128)(2,1)S(1)} %get-tuple-element.19), channel_id=1, source_target_pairs={{0,24},{1,25},{2,26},{3,27},{4,28},{5,29},{6,30},{7,31},{8,16},{9,... | collective-permute-start | bytes 393224 | tf_op jit(solution)/shard_map/ppermute | solution.py:265
  44.1 6.7 %collective-permute-start.20 = (bf16[8,4096]{1,0:T(8,128)(2,1)S(1)}, bf16[8,4096]{1,0:T(8,128)(2,1)S(1)}, u32[]{:S(2)}, u32[]{:S(2)}) collective-permute-start(bf16[8,4096]{1,0:T(8,128)(2,1)S(1)} %get-tuple-element.23), channel_id=1, source_target_pairs={{0,3},{1,2},{2,1},{3,0},{4,7},{5,6},{6,5},{7,4},{8,11},{9,10},{10,... | collective-permute-start | bytes 196616 | tf_op jit(solution)/shard_map/ppermute | solution.py:265
  48.0 5.2 %collective-permute-start.19 = (bf16[8,4096]{1,0:T(8,128)(2,1)S(1)}, bf16[8,4096]{1,0:T(8,128)(2,1)S(1)}, u32[]{:S(2)}, u32[]{:S(2)}) collective-permute-start(bf16[8,4096]{1,0:T(8,128)(2,1)S(1)} %get-tuple-element.22), channel_id=1, source_target_pairs={{0,2},{1,3},{2,0},{3,1},{4,6},{5,7},{6,4},{7,5},{8,10},{9,11},{10,... | collective-permute-start | bytes 196616 | tf_op jit(solution)/shard_map/ppermute | solution.py:265
  49.6 4.3 %collective-permute-start.21 = (bf16[8,4096]{1,0:T(8,128)(2,1)S(1)}, bf16[8,4096]{1,0:T(8,128)(2,1)S(1)}, u32[]{:S(2)}, u32[]{:S(2)}) collective-permute-start(bf16[8,4096]{1,0:T(8,128)(2,1)S(1)} %slice.75), channel_id=1, source_target_pairs={{0,1},{1,0},{2,3},{3,2},{4,5},{5,4},{6,7},{7,6},{8,9},{9,8},{10,11... | collective-permute-start | bytes 196616 | tf_op jit(solution)/shard_map/ppermute | solution.py:265

commit v5 on v4

--- a/solution.py
+++ b/solution.py
@@ -268,7 +268,7 @@
 def masks():
     locals_, nodes = lax.axis_size("local"), lax.axis_size("node")
     near, far = list(range(locals_ // 2)), list(range(locals_ // 2, locals_))
-    return near, far, [nodes - 2] + list(range(2, nodes - 2, 2))
+    return near, far, list(range(nodes - 4, 0, -2)) + [nodes - 2]
 
 
 def gather_plane(line, after=()):
@@ -321,15 +321,15 @@
     first = gather_plane(pack([rows] + [line[k] for k in near[1:]]), after=(second,))
     pieces = (gate_weight[0], up_weight[0], down_weight[0])
     first, first_other = expert_piece(first, exchange(first, 1, 0), experts, pieces)
-    second = gather_plane(second)
-    second_other = exchange(second, 1, 0)
-    second, second_other = expert_piece(second, second_other, experts, pieces, (first,))
+    second = gather_plane(second, after=(first,))
+    second, first_other = lax.optimization_barrier((second, first_other))
+    second, second_other = expert_piece(second, exchange(second, 1, 0), experts, pieces)
     plane = masks()[2]
     sums = core_sum(second, second_other)
     size = sums.shape[0] // (1 + len(plane))
     packed, farther = sums.astype(jnp.bfloat16), sums[:size]
     arrived = [exchange(block(packed, size, i + 1), n, 0) for i, n in enumerate(plane)]
-    arrived[1], nearer = lax.optimization_barrier((arrived[1], core_sum(first, first_other)))
+    arrived[0], nearer = lax.optimization_barrier((arrived[0], core_sum(first, first_other)))
     for piece in arrived:
         farther = farther + f32(piece)
     farther = farther.astype(jnp.bfloat16)

time: 54.8 us -> 53.8 us (0.982)
  waiting for transfers between devices: 16.9 us -> 15.6 us
    ppermute x22, waiting for transfers between devices: 16.9 us -> 15.6 us  [exchange(): return lax.ppermute(rows, ('node', 'local'), pairs)]
  transfers between devices with their start and end apart: 22 -> 22, of which waited for: 11 -> 12; matrix products, arithmetic and copies ran while one was open for 1% -> 1% of each run, Pallas kernels for 11% -> 11%
where the time goes in v5:
time: 53.8 us; the launch traced here: 53.6 us
  starting transfers between devices  26.2 us (49%)
  waiting for transfers between devices  15.6 us (29%)
  Pallas kernels  9.88 us (18%)
  other arithmetic  1.07 us (2%)
  between operations  0.8 us (1%)
    ppermute x22, starting transfers between devices, exchange(): return lax.ppermute(rows, ('node', 'local'), pairs)  26.2 us
    ppermute x22, waiting for transfers between devices, exchange(): return lax.ppermute(rows, ('node', 'local'), pairs)  15.6 us
    pallas_call x2, Pallas kernels, expert_piece(): pl.pallas_call(functools.partial(experts_kernel, experts, len(after)), ou...  5.39 us
    pallas_call x1, Pallas kernels, attend(): pl.pallas_call(functools.partial(attend_kernel, kv_heads, 1.0 / math.sqrt...  3.33 us
  transfers between devices with their start and end apart: 22, of which 12 were waited for; matrix products, arithmetic and copies ran while one was open for 1% of the time, Pallas kernels for 11%

profile of v5, /device:TPU:0, one launch (start us, length us, event | category | flops | bytes accessed | tf_op | source)
XLA Modules:
  0.0 53.6 jit_solution(8657524013707022782)
XLA Ops:
  0.6 1.1 %prepare.1.refs_0_ = bf16[8,4224]{1,0:T(8,128)(2,1)S(1)} custom-call(bf16[8,4096]{1,0:T(8,128)(2,1)} %hidden_hbm.1, bf16[4096]{0:T(1024)(128)(2,1)} %gain_hbm.1, s32[8,8]{1,0:T(8,128)} %ids_hbm.1, f32[8,8]{1,0:T(8,128)} %scores_hbm.1), custom_call_target="tpu_custom_call" | custom-call | tf_op jit(solution)/shard_map/prepare/pallas_call | solution.py:58
  1.7 3.1 %collective-permute-start.2 = (bf16[8,4224]{1,0:T(8,128)(2,1)S(1)}, bf16[8,4224]{1,0:T(8,128)(2,1)S(1)}, u32[]{:S(2)}, u32[]{:S(2)}) collective-permute-start(bf16[8,4224]{1,0:T(8,128)(2,1)S(1)} %prepare.1.refs_0_), channel_id=1, source_target_pairs={{0,1},{1,0},{2,3},{3,2},{4,5},{5,4},{6,7},{7,6},{8,9},{9,8},{10,11... | collective-permute-start | bytes 202760 | tf_op jit(solution)/shard_map/ppermute | solution.py:265
  4.8 2.5 %collective-permute-start.1 = (bf16[8,4224]{1,0:T(8,128)(2,1)S(1)}, bf16[8,4224]{1,0:T(8,128)(2,1)S(1)}, u32[]{:S(2)}, u32[]{:S(2)}) collective-permute-start(bf16[8,4224]{1,0:T(8,128)(2,1)S(1)} %prepare.1.refs_0_), channel_id=1, source_target_pairs={{0,3},{1,2},{2,1},{3,0},{4,7},{5,6},{6,5},{7,4},{8,11},{9,10},{10,... | collective-permute-start | bytes 202760 | tf_op jit(solution)/shard_map/ppermute | solution.py:265
  7.3 0.1 collective-permute-start
  7.4 0.0 collective-permute-done.2.refs_1_
  7.4 2.6 %collective-permute-start.5 = (bf16[16,4224]{1,0:T(8,128)(2,1)S(1)}, bf16[16,4224]{1,0:T(8,128)(2,1)S(1)}, u32[]{:S(2)}, u32[]{:S(2)}) collective-permute-start(bf16[16,4224]{1,0:T(8,128)(2,1)S(1)} %pack.5.refs_1_), channel_id=1, source_target_pairs={{0,24},{1,25},{2,26},{3,27},{4,28},{5,29},{6,30},{7,31},{8,16},{9,... | collective-permute-start | bytes 405512 | tf_op jit(solution)/shard_map/ppermute | solution.py:265
  10.0 0.5 collective-permute-start.4
  10.6 0.4 collective-permute-start.3
  11.0 3.3 %attend.1.refs_0_ = bf16[8,8192]{1,0:T(8,128)(2,1)} custom-call(s32[8]{0:T(128)} %lengths_hbm.1, bf16[8,64,128]{2,1,0:T(8,128)(2,1)} %queries_hbm.1, bf16[8,384,128]{2,1,0:T(8,128)(2,1)} %bitcast.11, bf16[8,384,128]{2,1,0:T(8,128)(2,1)} %bitcast.12, bf16[8,4,128]{2,1,0:T(4,128)(2,1)} %fresh_hbm.1, bf16[8,4,128]{2,1,0:T(4,128)(2,1)} %new_hbm.1), custom_call_target="tpu_custom_call" | custom-call | flops 12000000000 | bytes 1572864 | tf_op jit(solution)/shard_map/attend/pallas_call | solution.py:144
  14.3 0.0 collective-permute-done.1.refs_2_
  14.3 0.3 collective-permute-done.5.refs_4_
  14.7 1.4 %collective-permute-done.4.refs_3_ = bf16[16,4224]{1,0:T(8,128)(2,1)S(1)} collective-permute-done((bf16[16,4224]{1,0:T(8,128)(2,1)S(1)}, bf16[16,4224]{1,0:T(8,128)(2,1)S(1)}, u32[]{:S(2)}, u32[]{:S(2)}) %collective-permute-start.4) | collective-permute-done | bytes 135200 | tf_op jit(solution)/shard_map/ppermute | solution.py:265
  16.1 0.0 collective-permute-done.3.refs_2_
  16.2 0.1 collective-permute-start.6
  16.2 2.4 %collective-permute-start.9 = (bf16[16,4224]{1,0:T(8,128)(2,1)S(1)}, bf16[16,4224]{1,0:T(8,128)(2,1)S(1)}, u32[]{:S(2)}, u32[]{:S(2)}) collective-permute-start(bf16[16,4224]{1,0:T(8,128)(2,1)S(1)} %pack.4.refs_0_.refs_1_), channel_id=1, source_target_pairs={{0,24},{1,25},{2,26},{3,27},{4,28},{5,29},{6,30},{7,31},{8,16},{9,... | collective-permute-start | bytes 405512 | tf_op jit(solution)/shard_map/ppermute | solution.py:265
  18.7 0.5 collective-permute-start.8
  19.2 0.6 %collective-permute-start.7 = (bf16[16,4224]{1,0:T(8,128)(2,1)S(1)}, bf16[16,4224]{1,0:T(8,128)(2,1)S(1)}, u32[]{:S(2)}, u32[]{:S(2)}) collective-permute-start(bf16[16,4224]{1,0:T(8,128)(2,1)S(1)} %pack.4.refs_0_.refs_1_), channel_id=1, source_target_pairs={{0,16},{1,17},{2,18},{3,19},{4,20},{5,21},{6,22},{7,23},{8,24},{9,... | collective-permute-start | bytes 405512 | tf_op jit(solution)/shard_map/ppermute | solution.py:265
  19.8 2.7 %expert_piece.2 = (bf16[64,4096]{1,0:T(8,128)(2,1)S(1)}, bf16[64,4096]{1,0:T(8,128)(2,1)S(1)}) custom-call(bf16[64,4224]{1,0:T(8,128)(2,1)S(1)} %pack.6.here_ref, bf16[64,4224]{1,0:T(8,128)(2,1)S(1)} %collective-permute-done.6.there_ref, bf16[4096,768]{1,0:T(8,128)(2,1)S(1)} %bitcast.5, bf16[4096,768]{1,0:T(8,128)(2,1)S(1)} %bitcast.7, ...), custom_call_target="tpu_custom_call" | custom-call | flops 2415919104 | tf_op jit(solution)/shard_map/expert_piece/pallas_call | solution.py:240
  22.5 1.1 %collective-permute-done.9.refs_4_ = bf16[16,4224]{1,0:T(8,128)(2,1)S(1)} collective-permute-done((bf16[16,4224]{1,0:T(8,128)(2,1)S(1)}, bf16[16,4224]{1,0:T(8,128)(2,1)S(1)}, u32[]{:S(2)}, u32[]{:S(2)}) %collective-permute-start.9) | collective-permute-done | bytes 135200 | tf_op jit(solution)/shard_map/ppermute | solution.py:265
  23.6 2.5 %collective-permute-done.8.refs_3_ = bf16[16,4224]{1,0:T(8,128)(2,1)S(1)} collective-permute-done((bf16[16,4224]{1,0:T(8,128)(2,1)S(1)}, bf16[16,4224]{1,0:T(8,128)(2,1)S(1)}, u32[]{:S(2)}, u32[]{:S(2)}) %collective-permute-start.8) | collective-permute-done | bytes 135200 | tf_op jit(solution)/shard_map/ppermute | solution.py:265
  26.1 0.1 collective-permute-start.10
  26.2 1.9 %collective-permute-done.10.there_ref = bf16[64,4224]{1,0:T(8,128)(2,1)S(1)} collective-permute-done((bf16[64,4224]{1,0:T(8,128)(2,1)S(1)}, bf16[64,4224]{1,0:T(8,128)(2,1)S(1)}, u32[]{:S(2)}, u32[]{:S(2)}) %collective-permute-start.10) | collective-permute-done | bytes 540704 | tf_op jit(solution)/shard_map/ppermute | solution.py:265
  28.1 2.7 %expert_piece.3 = (bf16[64,4096]{1,0:T(8,128)(2,1)S(1)}, bf16[64,4096]{1,0:T(8,128)(2,1)S(1)}) custom-call(bf16[64,4224]{1,0:T(8,128)(2,1)S(1)} %pack.7.here_ref, bf16[64,4224]{1,0:T(8,128)(2,1)S(1)} %collective-permute-done.10.there_ref, bf16[4096,768]{1,0:T(8,128)(2,1)S(1)} %bitcast.6, bf16[4096,768]{1,0:T(8,128)(2,1)S(1)} %bitcast.8, ...), custom_call_target="tpu_custom_call" | custom-call | flops 2415919104 | tf_op jit(solution)/shard_map/expert_piece/pallas_call | solution.py:240
  30.8 0.2 collective-permute-start.11
  31.0 0.4 collective-permute-start.13
  31.4 1.4 %collective-permute-done.11 = bf16[64,4096]{1,0:T(8,128)(2,1)S(1)} collective-permute-done((bf16[64,4096]{1,0:T(8,128)(2,1)S(1)}, bf16[64,4096]{1,0:T(8,128)(2,1)S(1)}, u32[]{:S(2)}, u32[]{:S(2)}) %collective-permute-start.11) | collective-permute-done | bytes 524320 | tf_op jit(solution)/shard_map/ppermute | solution.py:265
  32.8 0.1 convert_add_fusion.1
  32.9 1.5 %collective-permute-start.12 = (bf16[16,4096]{1,0:T(8,128)(2,1)S(1)}, bf16[16,4096]{1,0:T(8,128)(2,1)S(1)}, u32[]{:S(2)}, u32[]{:S(2)}) collective-permute-start(bf16[16,4096]{1,0:T(8,128)(2,1)S(1)} %get-tuple-element.22), channel_id=1, source_target_pairs={{0,16},{1,17},{2,18},{3,19},{4,20},{5,21},{6,22},{7,23},{8,24},{9,... | collective-permute-start | bytes 393224 | tf_op jit(solution)/shard_map/ppermute | solution.py:265
  34.4 0.1 convert_add_fusion
  34.5 1.6 %collective-permute-start.17 = (bf16[16,4096]{1,0:T(8,128)(2,1)S(1)}, bf16[16,4096]{1,0:T(8,128)(2,1)S(1)}, u32[]{:S(2)}, u32[]{:S(2)}) collective-permute-start(bf16[16,4096]{1,0:T(8,128)(2,1)S(1)} %get-tuple-element.20), channel_id=1, source_target_pairs={{0,8},{1,9},{2,10},{3,11},{4,12},{5,13},{6,14},{7,15},{8,0},{9,1},... | collective-permute-start | bytes 393224 | tf_op jit(solution)/shard_map/ppermute | solution.py:265
  36.1 0.6 %collective-permute-start.18 = (bf16[16,4096]{1,0:T(8,128)(2,1)S(1)}, bf16[16,4096]{1,0:T(8,128)(2,1)S(1)}, u32[]{:S(2)}, u32[]{:S(2)}) collective-permute-start(bf16[16,4096]{1,0:T(8,128)(2,1)S(1)} %get-tuple-element.21), channel_id=1, source_target_pairs={{0,24},{1,25},{2,26},{3,27},{4,28},{5,29},{6,30},{7,31},{8,16},{9,... | collective-permute-start | bytes 393224 | tf_op jit(solution)/shard_map/ppermute | solution.py:265
  36.7 1.9 %collective-permute-done.12 = bf16[16,4096]{1,0:T(8,128)(2,1)S(1)} collective-permute-done((bf16[16,4096]{1,0:T(8,128)(2,1)S(1)}, bf16[16,4096]{1,0:T(8,128)(2,1)S(1)}, u32[]{:S(2)}, u32[]{:S(2)}) %collective-permute-start.12) | collective-permute-done | bytes 131104 | tf_op jit(solution)/shard_map/ppermute | solution.py:265
  38.6 0.1 convert_element_type.59
  38.7 1.5 %collective-permute-start.14 = (bf16[16,4096]{1,0:T(8,128)(2,1)S(1)}, bf16[16,4096]{1,0:T(8,128)(2,1)S(1)}, u32[]{:S(2)}, u32[]{:S(2)}) collective-permute-start(bf16[16,4096]{1,0:T(8,128)(2,1)S(1)} %get-tuple-element.23), channel_id=1, source_target_pairs={{0,16},{1,17},{2,18},{3,19},{4,20},{5,21},{6,22},{7,23},{8,24},{9,... | collective-permute-start | bytes 393224 | tf_op jit(solution)/shard_map/ppermute | solution.py:265
  40.1 1.5 %collective-permute-start.16 = (bf16[16,4096]{1,0:T(8,128)(2,1)S(1)}, bf16[16,4096]{1,0:T(8,128)(2,1)S(1)}, u32[]{:S(2)}, u32[]{:S(2)}) collective-permute-start(bf16[16,4096]{1,0:T(8,128)(2,1)S(1)} %get-tuple-element.24), channel_id=1, source_target_pairs={{0,24},{1,25},{2,26},{3,27},{4,28},{5,29},{6,30},{7,31},{8,16},{9,... | collective-permute-start | bytes 393224 | tf_op jit(solution)/shard_map/ppermute | solution.py:265
  41.7 0.5 %collective-permute-start.15 = (bf16[16,4096]{1,0:T(8,128)(2,1)S(1)}, bf16[16,4096]{1,0:T(8,128)(2,1)S(1)}, u32[]{:S(2)}, u32[]{:S(2)}) collective-permute-start(bf16[16,4096]{1,0:T(8,128)(2,1)S(1)} %get-tuple-element.25), channel_id=1, source_target_pairs={{0,8},{1,9},{2,10},{3,11},{4,12},{5,13},{6,14},{7,15},{8,0},{9,1},... | collective-permute-start | bytes 393224 | tf_op jit(solution)/shard_map/ppermute | solution.py:265
  42.2 1.0 %collective-permute-done.18 = bf16[16,4096]{1,0:T(8,128)(2,1)S(1)} collective-permute-done((bf16[16,4096]{1,0:T(8,128)(2,1)S(1)}, bf16[16,4096]{1,0:T(8,128)(2,1)S(1)}, u32[]{:S(2)}, u32[]{:S(2)}) %collective-permute-start.18) | collective-permute-done | bytes 131104 | tf_op jit(solution)/shard_map/ppermute | solution.py:265
  43.2 0.1 fusion.2
  43.3 2.6 %collective-permute-start.19 = (bf16[8,4096]{1,0:T(8,128)(2,1)S(1)}, bf16[8,4096]{1,0:T(8,128)(2,1)S(1)}, u32[]{:S(2)}, u32[]{:S(2)}) collective-permute-start(bf16[8,4096]{1,0:T(8,128)(2,1)S(1)} %get-tuple-element.26), channel_id=1, source_target_pairs={{0,2},{1,3},{2,0},{3,1},{4,6},{5,7},{6,4},{7,5},{8,10},{9,11},{10,... | collective-permute-start | bytes 196616 | tf_op jit(solution)/shard_map/ppermute | solution.py:265
  45.9 1.4 %collective-permute-start.20 = (bf16[8,4096]{1,0:T(8,128)(2,1)S(1)}, bf16[8,4096]{1,0:T(8,128)(2,1)S(1)}, u32[]{:S(2)}, u32[]{:S(2)}) collective-permute-start(bf16[8,4096]{1,0:T(8,128)(2,1)S(1)} %get-tuple-element.27), channel_id=1, source_target_pairs={{0,3},{1,2},{2,1},{3,0},{4,7},{5,6},{6,5},{7,4},{8,11},{9,10},{10,... | collective-permute-start | bytes 196616 | tf_op jit(solution)/shard_map/ppermute | solution.py:265
  47.3 1.1 %collective-permute-done.14 = bf16[16,4096]{1,0:T(8,128)(2,1)S(1)} collective-permute-done((bf16[16,4096]{1,0:T(8,128)(2,1)S(1)}, bf16[16,4096]{1,0:T(8,128)(2,1)S(1)}, u32[]{:S(2)}, u32[]{:S(2)}) %collective-permute-start.14) | collective-permute-done | bytes 131104 | tf_op jit(solution)/shard_map/ppermute | solution.py:265
  48.3 0.0 collective-permute-done.15
  48.3 0.1 convert_add_fusion.2
  48.4 1.6 %collective-permute-start.21 = (bf16[8,4096]{1,0:T(8,128)(2,1)S(1)}, bf16[8,4096]{1,0:T(8,128)(2,1)S(1)}, u32[]{:S(2)}, u32[]{:S(2)}) collective-permute-start(bf16[8,4096]{1,0:T(8,128)(2,1)S(1)} %slice.75), channel_id=1, source_target_pairs={{0,1},{1,0},{2,3},{3,2},{4,5},{5,4},{6,7},{7,6},{8,9},{9,8},{10,11... | collective-permute-start | bytes 196616 | tf_op jit(solution)/shard_map/ppermute | solution.py:265
  50.0 0.5 %collective-permute-done.19 = bf16[8,4096]{1,0:T(8,128)(2,1)S(1)} collective-permute-done((bf16[8,4096]{1,0:T(8,128)(2,1)S(1)}, bf16[8,4096]{1,0:T(8,128)(2,1)S(1)}, u32[]{:S(2)}, u32[]{:S(2)}) %collective-permute-start.19) | collective-permute-done | bytes 65568 | tf_op jit(solution)/shard_map/ppermute | solution.py:265
  50.5 1.5 %collective-permute-done.20 = bf16[8,4096]{1,0:T(8,128)(2,1)S(1)} collective-permute-done((bf16[8,4096]{1,0:T(8,128)(2,1)S(1)}, bf16[8,4096]{1,0:T(8,128)(2,1)S(1)}, u32[]{:S(2)}, u32[]{:S(2)}) %collective-permute-start.20) | collective-permute-done | bytes 65568 | tf_op jit(solution)/shard_map/ppermute | solution.py:265
  52.1 0.9 %collective-permute-done.21 = bf16[8,4096]{1,0:T(8,128)(2,1)S(1)} collective-permute-done((bf16[8,4096]{1,0:T(8,128)(2,1)S(1)}, bf16[8,4096]{1,0:T(8,128)(2,1)S(1)}, u32[]{:S(2)}, u32[]{:S(2)}) %collective-permute-start.21) | collective-permute-done | bytes 65568 | tf_op jit(solution)/shard_map/ppermute | solution.py:265
  53.0 0.7 %fusion.5 = bf16[8,4096]{1,0:T(8,128)(2,1)} fusion(f32[16,4096]{1,0:T(8,128)S(1)} %convert_add_fusion.2, bf16[8,4096]{1,0:T(8,128)(2,1)S(1)} %collective-permute-done.21, bf16[8,4096]{1,0:T(8,128)(2,1)S(1)} %collective-permute-done.20, bf16[8,4096]{1,0:T(8,128)(2,1)S(1)} %collective-permute-done.19), kind=kLoop, calls=%fused_computation.11 | loop fusion | flops 229376 | bytes 393216 | tf_op jit(solution)/shard_map/convert_element_type | solution.py:342
  (20 shorter events, 0.2 us)
Async XLA Ops:
  1.7 5.7 %collective-permute-start.2 = (bf16[8,4224]{1,0:T(8,128)(2,1)S(1)}, bf16[8,4224]{1,0:T(8,128)(2,1)S(1)}, u32[]{:S(2)}, u32[]{:S(2)}) collective-permute-start(bf16[8,4224]{1,0:T(8,128)(2,1)S(1)} %prepare.1.refs_0_), channel_id=1, source_target_pairs={{0,1},{1,0},{2,3},{3,2},{4,5},{5,4},{6,7},{7,6},{8,9},{9,8},{10,11... | collective-permute-start | bytes 202760 | tf_op jit(solution)/shard_map/ppermute | solution.py:265
  4.8 9.5 %collective-permute-start.1 = (bf16[8,4224]{1,0:T(8,128)(2,1)S(1)}, bf16[8,4224]{1,0:T(8,128)(2,1)S(1)}, u32[]{:S(2)}, u32[]{:S(2)}) collective-permute-start(bf16[8,4224]{1,0:T(8,128)(2,1)S(1)} %prepare.1.refs_0_), channel_id=1, source_target_pairs={{0,3},{1,2},{2,1},{3,0},{4,7},{5,6},{6,5},{7,4},{8,11},{9,10},{10,... | collective-permute-start | bytes 202760 | tf_op jit(solution)/shard_map/ppermute | solution.py:265
  7.3 7.0 %collective-permute-start = (bf16[8,4224]{1,0:T(8,128)(2,1)S(1)}, bf16[8,4224]{1,0:T(8,128)(2,1)S(1)}, u32[]{:S(2)}, u32[]{:S(2)}) collective-permute-start(bf16[8,4224]{1,0:T(8,128)(2,1)S(1)} %prepare.1.refs_0_), channel_id=1, source_target_pairs={{0,2},{1,3},{2,0},{3,1},{4,6},{5,7},{6,4},{7,5},{8,10},{9,11},{10,... | collective-permute-start | bytes 202760 | tf_op jit(solution)/shard_map/ppermute | solution.py:265
  7.4 7.3 %collective-permute-start.5 = (bf16[16,4224]{1,0:T(8,128)(2,1)S(1)}, bf16[16,4224]{1,0:T(8,128)(2,1)S(1)}, u32[]{:S(2)}, u32[]{:S(2)}) collective-permute-start(bf16[16,4224]{1,0:T(8,128)(2,1)S(1)} %pack.5.refs_1_), channel_id=1, source_target_pairs={{0,24},{1,25},{2,26},{3,27},{4,28},{5,29},{6,30},{7,31},{8,16},{9,... | collective-permute-start | bytes 405512 | tf_op jit(solution)/shard_map/ppermute | solution.py:265
  10.0 6.1 %collective-permute-start.4 = (bf16[16,4224]{1,0:T(8,128)(2,1)S(1)}, bf16[16,4224]{1,0:T(8,128)(2,1)S(1)}, u32[]{:S(2)}, u32[]{:S(2)}) collective-permute-start(bf16[16,4224]{1,0:T(8,128)(2,1)S(1)} %pack.5.refs_1_), channel_id=1, source_target_pairs={{0,8},{1,9},{2,10},{3,11},{4,12},{5,13},{6,14},{7,15},{8,0},{9,1},... | collective-permute-start | bytes 405512 | tf_op jit(solution)/shard_map/ppermute | solution.py:265
  10.6 5.5 %collective-permute-start.3 = (bf16[16,4224]{1,0:T(8,128)(2,1)S(1)}, bf16[16,4224]{1,0:T(8,128)(2,1)S(1)}, u32[]{:S(2)}, u32[]{:S(2)}) collective-permute-start(bf16[16,4224]{1,0:T(8,128)(2,1)S(1)} %pack.5.refs_1_), channel_id=1, source_target_pairs={{0,16},{1,17},{2,18},{3,19},{4,20},{5,21},{6,22},{7,23},{8,24},{9,... | collective-permute-start | bytes 405512 | tf_op jit(solution)/shard_map/ppermute | solution.py:265
  11.0 8.8 %copy-start = (bf16[1,4096,768]{2,1,0:T(8,128)(2,1)S(1)}, bf16[1,4096,768]{2,1,0:T(8,128)(2,1)}, u32[]{:S(2)}) copy-start(bf16[1,4096,768]{2,1,0:T(8,128)(2,1)} %param.23) | copy-start | bytes 18874372
  11.0 8.8 %copy-start.1 = (bf16[1,4096,768]{2,1,0:T(8,128)(2,1)S(1)}, bf16[1,4096,768]{2,1,0:T(8,128)(2,1)}, u32[]{:S(2)}) copy-start(bf16[1,4096,768]{2,1,0:T(8,128)(2,1)} %param.24) | copy-start | bytes 18874372
  11.0 8.8 %copy-start.2 = (bf16[1,768,4096]{2,1,0:T(8,128)(2,1)S(1)}, bf16[1,768,4096]{2,1,0:T(8,128)(2,1)}, u32[]{:S(2)}) copy-start(bf16[1,768,4096]{2,1,0:T(8,128)(2,1)} %param.25) | copy-start | bytes 18874372
  16.2 3.6 %collective-permute-start.6 = (bf16[64,4224]{1,0:T(8,128)(2,1)S(1)}, bf16[64,4224]{1,0:T(8,128)(2,1)S(1)}, u32[]{:S(2)}, u32[]{:S(2)}) collective-permute-start(bf16[64,4224]{1,0:T(8,128)(2,1)S(1)} %pack.6.here_ref), channel_id=1, source_target_pairs={{0,4},{1,5},{2,6},{3,7},{4,0},{5,1},{6,2},{7,3},{8,12},{9,13},{10,... | collective-permute-start | bytes 1622024 | tf_op jit(solution)/shard_map/ppermute | solution.py:265
  16.2 7.3 %collective-permute-start.9 = (bf16[16,4224]{1,0:T(8,128)(2,1)S(1)}, bf16[16,4224]{1,0:T(8,128)(2,1)S(1)}, u32[]{:S(2)}, u32[]{:S(2)}) collective-permute-start(bf16[16,4224]{1,0:T(8,128)(2,1)S(1)} %pack.4.refs_0_.refs_1_), channel_id=1, source_target_pairs={{0,24},{1,25},{2,26},{3,27},{4,28},{5,29},{6,30},{7,31},{8,16},{9,... | collective-permute-start | bytes 405512 | tf_op jit(solution)/shard_map/ppermute | solution.py:265
  18.7 7.4 %collective-permute-start.8 = (bf16[16,4224]{1,0:T(8,128)(2,1)S(1)}, bf16[16,4224]{1,0:T(8,128)(2,1)S(1)}, u32[]{:S(2)}, u32[]{:S(2)}) collective-permute-start(bf16[16,4224]{1,0:T(8,128)(2,1)S(1)} %pack.4.refs_0_.refs_1_), channel_id=1, source_target_pairs={{0,8},{1,9},{2,10},{3,11},{4,12},{5,13},{6,14},{7,15},{8,0},{9,1},... | collective-permute-start | bytes 405512 | tf_op jit(solution)/shard_map/ppermute | solution.py:265
  19.2 6.9 %collective-permute-start.7 = (bf16[16,4224]{1,0:T(8,128)(2,1)S(1)}, bf16[16,4224]{1,0:T(8,128)(2,1)S(1)}, u32[]{:S(2)}, u32[]{:S(2)}) collective-permute-start(bf16[16,4224]{1,0:T(8,128)(2,1)S(1)} %pack.4.refs_0_.refs_1_), channel_id=1, source_target_pairs={{0,16},{1,17},{2,18},{3,19},{4,20},{5,21},{6,22},{7,23},{8,24},{9,... | collective-permute-start | bytes 405512 | tf_op jit(solution)/shard_map/ppermute | solution.py:265
  26.1 2.0 %collective-permute-start.10 = (bf16[64,4224]{1,0:T(8,128)(2,1)S(1)}, bf16[64,4224]{1,0:T(8,128)(2,1)S(1)}, u32[]{:S(2)}, u32[]{:S(2)}) collective-permute-start(bf16[64,4224]{1,0:T(8,128)(2,1)S(1)} %pack.7.here_ref), channel_id=1, source_target_pairs={{0,4},{1,5},{2,6},{3,7},{4,0},{5,1},{6,2},{7,3},{8,12},{9,13},{10,... | collective-permute-start | bytes 1622024 | tf_op jit(solution)/shard_map/ppermute | solution.py:265
  30.8 2.0 %collective-permute-start.11 = (bf16[64,4096]{1,0:T(8,128)(2,1)S(1)}, bf16[64,4096]{1,0:T(8,128)(2,1)S(1)}, u32[]{:S(2)}, u32[]{:S(2)}) collective-permute-start(bf16[64,4096]{1,0:T(8,128)(2,1)S(1)} %get-tuple-element.14), channel_id=1, source_target_pairs={{0,4},{1,5},{2,6},{3,7},{4,0},{5,1},{6,2},{7,3},{8,12},{9,13},{10,... | collective-permute-start | bytes 1572872 | tf_op jit(solution)/shard_map/ppermute | solution.py:265
  31.0 3.4 %collective-permute-start.13 = (bf16[64,4096]{1,0:T(8,128)(2,1)S(1)}, bf16[64,4096]{1,0:T(8,128)(2,1)S(1)}, u32[]{:S(2)}, u32[]{:S(2)}) collective-permute-start(bf16[64,4096]{1,0:T(8,128)(2,1)S(1)} %get-tuple-element.15), channel_id=1, source_target_pairs={{0,4},{1,5},{2,6},{3,7},{4,0},{5,1},{6,2},{7,3},{8,12},{9,13},{10,... | collective-permute-start | bytes 1572872 | tf_op jit(solution)/shard_map/ppermute | solution.py:265
  32.9 5.6 %collective-permute-start.12 = (bf16[16,4096]{1,0:T(8,128)(2,1)S(1)}, bf16[16,4096]{1,0:T(8,128)(2,1)S(1)}, u32[]{:S(2)}, u32[]{:S(2)}) collective-permute-start(bf16[16,4096]{1,0:T(8,128)(2,1)S(1)} %get-tuple-element.22), channel_id=1, source_target_pairs={{0,16},{1,17},{2,18},{3,19},{4,20},{5,21},{6,22},{7,23},{8,24},{9,... | collective-permute-start | bytes 393224 | tf_op jit(solution)/shard_map/ppermute | solution.py:265
  34.5 7.7 %collective-permute-start.17 = (bf16[16,4096]{1,0:T(8,128)(2,1)S(1)}, bf16[16,4096]{1,0:T(8,128)(2,1)S(1)}, u32[]{:S(2)}, u32[]{:S(2)}) collective-permute-start(bf16[16,4096]{1,0:T(8,128)(2,1)S(1)} %get-tuple-element.20), channel_id=1, source_target_pairs={{0,8},{1,9},{2,10},{3,11},{4,12},{5,13},{6,14},{7,15},{8,0},{9,1},... | collective-permute-start | bytes 393224 | tf_op jit(solution)/shard_map/ppermute | solution.py:265
  36.1 7.1 %collective-permute-start.18 = (bf16[16,4096]{1,0:T(8,128)(2,1)S(1)}, bf16[16,4096]{1,0:T(8,128)(2,1)S(1)}, u32[]{:S(2)}, u32[]{:S(2)}) collective-permute-start(bf16[16,4096]{1,0:T(8,128)(2,1)S(1)} %get-tuple-element.21), channel_id=1, source_target_pairs={{0,24},{1,25},{2,26},{3,27},{4,28},{5,29},{6,30},{7,31},{8,16},{9,... | collective-permute-start | bytes 393224 | tf_op jit(solution)/shard_map/ppermute | solution.py:265
  38.7 9.7 %collective-permute-start.14 = (bf16[16,4096]{1,0:T(8,128)(2,1)S(1)}, bf16[16,4096]{1,0:T(8,128)(2,1)S(1)}, u32[]{:S(2)}, u32[]{:S(2)}) collective-permute-start(bf16[16,4096]{1,0:T(8,128)(2,1)S(1)} %get-tuple-element.23), channel_id=1, source_target_pairs={{0,16},{1,17},{2,18},{3,19},{4,20},{5,21},{6,22},{7,23},{8,24},{9,... | collective-permute-start | bytes 393224 | tf_op jit(solution)/shard_map/ppermute | solution.py:265
  40.1 8.2 %collective-permute-start.16 = (bf16[16,4096]{1,0:T(8,128)(2,1)S(1)}, bf16[16,4096]{1,0:T(8,128)(2,1)S(1)}, u32[]{:S(2)}, u32[]{:S(2)}) collective-permute-start(bf16[16,4096]{1,0:T(8,128)(2,1)S(1)} %get-tuple-element.24), channel_id=1, source_target_pairs={{0,24},{1,25},{2,26},{3,27},{4,28},{5,29},{6,30},{7,31},{8,16},{9,... | collective-permute-start | bytes 393224 | tf_op jit(solution)/shard_map/ppermute | solution.py:265
  41.7 6.7 %collective-permute-start.15 = (bf16[16,4096]{1,0:T(8,128)(2,1)S(1)}, bf16[16,4096]{1,0:T(8,128)(2,1)S(1)}, u32[]{:S(2)}, u32[]{:S(2)}) collective-permute-start(bf16[16,4096]{1,0:T(8,128)(2,1)S(1)} %get-tuple-element.25), channel_id=1, source_target_pairs={{0,8},{1,9},{2,10},{3,11},{4,12},{5,13},{6,14},{7,15},{8,0},{9,1},... | collective-permute-start | bytes 393224 | tf_op jit(solution)/shard_map/ppermute | solution.py:265
  43.3 7.2 %collective-permute-start.19 = (bf16[8,4096]{1,0:T(8,128)(2,1)S(1)}, bf16[8,4096]{1,0:T(8,128)(2,1)S(1)}, u32[]{:S(2)}, u32[]{:S(2)}) collective-permute-start(bf16[8,4096]{1,0:T(8,128)(2,1)S(1)} %get-tuple-element.26), channel_id=1, source_target_pairs={{0,2},{1,3},{2,0},{3,1},{4,6},{5,7},{6,4},{7,5},{8,10},{9,11},{10,... | collective-permute-start | bytes 196616 | tf_op jit(solution)/shard_map/ppermute | solution.py:265
  45.9 6.2 %collective-permute-start.20 = (bf16[8,4096]{1,0:T(8,128)(2,1)S(1)}, bf16[8,4096]{1,0:T(8,128)(2,1)S(1)}, u32[]{:S(2)}, u32[]{:S(2)}) collective-permute-start(bf16[8,4096]{1,0:T(8,128)(2,1)S(1)} %get-tuple-element.27), channel_id=1, source_target_pairs={{0,3},{1,2},{2,1},{3,0},{4,7},{5,6},{6,5},{7,4},{8,11},{9,10},{10,... | collective-permute-start | bytes 196616 | tf_op jit(solution)/shard_map/ppermute | solution.py:265
  48.4 4.6 %collective-permute-start.21 = (bf16[8,4096]{1,0:T(8,128)(2,1)S(1)}, bf16[8,4096]{1,0:T(8,128)(2,1)S(1)}, u32[]{:S(2)}, u32[]{:S(2)}) collective-permute-start(bf16[8,4096]{1,0:T(8,128)(2,1)S(1)} %slice.75), channel_id=1, source_target_pairs={{0,1},{1,0},{2,3},{3,2},{4,5},{5,4},{6,7},{7,6},{8,9},{9,8},{10,11... | collective-permute-start | bytes 196616 | tf_op jit(solution)/shard_map/ppermute | solution.py:265

commit v6 on v5

--- a/solution.py
+++ b/solution.py
@@ -10,8 +10,8 @@
 
 
 MIB = 1024 * 1024
-TILE = 256
-DOWN_TILE = 1024
+TILE = 768
+DOWN_TILE = 4096
 ATTEND_LIMIT = 12 * MIB
 
 

time: 53.8 us -> 53.8 us (level)
  no operation moved by 1% of the time
where the time goes in v6:
time: 53.8 us; the launch traced here: 53.7 us
  starting transfers between devices  26.2 us (49%)
  waiting for transfers between devices  15.6 us (29%)
  Pallas kernels  9.9 us (18%)
  other arithmetic  1.07 us (2%)
  between operations  0.8 us (1%)
    ppermute x22, starting transfers between devices, exchange(): return lax.ppermute(rows, ('node', 'local'), pairs)  26.2 us
    ppermute x22, waiting for transfers between devices, exchange(): return lax.ppermute(rows, ('node', 'local'), pairs)  15.6 us
    pallas_call x2, Pallas kernels, expert_piece(): pl.pallas_call(functools.partial(experts_kernel, experts, len(after)), ou...  5.41 us
    pallas_call x1, Pallas kernels, attend(): pl.pallas_call(functools.partial(attend_kernel, kv_heads, 1.0 / math.sqrt...  3.33 us
  transfers between devices with their start and end apart: 22, of which 12 were waited for; matrix products, arithmetic and copies ran while one was open for 1% of the time, Pallas kernels for 11%

profile of v6, /device:TPU:0, one launch (start us, length us, event | category | flops | bytes accessed | tf_op | source)
XLA Modules:
  0.0 53.7 jit_solution(3817073298234876539)
XLA Ops:
  0.6 1.1 %prepare.1.refs_0_ = bf16[8,4224]{1,0:T(8,128)(2,1)S(1)} custom-call(bf16[8,4096]{1,0:T(8,128)(2,1)} %hidden_hbm.1, bf16[4096]{0:T(1024)(128)(2,1)} %gain_hbm.1, s32[8,8]{1,0:T(8,128)} %ids_hbm.1, f32[8,8]{1,0:T(8,128)} %scores_hbm.1), custom_call_target="tpu_custom_call" | custom-call | tf_op jit(solution)/shard_map/prepare/pallas_call | solution.py:58
  1.7 3.1 %collective-permute-start.2 = (bf16[8,4224]{1,0:T(8,128)(2,1)S(1)}, bf16[8,4224]{1,0:T(8,128)(2,1)S(1)}, u32[]{:S(2)}, u32[]{:S(2)}) collective-permute-start(bf16[8,4224]{1,0:T(8,128)(2,1)S(1)} %prepare.1.refs_0_), channel_id=1, source_target_pairs={{0,1},{1,0},{2,3},{3,2},{4,5},{5,4},{6,7},{7,6},{8,9},{9,8},{10,11... | collective-permute-start | bytes 202760 | tf_op jit(solution)/shard_map/ppermute | solution.py:265
  4.8 2.5 %collective-permute-start.1 = (bf16[8,4224]{1,0:T(8,128)(2,1)S(1)}, bf16[8,4224]{1,0:T(8,128)(2,1)S(1)}, u32[]{:S(2)}, u32[]{:S(2)}) collective-permute-start(bf16[8,4224]{1,0:T(8,128)(2,1)S(1)} %prepare.1.refs_0_), channel_id=1, source_target_pairs={{0,3},{1,2},{2,1},{3,0},{4,7},{5,6},{6,5},{7,4},{8,11},{9,10},{10,... | collective-permute-start | bytes 202760 | tf_op jit(solution)/shard_map/ppermute | solution.py:265
  7.3 0.1 collective-permute-start
  7.4 0.0 collective-permute-done.2.refs_1_
  7.4 2.6 %collective-permute-start.5 = (bf16[16,4224]{1,0:T(8,128)(2,1)S(1)}, bf16[16,4224]{1,0:T(8,128)(2,1)S(1)}, u32[]{:S(2)}, u32[]{:S(2)}) collective-permute-start(bf16[16,4224]{1,0:T(8,128)(2,1)S(1)} %pack.5.refs_1_), channel_id=1, source_target_pairs={{0,24},{1,25},{2,26},{3,27},{4,28},{5,29},{6,30},{7,31},{8,16},{9,... | collective-permute-start | bytes 405512 | tf_op jit(solution)/shard_map/ppermute | solution.py:265
  10.0 0.5 collective-permute-start.4
  10.6 0.4 collective-permute-start.3
  11.0 3.3 %attend.1.refs_0_ = bf16[8,8192]{1,0:T(8,128)(2,1)} custom-call(s32[8]{0:T(128)} %lengths_hbm.1, bf16[8,64,128]{2,1,0:T(8,128)(2,1)} %queries_hbm.1, bf16[8,384,128]{2,1,0:T(8,128)(2,1)} %bitcast.11, bf16[8,384,128]{2,1,0:T(8,128)(2,1)} %bitcast.12, bf16[8,4,128]{2,1,0:T(4,128)(2,1)} %fresh_hbm.1, bf16[8,4,128]{2,1,0:T(4,128)(2,1)} %new_hbm.1), custom_call_target="tpu_custom_call" | custom-call | flops 12000000000 | bytes 1572864 | tf_op jit(solution)/shard_map/attend/pallas_call | solution.py:144
  14.3 0.0 collective-permute-done.1.refs_2_
  14.3 0.3 collective-permute-done.5.refs_4_
  14.7 1.4 %collective-permute-done.4.refs_3_ = bf16[16,4224]{1,0:T(8,128)(2,1)S(1)} collective-permute-done((bf16[16,4224]{1,0:T(8,128)(2,1)S(1)}, bf16[16,4224]{1,0:T(8,128)(2,1)S(1)}, u32[]{:S(2)}, u32[]{:S(2)}) %collective-permute-start.4) | collective-permute-done | bytes 135200 | tf_op jit(solution)/shard_map/ppermute | solution.py:265
  16.1 0.0 collective-permute-done.3.refs_2_
  16.2 0.1 collective-permute-start.6
  16.2 2.4 %collective-permute-start.9 = (bf16[16,4224]{1,0:T(8,128)(2,1)S(1)}, bf16[16,4224]{1,0:T(8,128)(2,1)S(1)}, u32[]{:S(2)}, u32[]{:S(2)}) collective-permute-start(bf16[16,4224]{1,0:T(8,128)(2,1)S(1)} %pack.4.refs_0_.refs_1_), channel_id=1, source_target_pairs={{0,24},{1,25},{2,26},{3,27},{4,28},{5,29},{6,30},{7,31},{8,16},{9,... | collective-permute-start | bytes 405512 | tf_op jit(solution)/shard_map/ppermute | solution.py:265
  18.7 0.5 collective-permute-start.8
  19.2 0.6 %collective-permute-start.7 = (bf16[16,4224]{1,0:T(8,128)(2,1)S(1)}, bf16[16,4224]{1,0:T(8,128)(2,1)S(1)}, u32[]{:S(2)}, u32[]{:S(2)}) collective-permute-start(bf16[16,4224]{1,0:T(8,128)(2,1)S(1)} %pack.4.refs_0_.refs_1_), channel_id=1, source_target_pairs={{0,16},{1,17},{2,18},{3,19},{4,20},{5,21},{6,22},{7,23},{8,24},{9,... | collective-permute-start | bytes 405512 | tf_op jit(solution)/shard_map/ppermute | solution.py:265
  19.8 2.7 %expert_piece.2 = (bf16[64,4096]{1,0:T(8,128)(2,1)S(1)}, bf16[64,4096]{1,0:T(8,128)(2,1)S(1)}) custom-call(bf16[64,4224]{1,0:T(8,128)(2,1)S(1)} %pack.6.here_ref, bf16[64,4224]{1,0:T(8,128)(2,1)S(1)} %collective-permute-done.6.there_ref, bf16[4096,768]{1,0:T(8,128)(2,1)S(1)} %bitcast.5, bf16[4096,768]{1,0:T(8,128)(2,1)S(1)} %bitcast.7, ...), custom_call_target="tpu_custom_call" | custom-call | flops 2415919104 | tf_op jit(solution)/shard_map/expert_piece/pallas_call | solution.py:240
  22.5 1.1 %collective-permute-done.9.refs_4_ = bf16[16,4224]{1,0:T(8,128)(2,1)S(1)} collective-permute-done((bf16[16,4224]{1,0:T(8,128)(2,1)S(1)}, bf16[16,4224]{1,0:T(8,128)(2,1)S(1)}, u32[]{:S(2)}, u32[]{:S(2)}) %collective-permute-start.9) | collective-permute-done | bytes 135200 | tf_op jit(solution)/shard_map/ppermute | solution.py:265
  23.6 2.5 %collective-permute-done.8.refs_3_ = bf16[16,4224]{1,0:T(8,128)(2,1)S(1)} collective-permute-done((bf16[16,4224]{1,0:T(8,128)(2,1)S(1)}, bf16[16,4224]{1,0:T(8,128)(2,1)S(1)}, u32[]{:S(2)}, u32[]{:S(2)}) %collective-permute-start.8) | collective-permute-done | bytes 135200 | tf_op jit(solution)/shard_map/ppermute | solution.py:265
  26.1 0.1 collective-permute-start.10
  26.2 1.9 %collective-permute-done.10.there_ref = bf16[64,4224]{1,0:T(8,128)(2,1)S(1)} collective-permute-done((bf16[64,4224]{1,0:T(8,128)(2,1)S(1)}, bf16[64,4224]{1,0:T(8,128)(2,1)S(1)}, u32[]{:S(2)}, u32[]{:S(2)}) %collective-permute-start.10) | collective-permute-done | bytes 540704 | tf_op jit(solution)/shard_map/ppermute | solution.py:265
  28.1 2.7 %expert_piece.3 = (bf16[64,4096]{1,0:T(8,128)(2,1)S(1)}, bf16[64,4096]{1,0:T(8,128)(2,1)S(1)}) custom-call(bf16[64,4224]{1,0:T(8,128)(2,1)S(1)} %pack.7.here_ref, bf16[64,4224]{1,0:T(8,128)(2,1)S(1)} %collective-permute-done.10.there_ref, bf16[4096,768]{1,0:T(8,128)(2,1)S(1)} %bitcast.6, bf16[4096,768]{1,0:T(8,128)(2,1)S(1)} %bitcast.8, ...), custom_call_target="tpu_custom_call" | custom-call | flops 2415919104 | tf_op jit(solution)/shard_map/expert_piece/pallas_call | solution.py:240
  30.8 0.2 collective-permute-start.11
  31.0 0.4 collective-permute-start.13
  31.4 1.4 %collective-permute-done.11 = bf16[64,4096]{1,0:T(8,128)(2,1)S(1)} collective-permute-done((bf16[64,4096]{1,0:T(8,128)(2,1)S(1)}, bf16[64,4096]{1,0:T(8,128)(2,1)S(1)}, u32[]{:S(2)}, u32[]{:S(2)}) %collective-permute-start.11) | collective-permute-done | bytes 524320 | tf_op jit(solution)/shard_map/ppermute | solution.py:265
  32.8 0.1 convert_add_fusion.1
  33.0 1.5 %collective-permute-start.12 = (bf16[16,4096]{1,0:T(8,128)(2,1)S(1)}, bf16[16,4096]{1,0:T(8,128)(2,1)S(1)}, u32[]{:S(2)}, u32[]{:S(2)}) collective-permute-start(bf16[16,4096]{1,0:T(8,128)(2,1)S(1)} %get-tuple-element.22), channel_id=1, source_target_pairs={{0,16},{1,17},{2,18},{3,19},{4,20},{5,21},{6,22},{7,23},{8,24},{9,... | collective-permute-start | bytes 393224 | tf_op jit(solution)/shard_map/ppermute | solution.py:265
  34.4 0.1 convert_add_fusion
  34.6 1.6 %collective-permute-start.17 = (bf16[16,4096]{1,0:T(8,128)(2,1)S(1)}, bf16[16,4096]{1,0:T(8,128)(2,1)S(1)}, u32[]{:S(2)}, u32[]{:S(2)}) collective-permute-start(bf16[16,4096]{1,0:T(8,128)(2,1)S(1)} %get-tuple-element.20), channel_id=1, source_target_pairs={{0,8},{1,9},{2,10},{3,11},{4,12},{5,13},{6,14},{7,15},{8,0},{9,1},... | collective-permute-start | bytes 393224 | tf_op jit(solution)/shard_map/ppermute | solution.py:265
  36.1 0.6 %collective-permute-start.18 = (bf16[16,4096]{1,0:T(8,128)(2,1)S(1)}, bf16[16,4096]{1,0:T(8,128)(2,1)S(1)}, u32[]{:S(2)}, u32[]{:S(2)}) collective-permute-start(bf16[16,4096]{1,0:T(8,128)(2,1)S(1)} %get-tuple-element.21), channel_id=1, source_target_pairs={{0,24},{1,25},{2,26},{3,27},{4,28},{5,29},{6,30},{7,31},{8,16},{9,... | collective-permute-start | bytes 393224 | tf_op jit(solution)/shard_map/ppermute | solution.py:265
  36.7 1.9 %collective-permute-done.12 = bf16[16,4096]{1,0:T(8,128)(2,1)S(1)} collective-permute-done((bf16[16,4096]{1,0:T(8,128)(2,1)S(1)}, bf16[16,4096]{1,0:T(8,128)(2,1)S(1)}, u32[]{:S(2)}, u32[]{:S(2)}) %collective-permute-start.12) | collective-permute-done | bytes 131104 | tf_op jit(solution)/shard_map/ppermute | solution.py:265
  38.6 0.1 convert_element_type.59
  38.7 1.5 %collective-permute-start.14 = (bf16[16,4096]{1,0:T(8,128)(2,1)S(1)}, bf16[16,4096]{1,0:T(8,128)(2,1)S(1)}, u32[]{:S(2)}, u32[]{:S(2)}) collective-permute-start(bf16[16,4096]{1,0:T(8,128)(2,1)S(1)} %get-tuple-element.23), channel_id=1, source_target_pairs={{0,16},{1,17},{2,18},{3,19},{4,20},{5,21},{6,22},{7,23},{8,24},{9,... | collective-permute-start | bytes 393224 | tf_op jit(solution)/shard_map/ppermute | solution.py:265
  40.1 1.5 %collective-permute-start.16 = (bf16[16,4096]{1,0:T(8,128)(2,1)S(1)}, bf16[16,4096]{1,0:T(8,128)(2,1)S(1)}, u32[]{:S(2)}, u32[]{:S(2)}) collective-permute-start(bf16[16,4096]{1,0:T(8,128)(2,1)S(1)} %get-tuple-element.24), channel_id=1, source_target_pairs={{0,24},{1,25},{2,26},{3,27},{4,28},{5,29},{6,30},{7,31},{8,16},{9,... | collective-permute-start | bytes 393224 | tf_op jit(solution)/shard_map/ppermute | solution.py:265
  41.7 0.5 %collective-permute-start.15 = (bf16[16,4096]{1,0:T(8,128)(2,1)S(1)}, bf16[16,4096]{1,0:T(8,128)(2,1)S(1)}, u32[]{:S(2)}, u32[]{:S(2)}) collective-permute-start(bf16[16,4096]{1,0:T(8,128)(2,1)S(1)} %get-tuple-element.25), channel_id=1, source_target_pairs={{0,8},{1,9},{2,10},{3,11},{4,12},{5,13},{6,14},{7,15},{8,0},{9,1},... | collective-permute-start | bytes 393224 | tf_op jit(solution)/shard_map/ppermute | solution.py:265
  42.2 1.0 %collective-permute-done.18 = bf16[16,4096]{1,0:T(8,128)(2,1)S(1)} collective-permute-done((bf16[16,4096]{1,0:T(8,128)(2,1)S(1)}, bf16[16,4096]{1,0:T(8,128)(2,1)S(1)}, u32[]{:S(2)}, u32[]{:S(2)}) %collective-permute-start.18) | collective-permute-done | bytes 131104 | tf_op jit(solution)/shard_map/ppermute | solution.py:265
  43.2 0.1 fusion.2
  43.3 2.6 %collective-permute-start.19 = (bf16[8,4096]{1,0:T(8,128)(2,1)S(1)}, bf16[8,4096]{1,0:T(8,128)(2,1)S(1)}, u32[]{:S(2)}, u32[]{:S(2)}) collective-permute-start(bf16[8,4096]{1,0:T(8,128)(2,1)S(1)} %get-tuple-element.26), channel_id=1, source_target_pairs={{0,2},{1,3},{2,0},{3,1},{4,6},{5,7},{6,4},{7,5},{8,10},{9,11},{10,... | collective-permute-start | bytes 196616 | tf_op jit(solution)/shard_map/ppermute | solution.py:265
  45.9 1.3 %collective-permute-start.20 = (bf16[8,4096]{1,0:T(8,128)(2,1)S(1)}, bf16[8,4096]{1,0:T(8,128)(2,1)S(1)}, u32[]{:S(2)}, u32[]{:S(2)}) collective-permute-start(bf16[8,4096]{1,0:T(8,128)(2,1)S(1)} %get-tuple-element.27), channel_id=1, source_target_pairs={{0,3},{1,2},{2,1},{3,0},{4,7},{5,6},{6,5},{7,4},{8,11},{9,10},{10,... | collective-permute-start | bytes 196616 | tf_op jit(solution)/shard_map/ppermute | solution.py:265
  47.3 1.1 %collective-permute-done.14 = bf16[16,4096]{1,0:T(8,128)(2,1)S(1)} collective-permute-done((bf16[16,4096]{1,0:T(8,128)(2,1)S(1)}, bf16[16,4096]{1,0:T(8,128)(2,1)S(1)}, u32[]{:S(2)}, u32[]{:S(2)}) %collective-permute-start.14) | collective-permute-done | bytes 131104 | tf_op jit(solution)/shard_map/ppermute | solution.py:265
  48.3 0.0 collective-permute-done.15
  48.3 0.1 convert_add_fusion.2
  48.4 1.6 %collective-permute-start.21 = (bf16[8,4096]{1,0:T(8,128)(2,1)S(1)}, bf16[8,4096]{1,0:T(8,128)(2,1)S(1)}, u32[]{:S(2)}, u32[]{:S(2)}) collective-permute-start(bf16[8,4096]{1,0:T(8,128)(2,1)S(1)} %slice.75), channel_id=1, source_target_pairs={{0,1},{1,0},{2,3},{3,2},{4,5},{5,4},{6,7},{7,6},{8,9},{9,8},{10,11... | collective-permute-start | bytes 196616 | tf_op jit(solution)/shard_map/ppermute | solution.py:265
  50.0 0.5 collective-permute-done.19
  50.5 1.6 %collective-permute-done.20 = bf16[8,4096]{1,0:T(8,128)(2,1)S(1)} collective-permute-done((bf16[8,4096]{1,0:T(8,128)(2,1)S(1)}, bf16[8,4096]{1,0:T(8,128)(2,1)S(1)}, u32[]{:S(2)}, u32[]{:S(2)}) %collective-permute-start.20) | collective-permute-done | bytes 65568 | tf_op jit(solution)/shard_map/ppermute | solution.py:265
  52.1 0.9 %collective-permute-done.21 = bf16[8,4096]{1,0:T(8,128)(2,1)S(1)} collective-permute-done((bf16[8,4096]{1,0:T(8,128)(2,1)S(1)}, bf16[8,4096]{1,0:T(8,128)(2,1)S(1)}, u32[]{:S(2)}, u32[]{:S(2)}) %collective-permute-start.21) | collective-permute-done | bytes 65568 | tf_op jit(solution)/shard_map/ppermute | solution.py:265
  53.0 0.7 %fusion.5 = bf16[8,4096]{1,0:T(8,128)(2,1)} fusion(f32[16,4096]{1,0:T(8,128)S(1)} %convert_add_fusion.2, bf16[8,4096]{1,0:T(8,128)(2,1)S(1)} %collective-permute-done.21, bf16[8,4096]{1,0:T(8,128)(2,1)S(1)} %collective-permute-done.20, bf16[8,4096]{1,0:T(8,128)(2,1)S(1)} %collective-permute-done.19), kind=kLoop, calls=%fused_computation.11 | loop fusion | flops 229376 | bytes 393216 | tf_op jit(solution)/shard_map/convert_element_type | solution.py:342
  (20 shorter events, 0.2 us)
Async XLA Ops:
  1.7 5.7 %collective-permute-start.2 = (bf16[8,4224]{1,0:T(8,128)(2,1)S(1)}, bf16[8,4224]{1,0:T(8,128)(2,1)S(1)}, u32[]{:S(2)}, u32[]{:S(2)}) collective-permute-start(bf16[8,4224]{1,0:T(8,128)(2,1)S(1)} %prepare.1.refs_0_), channel_id=1, source_target_pairs={{0,1},{1,0},{2,3},{3,2},{4,5},{5,4},{6,7},{7,6},{8,9},{9,8},{10,11... | collective-permute-start | bytes 202760 | tf_op jit(solution)/shard_map/ppermute | solution.py:265
  4.8 9.5 %collective-permute-start.1 = (bf16[8,4224]{1,0:T(8,128)(2,1)S(1)}, bf16[8,4224]{1,0:T(8,128)(2,1)S(1)}, u32[]{:S(2)}, u32[]{:S(2)}) collective-permute-start(bf16[8,4224]{1,0:T(8,128)(2,1)S(1)} %prepare.1.refs_0_), channel_id=1, source_target_pairs={{0,3},{1,2},{2,1},{3,0},{4,7},{5,6},{6,5},{7,4},{8,11},{9,10},{10,... | collective-permute-start | bytes 202760 | tf_op jit(solution)/shard_map/ppermute | solution.py:265
  7.3 7.0 %collective-permute-start = (bf16[8,4224]{1,0:T(8,128)(2,1)S(1)}, bf16[8,4224]{1,0:T(8,128)(2,1)S(1)}, u32[]{:S(2)}, u32[]{:S(2)}) collective-permute-start(bf16[8,4224]{1,0:T(8,128)(2,1)S(1)} %prepare.1.refs_0_), channel_id=1, source_target_pairs={{0,2},{1,3},{2,0},{3,1},{4,6},{5,7},{6,4},{7,5},{8,10},{9,11},{10,... | collective-permute-start | bytes 202760 | tf_op jit(solution)/shard_map/ppermute | solution.py:265
  7.4 7.3 %collective-permute-start.5 = (bf16[16,4224]{1,0:T(8,128)(2,1)S(1)}, bf16[16,4224]{1,0:T(8,128)(2,1)S(1)}, u32[]{:S(2)}, u32[]{:S(2)}) collective-permute-start(bf16[16,4224]{1,0:T(8,128)(2,1)S(1)} %pack.5.refs_1_), channel_id=1, source_target_pairs={{0,24},{1,25},{2,26},{3,27},{4,28},{5,29},{6,30},{7,31},{8,16},{9,... | collective-permute-start | bytes 405512 | tf_op jit(solution)/shard_map/ppermute | solution.py:265
  10.0 6.1 %collective-permute-start.4 = (bf16[16,4224]{1,0:T(8,128)(2,1)S(1)}, bf16[16,4224]{1,0:T(8,128)(2,1)S(1)}, u32[]{:S(2)}, u32[]{:S(2)}) collective-permute-start(bf16[16,4224]{1,0:T(8,128)(2,1)S(1)} %pack.5.refs_1_), channel_id=1, source_target_pairs={{0,8},{1,9},{2,10},{3,11},{4,12},{5,13},{6,14},{7,15},{8,0},{9,1},... | collective-permute-start | bytes 405512 | tf_op jit(solution)/shard_map/ppermute | solution.py:265
  10.6 5.5 %collective-permute-start.3 = (bf16[16,4224]{1,0:T(8,128)(2,1)S(1)}, bf16[16,4224]{1,0:T(8,128)(2,1)S(1)}, u32[]{:S(2)}, u32[]{:S(2)}) collective-permute-start(bf16[16,4224]{1,0:T(8,128)(2,1)S(1)} %pack.5.refs_1_), channel_id=1, source_target_pairs={{0,16},{1,17},{2,18},{3,19},{4,20},{5,21},{6,22},{7,23},{8,24},{9,... | collective-permute-start | bytes 405512 | tf_op jit(solution)/shard_map/ppermute | solution.py:265
  11.0 8.8 %copy-start = (bf16[1,4096,768]{2,1,0:T(8,128)(2,1)S(1)}, bf16[1,4096,768]{2,1,0:T(8,128)(2,1)}, u32[]{:S(2)}) copy-start(bf16[1,4096,768]{2,1,0:T(8,128)(2,1)} %param.23) | copy-start | bytes 18874372
  11.0 8.8 %copy-start.1 = (bf16[1,4096,768]{2,1,0:T(8,128)(2,1)S(1)}, bf16[1,4096,768]{2,1,0:T(8,128)(2,1)}, u32[]{:S(2)}) copy-start(bf16[1,4096,768]{2,1,0:T(8,128)(2,1)} %param.24) | copy-start | bytes 18874372
  11.0 8.8 %copy-start.2 = (bf16[1,768,4096]{2,1,0:T(8,128)(2,1)S(1)}, bf16[1,768,4096]{2,1,0:T(8,128)(2,1)}, u32[]{:S(2)}) copy-start(bf16[1,768,4096]{2,1,0:T(8,128)(2,1)} %param.25) | copy-start | bytes 18874372
  16.2 3.6 %collective-permute-start.6 = (bf16[64,4224]{1,0:T(8,128)(2,1)S(1)}, bf16[64,4224]{1,0:T(8,128)(2,1)S(1)}, u32[]{:S(2)}, u32[]{:S(2)}) collective-permute-start(bf16[64,4224]{1,0:T(8,128)(2,1)S(1)} %pack.6.here_ref), channel_id=1, source_target_pairs={{0,4},{1,5},{2,6},{3,7},{4,0},{5,1},{6,2},{7,3},{8,12},{9,13},{10,... | collective-permute-start | bytes 1622024 | tf_op jit(solution)/shard_map/ppermute | solution.py:265
  16.2 7.3 %collective-permute-start.9 = (bf16[16,4224]{1,0:T(8,128)(2,1)S(1)}, bf16[16,4224]{1,0:T(8,128)(2,1)S(1)}, u32[]{:S(2)}, u32[]{:S(2)}) collective-permute-start(bf16[16,4224]{1,0:T(8,128)(2,1)S(1)} %pack.4.refs_0_.refs_1_), channel_id=1, source_target_pairs={{0,24},{1,25},{2,26},{3,27},{4,28},{5,29},{6,30},{7,31},{8,16},{9,... | collective-permute-start | bytes 405512 | tf_op jit(solution)/shard_map/ppermute | solution.py:265
  18.7 7.4 %collective-permute-start.8 = (bf16[16,4224]{1,0:T(8,128)(2,1)S(1)}, bf16[16,4224]{1,0:T(8,128)(2,1)S(1)}, u32[]{:S(2)}, u32[]{:S(2)}) collective-permute-start(bf16[16,4224]{1,0:T(8,128)(2,1)S(1)} %pack.4.refs_0_.refs_1_), channel_id=1, source_target_pairs={{0,8},{1,9},{2,10},{3,11},{4,12},{5,13},{6,14},{7,15},{8,0},{9,1},... | collective-permute-start | bytes 405512 | tf_op jit(solution)/shard_map/ppermute | solution.py:265
  19.2 6.9 %collective-permute-start.7 = (bf16[16,4224]{1,0:T(8,128)(2,1)S(1)}, bf16[16,4224]{1,0:T(8,128)(2,1)S(1)}, u32[]{:S(2)}, u32[]{:S(2)}) collective-permute-start(bf16[16,4224]{1,0:T(8,128)(2,1)S(1)} %pack.4.refs_0_.refs_1_), channel_id=1, source_target_pairs={{0,16},{1,17},{2,18},{3,19},{4,20},{5,21},{6,22},{7,23},{8,24},{9,... | collective-permute-start | bytes 405512 | tf_op jit(solution)/shard_map/ppermute | solution.py:265
  26.1 2.0 %collective-permute-start.10 = (bf16[64,4224]{1,0:T(8,128)(2,1)S(1)}, bf16[64,4224]{1,0:T(8,128)(2,1)S(1)}, u32[]{:S(2)}, u32[]{:S(2)}) collective-permute-start(bf16[64,4224]{1,0:T(8,128)(2,1)S(1)} %pack.7.here_ref), channel_id=1, source_target_pairs={{0,4},{1,5},{2,6},{3,7},{4,0},{5,1},{6,2},{7,3},{8,12},{9,13},{10,... | collective-permute-start | bytes 1622024 | tf_op jit(solution)/shard_map/ppermute | solution.py:265
  30.8 2.0 %collective-permute-start.11 = (bf16[64,4096]{1,0:T(8,128)(2,1)S(1)}, bf16[64,4096]{1,0:T(8,128)(2,1)S(1)}, u32[]{:S(2)}, u32[]{:S(2)}) collective-permute-start(bf16[64,4096]{1,0:T(8,128)(2,1)S(1)} %get-tuple-element.14), channel_id=1, source_target_pairs={{0,4},{1,5},{2,6},{3,7},{4,0},{5,1},{6,2},{7,3},{8,12},{9,13},{10,... | collective-permute-start | bytes 1572872 | tf_op jit(solution)/shard_map/ppermute | solution.py:265
  31.0 3.4 %collective-permute-start.13 = (bf16[64,4096]{1,0:T(8,128)(2,1)S(1)}, bf16[64,4096]{1,0:T(8,128)(2,1)S(1)}, u32[]{:S(2)}, u32[]{:S(2)}) collective-permute-start(bf16[64,4096]{1,0:T(8,128)(2,1)S(1)} %get-tuple-element.15), channel_id=1, source_target_pairs={{0,4},{1,5},{2,6},{3,7},{4,0},{5,1},{6,2},{7,3},{8,12},{9,13},{10,... | collective-permute-start | bytes 1572872 | tf_op jit(solution)/shard_map/ppermute | solution.py:265
  33.0 5.6 %collective-permute-start.12 = (bf16[16,4096]{1,0:T(8,128)(2,1)S(1)}, bf16[16,4096]{1,0:T(8,128)(2,1)S(1)}, u32[]{:S(2)}, u32[]{:S(2)}) collective-permute-start(bf16[16,4096]{1,0:T(8,128)(2,1)S(1)} %get-tuple-element.22), channel_id=1, source_target_pairs={{0,16},{1,17},{2,18},{3,19},{4,20},{5,21},{6,22},{7,23},{8,24},{9,... | collective-permute-start | bytes 393224 | tf_op jit(solution)/shard_map/ppermute | solution.py:265
  34.6 7.7 %collective-permute-start.17 = (bf16[16,4096]{1,0:T(8,128)(2,1)S(1)}, bf16[16,4096]{1,0:T(8,128)(2,1)S(1)}, u32[]{:S(2)}, u32[]{:S(2)}) collective-permute-start(bf16[16,4096]{1,0:T(8,128)(2,1)S(1)} %get-tuple-element.20), channel_id=1, source_target_pairs={{0,8},{1,9},{2,10},{3,11},{4,12},{5,13},{6,14},{7,15},{8,0},{9,1},... | collective-permute-start | bytes 393224 | tf_op jit(solution)/shard_map/ppermute | solution.py:265
  36.1 7.1 %collective-permute-start.18 = (bf16[16,4096]{1,0:T(8,128)(2,1)S(1)}, bf16[16,4096]{1,0:T(8,128)(2,1)S(1)}, u32[]{:S(2)}, u32[]{:S(2)}) collective-permute-start(bf16[16,4096]{1,0:T(8,128)(2,1)S(1)} %get-tuple-element.21), channel_id=1, source_target_pairs={{0,24},{1,25},{2,26},{3,27},{4,28},{5,29},{6,30},{7,31},{8,16},{9,... | collective-permute-start | bytes 393224 | tf_op jit(solution)/shard_map/ppermute | solution.py:265
  38.7 9.7 %collective-permute-start.14 = (bf16[16,4096]{1,0:T(8,128)(2,1)S(1)}, bf16[16,4096]{1,0:T(8,128)(2,1)S(1)}, u32[]{:S(2)}, u32[]{:S(2)}) collective-permute-start(bf16[16,4096]{1,0:T(8,128)(2,1)S(1)} %get-tuple-element.23), channel_id=1, source_target_pairs={{0,16},{1,17},{2,18},{3,19},{4,20},{5,21},{6,22},{7,23},{8,24},{9,... | collective-permute-start | bytes 393224 | tf_op jit(solution)/shard_map/ppermute | solution.py:265
  40.1 8.2 %collective-permute-start.16 = (bf16[16,4096]{1,0:T(8,128)(2,1)S(1)}, bf16[16,4096]{1,0:T(8,128)(2,1)S(1)}, u32[]{:S(2)}, u32[]{:S(2)}) collective-permute-start(bf16[16,4096]{1,0:T(8,128)(2,1)S(1)} %get-tuple-element.24), channel_id=1, source_target_pairs={{0,24},{1,25},{2,26},{3,27},{4,28},{5,29},{6,30},{7,31},{8,16},{9,... | collective-permute-start | bytes 393224 | tf_op jit(solution)/shard_map/ppermute | solution.py:265
  41.7 6.7 %collective-permute-start.15 = (bf16[16,4096]{1,0:T(8,128)(2,1)S(1)}, bf16[16,4096]{1,0:T(8,128)(2,1)S(1)}, u32[]{:S(2)}, u32[]{:S(2)}) collective-permute-start(bf16[16,4096]{1,0:T(8,128)(2,1)S(1)} %get-tuple-element.25), channel_id=1, source_target_pairs={{0,8},{1,9},{2,10},{3,11},{4,12},{5,13},{6,14},{7,15},{8,0},{9,1},... | collective-permute-start | bytes 393224 | tf_op jit(solution)/shard_map/ppermute | solution.py:265
  43.3 7.2 %collective-permute-start.19 = (bf16[8,4096]{1,0:T(8,128)(2,1)S(1)}, bf16[8,4096]{1,0:T(8,128)(2,1)S(1)}, u32[]{:S(2)}, u32[]{:S(2)}) collective-permute-start(bf16[8,4096]{1,0:T(8,128)(2,1)S(1)} %get-tuple-element.26), channel_id=1, source_target_pairs={{0,2},{1,3},{2,0},{3,1},{4,6},{5,7},{6,4},{7,5},{8,10},{9,11},{10,... | collective-permute-start | bytes 196616 | tf_op jit(solution)/shard_map/ppermute | solution.py:265
  45.9 6.2 %collective-permute-start.20 = (bf16[8,4096]{1,0:T(8,128)(2,1)S(1)}, bf16[8,4096]{1,0:T(8,128)(2,1)S(1)}, u32[]{:S(2)}, u32[]{:S(2)}) collective-permute-start(bf16[8,4096]{1,0:T(8,128)(2,1)S(1)} %get-tuple-element.27), channel_id=1, source_target_pairs={{0,3},{1,2},{2,1},{3,0},{4,7},{5,6},{6,5},{7,4},{8,11},{9,10},{10,... | collective-permute-start | bytes 196616 | tf_op jit(solution)/shard_map/ppermute | solution.py:265
  48.4 4.6 %collective-permute-start.21 = (bf16[8,4096]{1,0:T(8,128)(2,1)S(1)}, bf16[8,4096]{1,0:T(8,128)(2,1)S(1)}, u32[]{:S(2)}, u32[]{:S(2)}) collective-permute-start(bf16[8,4096]{1,0:T(8,128)(2,1)S(1)} %slice.75), channel_id=1, source_target_pairs={{0,1},{1,0},{2,3},{3,2},{4,5},{5,4},{6,7},{7,6},{8,9},{9,8},{10,11... | collective-permute-start | bytes 196616 | tf_op jit(solution)/shard_map/ppermute | solution.py:265
